TPU v7x, 32 devices: a whole 2x2x4 slice. The times are simulated.
32 devices in a mesh: lat: 4 (over y, core), lon: 8 (over z, x).
Axes of the slice: x: 2, y: 2, z: 4, core: 2. Of those that a mesh axis runs over, the one named last changes fastest.
Arguments:
- source_cells: bfloat16 [73, 16384], P(None, ('lat', 'lon')), may hold values from -6 to 6
- recv_src: int32 [131072], P(('lat', 'lon')), may hold values from 0 to 511
- recv_cell: int32 [131072], P(('lat', 'lon')), may hold values from 0 to 32399
- recv_weight: float32 [131072], P(('lat', 'lon')), may hold values from 0 to 1, as said below
- enc_w1: bfloat16 [256, 73], replicated, may hold values from -0.75 to 0.75
- enc_b1: float32 [256], replicated, may hold values from -3 to 3
- enc_w2: bfloat16 [256, 256], replicated, may hold values from -0.375 to 0.375
- enc_b2: float32 [256], replicated, may hold values from -3 to 3
- mix_weight: bfloat16 [2, 256, 256], replicated, may hold values from -0.25 to 0.25
- fwd_table: bfloat16 [512, 512, 720], P(('lat', 'lon')), may hold values from -0.21875 to 0.21875
- inv_table: bfloat16 [512, 720, 512], P(('lat', 'lon')), may hold values from -0.25 to 0.25
Outputs:
- layer_out: bfloat16 [256, 1036800], P(None, ('lat', 'lon'))
Inputs may be any that keep to these rules, and one draw needn't show every extreme that they name: `recv_weight`: zero exactly on padding slots. For each target block and source device, the slots with nonzero weight come first; there are at most 512 of them, and for every target block one source device fills all 512.
All inputs are finite; a program needn't handle non-finite values.
Results may differ from a plain program's by a relative error of at most 0.011.
Values may be sent and summed in bfloat16 or wider, within the bound.
No kernel may reach another device: no remote copies, remote signals or barrier semaphores. Data moves between devices by JAX's collectives and lax.ppermute only.
A program may use at most 256 MiB of HBM per device.

v0:
```python
import math

import jax
import jax.numpy as jnp
from jax import lax
from jax.sharding import PartitionSpec as P

NLON = 1440
ORDERS = 512


def build_basis(order_list, points_total):
    points = jnp.arange(points_total, dtype=jnp.int32)
    angles = (order_list[:, None] * points[None, :] % points_total).astype(jnp.float32) * (
        2.0 * math.pi / points_total
    )
    factor = math.sqrt(2.0 / points_total)
    stacked = jnp.stack([factor * jnp.cos(angles), -factor * jnp.sin(angles)], axis=1)
    return stacked.astype(jnp.bfloat16).reshape(2 * order_list.shape[0], points_total)


def spread(running, values, weights, targets):
    channels = values.shape[-1]
    contrib = values.astype(jnp.float32) * weights[:, :, None]
    return running.at[targets.reshape(-1)].add(contrib.reshape(-1, channels))


def on_device(
    source_cells,
    recv_src,
    recv_cell,
    recv_weight,
    enc_w1,
    enc_b1,
    enc_w2,
    enc_b2,
    mix_weight,
    fwd_table,
    inv_table,
):
    lon_count = lax.axis_size("lon")
    lat_count = lax.axis_size("lat")
    channels = source_cells.shape[0]
    src_rows = source_cells.shape[1]
    slot_count = recv_src.shape[0] // lon_count
    sources = recv_src.reshape(lon_count, slot_count)
    targets = recv_cell.reshape(lon_count, slot_count)
    weights = recv_weight.reshape(lon_count, slot_count)
    lat_total = fwd_table.shape[2]
    lat_dev = lat_total // lat_count
    lon_dev = NLON // lon_count
    cells_dev = lat_dev * lon_dev
    width = enc_w1.shape[0]
    ch_dev = width // lon_count
    orders_total = ORDERS
    ord_dev = fwd_table.shape[0]
    empty = jnp.zeros((cells_dev, channels), jnp.float32)
    piece = lax.all_gather(source_cells, "lon", axis=1, tiled=True)
    shard_count = piece.shape[1] // src_rows
    piece_rows = piece.T
    offsets = jnp.arange(shard_count, dtype=jnp.int32)[:, None] * src_rows
    picked = jnp.take(piece_rows, (offsets + sources).reshape(-1), axis=0)
    picked = picked.reshape(shard_count, slot_count, channels)
    accumulated = spread(empty, picked, weights, targets)
    regridded = accumulated.T.astype(jnp.bfloat16)
    hidden = jnp.dot(enc_w1, regridded, preferred_element_type=jnp.float32) + enc_b1[:, None]
    hidden = jax.nn.gelu(hidden, approximate=False).astype(jnp.bfloat16)
    encoded = (
        jnp.dot(enc_w2, hidden, preferred_element_type=jnp.float32) + enc_b2[:, None]
    ).astype(jnp.bfloat16)
    blocked = encoded.reshape(width, lat_dev, 1, lon_dev)
    circles = lax.all_to_all(blocked, "lon", split_axis=0, concat_axis=2, tiled=True).reshape(
        ch_dev * lat_dev, NLON
    )
    natural_order = jnp.arange(orders_total, dtype=jnp.int32)
    dft_basis = build_basis(natural_order, NLON)
    spectra = lax.dot_general(
        dft_basis, circles, (((1,), (1,)), ((), ())), preferred_element_type=jnp.float32
    )
    spectra = spectra.astype(jnp.bfloat16).reshape(orders_total, 2, ch_dev, lat_dev)
    by_order = lax.all_to_all(
        lax.all_to_all(spectra, "lat", split_axis=0, concat_axis=3, tiled=True),
        "lon",
        split_axis=0,
        concat_axis=2,
        tiled=True,
    )
    by_order = by_order.reshape(ord_dev, 2 * width, lat_total)
    coeffs = jnp.einsum(
        "mrt,mlt->mrl", by_order, fwd_table, preferred_element_type=jnp.float32
    ).astype(jnp.bfloat16)
    real_part = mix_weight[0]
    imag_part = mix_weight[1]
    mix_block = jnp.concatenate(
        [
            jnp.concatenate([real_part, -imag_part], axis=1),
            jnp.concatenate([imag_part, real_part], axis=1),
        ],
        axis=0,
    )
    mixed = jnp.einsum("gr,mrl->mgl", mix_block, coeffs, preferred_element_type=jnp.float32).astype(
        jnp.bfloat16
    )
    synth_in = jnp.einsum(
        "mrl,mtl->mrt", mixed, inv_table, preferred_element_type=jnp.float32
    ).astype(jnp.bfloat16)
    synth_in = synth_in.reshape(ord_dev, 2, width, lat_total)
    returned_modes = lax.all_to_all(
        lax.all_to_all(synth_in, "lon", split_axis=2, concat_axis=0, tiled=True),
        "lat",
        split_axis=3,
        concat_axis=0,
        tiled=True,
    )
    returned_modes = returned_modes.reshape(2 * orders_total, ch_dev * lat_dev)
    synthesis = lax.dot_general(
        returned_modes, dft_basis, (((0,), (0,)), ((), ())), preferred_element_type=jnp.float32
    )
    synthesis = synthesis.astype(jnp.bfloat16).reshape(ch_dev, lat_dev, lon_count, lon_dev)
    regained = lax.all_to_all(synthesis, "lon", split_axis=2, concat_axis=0, tiled=True).reshape(
        width, cells_dev
    )
    return (encoded.astype(jnp.float32) + regained.astype(jnp.float32)).astype(jnp.bfloat16)


def solution(mesh):
    in_specs = (
        P(None, ("lat", "lon")),
        P(("lat", "lon")),
        P(("lat", "lon")),
        P(("lat", "lon")),
        P(),
        P(),
        P(),
        P(),
        P(),
        P(("lat", "lon"), None, None),
        P(("lat", "lon"), None, None),
    )
    out_specs = P(None, ("lat", "lon"))
    return jax.shard_map(
        on_device, mesh=mesh, in_specs=in_specs, out_specs=out_specs, check_vma=False
    )
```

profile of v0, /device:TPU:0, one launch (start us, length us, event | category | flops | bytes accessed | tf_op | source)
XLA Modules:
  0.0 2873.5 jit_solution(5845581102192416864)
XLA Ops:
  0.0 0.0 copy-start
  0.0 0.1 broadcast_bitcast_fusion
  0.1 0.7 compare_and_fusion
  0.8 0.7 compare_select_fusion.1
  1.6 1.0 copy.131
  2.6 34.7 %all_gather.3 = bf16[73,4096]{0,1:T(8,128)(2,1)S(1)} all-gather(bf16[73,512]{0,1:T(8,128)(2,1)S(1)} %copy.131), channel_id=1, replica_groups=mesh['lat'=4,'lon'=8] {'lon'}, dimensions={1}, use_global_device_ids=true | all-gather | bytes 672768 | tf_op jit(solution)/shard_map/all_gather | solution.py:58
  37.3 43.5 %scatter_custom_fusion = f32[32400,73]{1,0:T(8,128)} fusion(s32[4096]{0:T(1024)S(1)} %get-tuple-element.9, f32[]{:T(128)} %constant.40.clone.1, f32[4096]{0:T(1024)} %param.14, pred[4096]{0:T(1024)(128)(4,1)S(1)} %compare_and_fusion, bf16[]{:T(256)} %constant.14.clone.1, bf16[4096,73]{1,0:T(8,128)(2,1)S(1)} %bitcast.142, s32[4096]{0:T(1024)S(1)} %get-tuple-element.10), kind=kCustom, calls=%fused_computation.39 | custom fusion | flops 1196032 | bytes 10546246 | tf_op jit(solution)/shard_map/scatter-add | solution.py:25
  80.8 80.5 %fusion.1 = bf16[256,32400]{0,1:T(8,128)(2,1)} fusion(bf16[256,256]{1,0:T(8,128)(2,1)S(1)} %copy-done, f32[256]{0:T(256)} %param.18, bf16[256,73]{0,1:T(8,128)(2,1)} %param.15, f32[256]{0:T(256)} %param.16, f32[32400,73]{1,0:T(8,128)} %scatter_custom_fusion), kind=kOutput, calls=%fused_computation.7 | convolution fusion | flops 6024099840 | bytes 26220096 | tf_op jit(solution)/shard_map/dot_general | solution.py:69
  161.2 22.4 reshape.127
  183.6 31.8 %copy.133 = bf16[256,180,1,180]{3,1,2,0:T(8,128)(2,1)} copy(bf16[256,180,1,180]{0,3,1,2:T(8,128)(2,1)} %reshape.127) | data formatting | bytes 33177600 | tf_op jit(solution)/shard_map/reshape | solution.py:71
  215.5 6.3 all-to-all-start
  221.8 12.8 multiply_convert_fusion
  234.6 1.9 pad_maximum_fusion
  236.4 7.4 copy.132
  243.8 3.6 convert_element_type.89
  247.4 489.1 %all-to-all-done = bf16[256,180,1,180]{3,1,2,0:T(8,128)(2,1)} async-done(((bf16[256,180,1,180]{3,1,2,0:T(8,128)(2,1)}), bf16[256,180,1,180]{3,1,2,0:T(8,128)(2,1)}, u32[]{:S(2)}, u32[]{:S(2)}) %all-to-all-start) | async-done | bytes 16588832 | tf_op jit(solution)/shard_map/all_to_all | solution.py:72
  736.5 30.4 %copy.134 = bf16[256,180,1,180]{3,0,1,2:T(8,128)(2,1)} copy(bf16[256,180,1,180]{3,1,2,0:T(8,128)(2,1)} %all-to-all-done) | data formatting | bytes 33177600 | tf_op jit(solution)/shard_map/all_to_all | solution.py:72
  766.9 40.9 %copy.135 = bf16[32,180,8,1,180]{1,0,4,2,3:T(8,128)(2,1)} copy(bf16[32,180,8,1,180]{4,0,2,1,3:T(8,128)(2,1)} %bitcast.135) | data formatting | bytes 33177600 | tf_op jit(solution)/shard_map/all_to_all | solution.py:72
  807.8 41.1 %reshape.128 = bf16[5760,1440]{0,1:T(8,128)(2,1)} reshape(bf16[32,180,8,1,180]{1,0,4,2,3:T(8,128)(2,1)} %copy.135) | data formatting | bytes 33177600 | tf_op jit(solution)/shard_map/reshape | solution.py:72
  849.0 24.5 convolution_convert_fusion.1
  873.5 52.8 %reshape.129 = bf16[512,2,32,180]{3,2,1,0:T(8,128)(2,1)} reshape(bf16[1024,5760]{1,0:T(8,128)(2,1)} %convolution_convert_fusion.1) | data formatting | bytes 23592960 | tf_op jit(solution)/shard_map/reshape | solution.py:80
  926.2 194.1 %all_to_all.90 = bf16[512,2,32,180]{3,2,1,0:T(8,128)(2,1)} all-to-all(bf16[512,2,32,180]{3,2,1,0:T(8,128)(2,1)} %reshape.129), channel_id=1, replica_groups=mesh['lat'=4,'lon'=8] {'lat'}, dimensions={0} | all-to-all | bytes 23592960 | tf_op jit(solution)/shard_map/all_to_all | solution.py:82
  1120.3 28.8 %copy.136 = bf16[4,128,2,32,180]{1,3,4,0,2:T(8,128)(2,1)} copy(bf16[4,128,2,32,180]{4,3,2,1,0:T(8,128)(2,1)} %bitcast.136) | data formatting | bytes 23592960 | tf_op jit(solution)/shard_map/all_to_all | solution.py:82
  1149.1 18.0 copy.137
  1167.1 5.3 all-to-all-start.2
  1172.5 0.7 slice_bitcast_fusion
  1173.2 272.1 %all-to-all-done.2 = bf16[128,2,32,720]{3,2,1,0:T(8,128)(2,1)} async-done(((bf16[128,2,32,720]{3,2,1,0:T(8,128)(2,1)}), bf16[128,2,32,720]{3,2,1,0:T(8,128)(2,1)}, u32[]{:S(2)}, u32[]{:S(2)}) %all-to-all-start.2) | async-done | bytes 11796512 | tf_op jit(solution)/shard_map/all_to_all | solution.py:81
  1445.3 10.8 copy.138
  1456.2 17.7 fusion.23
  1473.9 14.2 fusion.32
  1488.0 24.3 reshape.131
  1512.3 40.7 %copy.141 = bf16[16,2,256,720]{3,1,0,2:T(2,128)(2,1)} copy(bf16[16,2,256,720]{2,1,3,0:T(2,128)(2,1)} %reshape.131) | data formatting | bytes 23592960 | tf_op jit(solution)/shard_map/reshape | solution.py:107
  1553.0 277.3 %all_to_all.91 = bf16[16,2,256,720]{3,1,0,2:T(2,128)(2,1)S(1)} all-to-all(bf16[16,2,256,720]{3,1,0,2:T(2,128)(2,1)} %copy.141), channel_id=1, replica_groups=mesh['lat'=4,'lon'=8] {'lon'}, dimensions={2} | all-to-all | bytes 23592960 | tf_op jit(solution)/shard_map/all_to_all | solution.py:109
  1830.3 10.3 copy.142
  1840.6 5.4 copy.143
  1846.0 17.9 copy.144
  1863.9 138.9 %all_to_all.92 = bf16[128,2,32,720]{0,2,1,3:T(8,128)(2,1)} all-to-all(bf16[128,2,32,720]{0,2,1,3:T(8,128)(2,1)} %copy.144), channel_id=1, replica_groups=mesh['lat'=4,'lon'=8] {'lat'}, dimensions={3} | all-to-all | bytes 23592960 | tf_op jit(solution)/shard_map/all_to_all | solution.py:108
  2002.8 28.3 copy.146
  2031.0 28.7 reshape.132
  2059.7 25.7 convolution_convert_fusion
  2085.4 72.7 %reshape.133 = bf16[32,180,8,180]{1,0,3,2:T(8,128)(2,1)} reshape(bf16[5760,1440]{0,1:T(8,128)(2,1)} %convolution_convert_fusion) | data formatting | bytes 33177600 | tf_op jit(solution)/shard_map/reshape | solution.py:119
  2158.2 40.9 %copy.147 = bf16[32,180,8,180]{3,0,1,2:T(8,128)(2,1)} copy(bf16[32,180,8,180]{1,0,3,2:T(8,128)(2,1)} %reshape.133) | data formatting | bytes 33177600 | tf_op jit(solution)/shard_map/reshape | solution.py:119
  2199.1 513.4 %all_to_all.93 = bf16[32,180,8,180]{3,0,1,2:T(8,128)(2,1)S(1)} all-to-all(bf16[32,180,8,180]{3,0,1,2:T(8,128)(2,1)} %copy.147), channel_id=1, replica_groups=mesh['lat'=4,'lon'=8] {'lon'}, dimensions={2} | all-to-all | bytes 33177600 | tf_op jit(solution)/shard_map/all_to_all | solution.py:120
  2712.5 16.0 convert_bitcast_fusion
  2728.5 44.9 %copy.148 = f32[8,32,180,1,180]{4,2,1,0,3:T(8,128)} copy(f32[8,32,180,1,180]{4,1,2,0,3:T(8,128)} %convert_bitcast_fusion) | data formatting | bytes 66355200 | tf_op jit(solution)/shard_map/convert_element_type | solution.py:123
  2773.4 44.4 %reshape.134 = f32[256,32400]{1,0:T(8,128)} reshape(f32[8,32,180,1,180]{4,2,1,0,3:T(8,128)} %copy.148) | data formatting | bytes 66355200 | tf_op jit(solution)/shard_map/convert_element_type | solution.py:123
  2817.8 33.4 %copy.149 = f32[256,32400]{0,1:T(8,128)} copy(f32[256,32400]{1,0:T(8,128)} %reshape.134) | data formatting | bytes 66355200 | tf_op jit(solution)/shard_map/convert_element_type | solution.py:123
  2851.2 22.1 add_convert_fusion
  (14 shorter events, 0.0 us)
Async XLA Ops:
  0.0 80.8 %copy-start = (bf16[256,256]{1,0:T(8,128)(2,1)S(1)}, bf16[256,256]{1,0:T(8,128)(2,1)}, u32[]{:S(2)}) copy-start(bf16[256,256]{1,0:T(8,128)(2,1)} %param.17) | copy-start | bytes 393220
  215.5 521.1 %all-to-all-start = ((bf16[256,180,1,180]{3,1,2,0:T(8,128)(2,1)}), bf16[256,180,1,180]{3,1,2,0:T(8,128)(2,1)}, u32[]{:S(2)}, u32[]{:S(2)}) async-start(bf16[256,180,1,180]{3,1,2,0:T(8,128)(2,1)} %copy.133), calls=%async_computation | async-start | bytes 48234496 | tf_op jit(solution)/shard_map/all_to_all | solution.py:72
  807.8 41.1 %copy-start.2 = (bf16[1024,1440]{1,0:T(8,128)(2,1)S(1)}, bf16[1024,1440]{1,0:T(8,128)(2,1)}, u32[]{:S(2)}) copy-start(bf16[1024,1440]{1,0:T(8,128)(2,1)} %convert_element_type.89) | copy-start | bytes 8847364
  1149.1 23.3 copy-start.3
  1167.1 278.2 %all-to-all-start.2 = ((bf16[128,2,32,720]{3,2,1,0:T(8,128)(2,1)}), bf16[128,2,32,720]{3,2,1,0:T(8,128)(2,1)}, u32[]{:S(2)}, u32[]{:S(2)}) async-start(bf16[128,2,32,720]{3,2,1,0:T(8,128)(2,1)} %copy.137), calls=%async_computation.2 | async-start | bytes 25165824 | tf_op jit(solution)/shard_map/all_to_all | solution.py:81
  1173.2 283.0 %copy-start.4 = (bf16[256,256]{1,0:T(8,128)(2,1)S(1)}, bf16[256,256]{1,0:T(8,128)(2,1)}, u32[]{:S(2)}) copy-start(bf16[256,256]{1,0:T(8,128)(2,1)} %get-tuple-element.5) | copy-start | bytes 393220
  1173.2 283.0 %copy-start.5 = (bf16[256,256]{1,0:T(8,128)(2,1)S(1)}, bf16[256,256]{1,0:T(8,128)(2,1)}, u32[]{:S(2)}) copy-start(bf16[256,256]{1,0:T(8,128)(2,1)} %get-tuple-element.6) | copy-start | bytes 393220
  2817.8 55.4 %copy-start.1 = (bf16[256,256]{1,0:T(8,128)(2,1)S(1)}, bf16[256,256]{1,0:T(8,128)(2,1)}, u32[]{:S(2)}) copy-start(bf16[256,256]{1,0:T(8,128)(2,1)} %param.17) | copy-start | bytes 393220
where the time goes:
time: 2890 us; the launch traced here: 2870 us
  blocking collectives  1160 us (40%)
  waiting for transfers between devices  761 us (26%)
  local copies, waits for them, and re-layouts  682 us (24%)
  matrix products  163 us (6%)
  other arithmetic  97.6 us (3%)
    all_to_all x1, blocking collectives, on_device(): lax.all_to_all(synthesis, 'lon', split_axis=2, concat_axis=0, tiled=True)  513 us
    all_to_all x1, waiting for transfers between devices, on_device(): lax.all_to_all(blocked, 'lon', split_axis=0, concat_axis=2, tiled=True)  489 us
    all_to_all x1, blocking collectives, on_device(): lax.all_to_all(synth_in, 'lon', split_axis=2, concat_axis=0, tiled=True)  277 us
    all_to_all x1, waiting for transfers between devices, on_device(): lax.all_to_all(lax.all_to_all(spectra, 'lat', split_axis=0, concat_axis=3...  272 us
    all_to_all x1, blocking collectives, on_device(): lax.all_to_all(spectra, 'lat', split_axis=0, concat_axis=3, tiled=True)  194 us
    all_to_all x1, blocking collectives, on_device(): lax.all_to_all(lax.all_to_all(synth_in, 'lon', split_axis=2, concat_axis=...  139 us
    convert_element_type x3, local copies, waits for them, and re-layouts, on_device(): regained.astype(jnp.float32)  123 us
    reshape x2, local copies, waits for them, and re-layouts, on_device(): synthesis.astype(jnp.bfloat16).reshape(ch_dev, lat_dev, lon_count, lon_dev)  114 us
  transfers between devices with their start and end apart: 2, of which 2 were waited for; matrix products, arithmetic and copies ran while one was open for 1% of the time, Pallas kernels for 0%

commit v1 on v0

--- a/solution.py
+++ b/solution.py
@@ -1,12 +1,22 @@
+import functools
 import math
 
 import jax
 import jax.numpy as jnp
 from jax import lax
+from jax.experimental import pallas as pl
+from jax.experimental.pallas import tpu as pltpu
 from jax.sharding import PartitionSpec as P
 
 NLON = 1440
 ORDERS = 512
+LANES = 128
+TILE = 16
+WINDOW = 48
+VMEM_BYTES = 60 * 1024 * 1024
+
+F32 = jnp.float32
+BF16 = jnp.bfloat16
 
 
 def build_basis(order_list, points_total):
@@ -19,13 +29,377 @@
     return stacked.astype(jnp.bfloat16).reshape(2 * order_list.shape[0], points_total)
 
 
+def basis_by_point(order_list, points):
+    shape = points.shape + order_list.shape
+    angles = (points[..., None] * order_list % NLON).astype(F32) * (2.0 * math.pi / NLON)
+    factor = math.sqrt(2.0 / NLON)
+    stacked = jnp.stack([factor * jnp.cos(angles), -factor * jnp.sin(angles)], axis=-1)
+    return stacked.astype(BF16).reshape(shape[:-1] + (2 * shape[-1],))
+
+
 def spread(running, values, weights, targets):
     channels = values.shape[-1]
     contrib = values.astype(jnp.float32) * weights[:, :, None]
     return running.at[targets.reshape(-1)].add(contrib.reshape(-1, channels))
 
 
-def on_device(
+def mixing_matrix(mix_weight):
+    real_part = mix_weight[0]
+    imag_part = mix_weight[1]
+    return jnp.concatenate(
+        [
+            jnp.concatenate([real_part, -imag_part], axis=1),
+            jnp.concatenate([imag_part, real_part], axis=1),
+        ],
+        axis=0,
+    )
+
+
+def dense_encoder(piece, sources, targets, weights, cells_dev, enc_w1, enc_b1, enc_w2, enc_b2):
+    shard_count, slot_count = sources.shape
+    channels = piece.shape[0]
+    src_rows = piece.shape[1] // shard_count
+    piece_rows = piece.T
+    offsets = jnp.arange(shard_count, dtype=jnp.int32)[:, None] * src_rows
+    picked = jnp.take(piece_rows, (offsets + sources).reshape(-1), axis=0)
+    picked = picked.reshape(shard_count, slot_count, channels)
+    empty = jnp.zeros((cells_dev, channels), jnp.float32)
+    regridded = spread(empty, picked, weights, targets).T.astype(jnp.bfloat16)
+    hidden = jnp.dot(enc_w1, regridded, preferred_element_type=jnp.float32) + enc_b1[:, None]
+    hidden = jax.nn.gelu(hidden, approximate=False).astype(jnp.bfloat16)
+    return (
+        jnp.dot(enc_w2, hidden, preferred_element_type=jnp.float32) + enc_b2[:, None]
+    ).astype(jnp.bfloat16)
+
+
+def regrid_kernel(src_ref, cols_ref, row_ref, out_ref, contrib, *, channels, shards, slots, src_rows):
+    step = pl.program_id(0)
+    rows = out_ref.shape[0]
+
+    @pl.when(step == 0)
+    def _():
+        contrib[...] = jnp.zeros_like(contrib)
+        lane = lax.broadcasted_iota(jnp.int32, (slots, src_rows), 1).astype(F32)
+
+        def one(j, carry):
+            at = pl.ds(pl.multiple_of(j * slots, slots), slots)
+            index = cols_ref[at, 0:1]
+            weight = cols_ref[at, 1:2]
+            hot = (index == lane).astype(BF16)
+            picked = lax.dot_general(
+                hot, src_ref[j], (((1,), (1,)), ((), ())), preferred_element_type=F32
+            )
+            value = picked * weight
+            upper = value.astype(BF16)
+            lower = (value - upper.astype(F32)).astype(BF16)
+            contrib[at, 0:channels] = upper
+            contrib[at, LANES : LANES + channels] = lower
+            return carry
+
+        lax.fori_loop(0, shards, one, 0)
+
+    here = pl.ds(pl.multiple_of(step * rows, rows), rows)
+    cell = cols_ref[here, 2:3]
+    total = jnp.zeros((rows, 2 * LANES), F32)
+    for s in range(shards):
+        same = (cell == row_ref[:, s * slots : (s + 1) * slots]).astype(BF16)
+        total += jnp.dot(same, contrib[s * slots : (s + 1) * slots, :], preferred_element_type=F32)
+    merged = total[:, :LANES] + total[:, LANES:]
+    lane = lax.broadcasted_iota(jnp.int32, (rows, LANES), 1)
+    for place in range(4):
+        merged = jnp.where(lane == channels + place, cols_ref[here, 3 + place : 4 + place], merged)
+    out_ref[...] = merged.astype(BF16)
+
+
+def regrid_listed(source_all, recv_src, recv_cell, recv_weight, lat_dev, lon_dev, slot_count):
+    shards, channels, src_rows = source_all.shape
+    total = recv_src.shape[0]
+    ordered = jnp.sort(recv_cell)
+    lead = jnp.concatenate([jnp.ones((1,), jnp.bool_), ordered[1:] != ordered[:-1]])
+    bounds = jnp.arange(total, dtype=jnp.int32) * lon_dev
+    limits = jnp.arange(lat_dev + 1, dtype=jnp.int32) * lon_dev
+    starts = jnp.sum((recv_cell[None, :] < limits[:, None]).astype(jnp.int32), axis=1)
+    starts = jnp.zeros((total,), jnp.int32).at[: lat_dev + 1].set(starts)
+    del bounds
+    cols = jnp.stack(
+        [
+            recv_src.astype(F32),
+            recv_weight,
+            ordered.astype(F32),
+            (ordered % lon_dev).astype(F32),
+            lead.astype(F32),
+            (starts // 128).astype(F32),
+            (starts % 128).astype(F32),
+            jnp.zeros((total,), F32),
+        ],
+        axis=1,
+    )
+    rows = min(512, total)
+    return pl.pallas_call(
+        functools.partial(
+            regrid_kernel, channels=channels, shards=shards, slots=slot_count, src_rows=src_rows
+        ),
+        grid=(total // rows,),
+        out_shape=jax.ShapeDtypeStruct((total, LANES), BF16),
+        in_specs=[
+            pl.BlockSpec((shards, channels, src_rows), lambda i: (0, 0, 0)),
+            pl.BlockSpec((total, 8), lambda i: (0, 0)),
+            pl.BlockSpec((1, total), lambda i: (0, 0)),
+        ],
+        out_specs=pl.BlockSpec((rows, LANES), lambda i: (i, 0)),
+        scratch_shapes=[pltpu.VMEM((total, 2 * LANES), BF16)],
+        compiler_params=pltpu.CompilerParams(vmem_limit_bytes=VMEM_BYTES),
+    )(source_all, cols, recv_cell.astype(F32)[None, :])
+
+
+def zonal_kernel(
+    starts,
+    rows_ref,
+    w1_ref,
+    b1_ref,
+    w2_ref,
+    b2_ref,
+    basis_ref,
+    sums_ref,
+    out_ref,
+    delta,
+    hots,
+    base,
+    *,
+    channels,
+    blocks,
+    block_rows,
+):
+    step = pl.program_id(0)
+    total = blocks * block_rows
+    groups, lats, height, width = out_ref.shape
+    columns = groups * height
+    chunk = min(512, block_rows)
+
+    def encode(values):
+        hidden = jnp.dot(values, w1_ref[...], preferred_element_type=F32) + b1_ref[...]
+        hidden = 0.5 * hidden * (1.0 + lax.erf(hidden * math.sqrt(0.5)))
+        encoded = jnp.dot(hidden.astype(BF16), w2_ref[...], preferred_element_type=F32)
+        return (encoded + b2_ref[...]).astype(BF16).astype(F32)
+
+    @pl.when(step == 0)
+    def _():
+        empty = encode(jnp.zeros((16, LANES), BF16))[0:1]
+        base[...] = sums_ref[...] * empty
+        delta[pl.ds(total, WINDOW), :] = jnp.zeros((WINDOW, width), BF16)
+        hots[pl.ds(total, WINDOW), :] = jnp.zeros((WINDOW, columns), BF16)
+        points = basis_ref.shape[1]
+        lane = lax.broadcasted_iota(jnp.int32, (chunk, points), 1).astype(F32)
+
+        def one(j, carry):
+            at = pl.ds(pl.multiple_of(j * chunk, chunk), chunk)
+            values = rows_ref[at, :]
+            delta[at, :] = (encode(values) - empty).astype(BF16)
+            point = values[:, channels : channels + 1].astype(F32)
+            lead = values[:, channels + 1 : channels + 2].astype(F32)
+            point = jnp.where(lead > 0.5, point, -1.0)
+            hot = (point == lane).astype(BF16)
+            block = basis_ref[j // (block_rows // chunk)]
+            hots[at, :] = jnp.dot(hot, block, preferred_element_type=F32).astype(BF16)
+            return carry
+
+        lax.fori_loop(0, total // chunk, one, 0)
+
+    place = lax.broadcasted_iota(jnp.int32, (WINDOW, columns), 0)
+
+    def latitude(tt, carry):
+        t = step * lats + tt
+        lows, highs, firsts = [], [], []
+        most = jnp.int32(1)
+        for k in range(blocks):
+            low = starts[k, t] + k * block_rows
+            high = starts[k, t + 1] + k * block_rows
+            first = (low // TILE) * TILE
+            most = jnp.maximum(most, (high - first + WINDOW - 1) // WINDOW)
+            lows.append(low)
+            highs.append(high)
+            firsts.append(first)
+
+        def window(j, running):
+            left, right = [], []
+            for k in range(blocks):
+                first = jnp.minimum(firsts[k] + j * WINDOW, total)
+                first = pl.multiple_of(first, TILE)
+                at = pl.ds(first, WINDOW)
+                inside = (place >= lows[k] - first) & (place < highs[k] - first)
+                left.append(jnp.where(inside, hots[at, :].astype(F32), 0.0).astype(BF16))
+                right.append(delta[at, :])
+            return running + lax.dot_general(
+                jnp.concatenate(left, axis=0),
+                jnp.concatenate(right, axis=0),
+                (((0,), (0,)), ((), ())),
+                preferred_element_type=F32,
+            )
+
+        result = window(0, base[...])
+        result = lax.fori_loop(1, most, window, result).astype(BF16)
+        for g in range(groups):
+            out_ref[g, tt] = result[g * height : (g + 1) * height, :]
+        return carry
+
+    lax.fori_loop(0, lats, latitude, 0)
+
+
+def zonal_transform(
+    rows, starts, w1, b1, w2, b2, basis, sums, lat_dev, groups, channels, lats=15
+):
+    blocks, block_rows, _ = rows.shape
+    width = w2.shape[1]
+    columns = basis.shape[2]
+    height = columns // groups
+    total = blocks * block_rows
+    whole = lambda shape: pl.BlockSpec(
+        shape, lambda i, s: (0,) * len(shape), pipeline_mode=pl.Buffered(1)
+    )
+    return pl.pallas_call(
+        functools.partial(
+            zonal_kernel, channels=channels, blocks=blocks, block_rows=block_rows
+        ),
+        grid_spec=pltpu.PrefetchScalarGridSpec(
+            num_scalar_prefetch=1,
+            grid=(lat_dev // lats,),
+            in_specs=[
+                whole((total, LANES)),
+                whole(w1.shape),
+                whole(b1.shape),
+                whole(w2.shape),
+                whole(b2.shape),
+                whole(basis.shape),
+                whole(sums.shape),
+            ],
+            out_specs=pl.BlockSpec((groups, lats, height, width), lambda i, s: (0, i, 0, 0)),
+            scratch_shapes=[
+                pltpu.VMEM((total + WINDOW, width), BF16),
+                pltpu.VMEM((total + WINDOW, columns), BF16),
+                pltpu.VMEM((columns, width), F32),
+            ],
+        ),
+        out_shape=jax.ShapeDtypeStruct((groups, lat_dev, height, width), BF16),
+        compiler_params=pltpu.CompilerParams(vmem_limit_bytes=VMEM_BYTES),
+    )(starts, rows.reshape(total, LANES), w1, b1, w2, b2, basis, sums)
+
+
+def orders_kernel(spec_ref, fwd_ref, inv_ref, mix_ref, swap_ref, out_ref, taken, made, *, group):
+    order = lax.rem(pl.program_id(0), group)
+    lat_total, _, width = spec_ref.shape
+    parts, halves, part_lats, _, lanes = out_ref.shape
+    side = 2 * group
+
+    @pl.when(order == 0)
+    def _():
+        def one(j, carry):
+            at = pl.ds(pl.multiple_of(j * side, side), side)
+            block = spec_ref[at].reshape(side * side, width)
+            turned = jnp.dot(swap_ref[...], block, preferred_element_type=F32).astype(BF16)
+            taken[:, at, :] = turned.reshape(side, side, width)
+            return carry
+
+        lax.fori_loop(0, lat_total // side, one, 0)
+
+    spectrum = jnp.concatenate([taken[2 * order], taken[2 * order + 1]], axis=1)
+    coeffs = jnp.dot(fwd_ref[0], spectrum, preferred_element_type=F32).astype(BF16)
+    mixed = jnp.dot(coeffs, mix_ref[...], preferred_element_type=F32).astype(BF16)
+    made[order] = jnp.dot(inv_ref[0], mixed, preferred_element_type=F32).astype(BF16)
+
+    @pl.when(order == group - 1)
+    def _():
+        def one(j, carry):
+            first = pl.multiple_of(j * side, side)
+            at = pl.ds(first, side)
+            columns = []
+            for h in range(halves):
+                pieces = []
+                for r in range(group):
+                    for c in range(2):
+                        low = (c * halves + h) * lanes
+                        pieces.append(made[r, at, low : low + lanes])
+                columns.append(jnp.concatenate(pieces, axis=0))
+            block = jnp.concatenate(columns, axis=1)
+            turned = jnp.dot(swap_ref[...], block, preferred_element_type=F32).astype(BF16)
+            for i in range(side):
+                lat = first + i
+                for h in range(halves):
+                    out_ref[lat // part_lats, h, lat % part_lats] = turned[
+                        i * side : (i + 1) * side, h * lanes : (h + 1) * lanes
+                    ]
+            return carry
+
+        lax.fori_loop(0, lat_total // side, one, 0)
+
+
+def order_steps(spectra, fwd_table, inv_table, mix_t, parts, halves):
+    lat_total, height, width = spectra.shape
+    ord_dev, degrees, _ = fwd_table.shape
+    group = 8
+    side = 2 * group
+    index = jnp.arange(side * side, dtype=jnp.int32)
+    swapped = (index % side) * side + index // side
+    swap = (swapped[:, None] == index[None, :]).astype(BF16)
+    both = 2 * width
+    part_lats = lat_total // parts
+    return pl.pallas_call(
+        functools.partial(orders_kernel, group=group),
+        grid=(ord_dev,),
+        in_specs=[
+            pl.BlockSpec((lat_total, side, width), lambda r: (0, r // group, 0)),
+            pl.BlockSpec((1, degrees, lat_total), lambda r: (r, 0, 0)),
+            pl.BlockSpec((1, lat_total, degrees), lambda r: (r, 0, 0)),
+            pl.BlockSpec((both, both), lambda r: (0, 0)),
+            pl.BlockSpec((side * side, side * side), lambda r: (0, 0)),
+        ],
+        out_specs=pl.BlockSpec(
+            (parts, halves, part_lats, side, width // halves),
+            lambda r: (0, 0, 0, r // group, 0),
+        ),
+        out_shape=jax.ShapeDtypeStruct(
+            (parts, halves, part_lats, height, width // halves), BF16
+        ),
+        scratch_shapes=[
+            pltpu.VMEM((side, lat_total, width), BF16),
+            pltpu.VMEM((group, lat_total, both), BF16),
+        ],
+        compiler_params=pltpu.CompilerParams(vmem_limit_bytes=VMEM_BYTES),
+    )(spectra, fwd_table, inv_table, mix_t, swap)
+
+
+def synthesis_kernel(modes_ref, basis_ref, out_ref):
+    sources, lats, height, lanes = modes_ref.shape
+    blocks, _, points, _ = out_ref.shape
+    right = jnp.concatenate(
+        [modes_ref[:, t].reshape(sources * height, lanes) for t in range(lats)], axis=1
+    )
+
+    def one(k, carry):
+        value = jnp.dot(basis_ref[k], right, preferred_element_type=F32).astype(BF16)
+        for t in range(lats):
+            out_ref[k, t] = value[:points, t * lanes : (t + 1) * lanes]
+        return carry
+
+    lax.fori_loop(0, blocks, one, 0)
+
+
+def synthesis_steps(modes, basis, points, lats):
+    sources, lat_part, height, lanes = modes.shape
+    blocks = basis.shape[0]
+    return pl.pallas_call(
+        synthesis_kernel,
+        grid=(lat_part // lats,),
+        in_specs=[
+            pl.BlockSpec((sources, lats, height, lanes), lambda i: (0, i, 0, 0)),
+            pl.BlockSpec(basis.shape, lambda i: (0, 0, 0)),
+        ],
+        out_specs=pl.BlockSpec((blocks, lats, points, lanes), lambda i: (0, i, 0, 0)),
+        out_shape=jax.ShapeDtypeStruct((blocks, lat_part, points, lanes), BF16),
+        compiler_params=pltpu.CompilerParams(vmem_limit_bytes=VMEM_BYTES),
+    )(modes, basis)
+
+
+def listed_plan(
     source_cells,
     recv_src,
     recv_cell,
@@ -41,7 +415,108 @@
     lon_count = lax.axis_size("lon")
     lat_count = lax.axis_size("lat")
     channels = source_cells.shape[0]
-    src_rows = source_cells.shape[1]
+    slot_count = recv_src.shape[0] // lon_count
+    lat_total = fwd_table.shape[2]
+    lat_dev = lat_total // lat_count
+    lon_dev = NLON // lon_count
+    cells_dev = lat_dev * lon_dev
+    width = enc_w1.shape[0]
+    ord_dev = fwd_table.shape[0]
+    halves = width // LANES
+    quarters = lon_count // halves
+    part_lats = lat_dev // quarters
+
+    source_all = lax.all_gather(source_cells, "lon", axis=0, tiled=False)
+    listed = regrid_listed(
+        source_all, recv_src, recv_cell, recv_weight, lat_dev, lon_dev, slot_count
+    )
+    band = lax.all_gather(listed, "lon", axis=0, tiled=False)
+    coded = band[:, : lat_dev + 1, channels + 2 : channels + 4].astype(jnp.int32)
+    starts = coded[:, :, 0] * 128 + coded[:, :, 1]
+
+    mine = lax.axis_index("lon")
+    owned = (
+        (jnp.arange(lat_count, dtype=jnp.int32)[:, None] * lon_count + mine) * ord_dev
+        + jnp.arange(ord_dev, dtype=jnp.int32)[None, :]
+    ).reshape(-1)
+    point_rows = -(-lon_dev // LANES) * LANES
+    at = jnp.arange(lon_count, dtype=jnp.int32)[:, None] * lon_dev + jnp.arange(
+        point_rows, dtype=jnp.int32
+    )
+    inside = (jnp.arange(point_rows) < lon_dev)[None, :, None]
+    basis_in = jnp.where(inside, basis_by_point(owned, at), 0)
+    sums = jnp.sum(basis_in.astype(F32), axis=(0, 1))[:, None]
+    w1 = jnp.zeros((LANES, width), BF16).at[:channels].set(enc_w1.T)
+    spectra = zonal_transform(
+        band,
+        starts,
+        w1,
+        enc_b1[None, :],
+        enc_w2.T,
+        enc_b2[None, :],
+        basis_in,
+        sums,
+        lat_dev,
+        lat_count,
+        channels,
+    )
+    spectra = lax.all_to_all(spectra, "lat", split_axis=0, concat_axis=0, tiled=True)
+    spectra = spectra.reshape(lat_total, 2 * ord_dev, width)
+    made = order_steps(
+        spectra,
+        fwd_table,
+        inv_table,
+        mixing_matrix(mix_weight).T,
+        lat_count * quarters,
+        halves,
+    )
+    made = made.reshape(lat_count * lon_count, part_lats, 2 * ord_dev, LANES)
+    modes = lax.all_to_all(made, ("lat", "lon"), split_axis=0, concat_axis=0, tiled=True)
+
+    pad_points = -(-lon_dev // TILE) * TILE
+    at = jnp.arange(lon_count, dtype=jnp.int32)[:, None] * lon_dev + jnp.arange(
+        pad_points, dtype=jnp.int32
+    )
+    inside = (jnp.arange(pad_points) < lon_dev)[None, :, None]
+    basis_out = basis_by_point(jnp.arange(ORDERS, dtype=jnp.int32), at)
+    basis_out = jnp.where(inside, basis_out, 0)
+    grid_part = synthesis_steps(modes, basis_out, lon_dev, 9)
+    grid_part = lax.all_to_all(grid_part, "lon", split_axis=0, concat_axis=0, tiled=True)
+    spectral = (
+        grid_part.reshape(quarters, halves, part_lats, lon_dev, LANES)
+        .transpose(1, 4, 0, 2, 3)
+        .reshape(width, cells_dev)
+    )
+    piece = source_all.transpose(1, 0, 2).reshape(channels, -1)
+    encoded = dense_encoder(
+        piece,
+        recv_src.reshape(lon_count, slot_count),
+        recv_cell.reshape(lon_count, slot_count),
+        recv_weight.reshape(lon_count, slot_count),
+        cells_dev,
+        enc_w1,
+        enc_b1,
+        enc_w2,
+        enc_b2,
+    )
+    return (encoded.astype(F32) + spectral.astype(F32)).astype(BF16)
+
+
+def dense_plan(
+    source_cells,
+    recv_src,
+    recv_cell,
+    recv_weight,
+    enc_w1,
+    enc_b1,
+    enc_w2,
+    enc_b2,
+    mix_weight,
+    fwd_table,
+    inv_table,
+):
+    lon_count = lax.axis_size("lon")
+    lat_count = lax.axis_size("lat")
     slot_count = recv_src.shape[0] // lon_count
     sources = recv_src.reshape(lon_count, slot_count)
     targets = recv_cell.reshape(lon_count, slot_count)
@@ -54,20 +529,10 @@
     ch_dev = width // lon_count
     orders_total = ORDERS
     ord_dev = fwd_table.shape[0]
-    empty = jnp.zeros((cells_dev, channels), jnp.float32)
     piece = lax.all_gather(source_cells, "lon", axis=1, tiled=True)
-    shard_count = piece.shape[1] // src_rows
-    piece_rows = piece.T
-    offsets = jnp.arange(shard_count, dtype=jnp.int32)[:, None] * src_rows
-    picked = jnp.take(piece_rows, (offsets + sources).reshape(-1), axis=0)
-    picked = picked.reshape(shard_count, slot_count, channels)
-    accumulated = spread(empty, picked, weights, targets)
-    regridded = accumulated.T.astype(jnp.bfloat16)
-    hidden = jnp.dot(enc_w1, regridded, preferred_element_type=jnp.float32) + enc_b1[:, None]
-    hidden = jax.nn.gelu(hidden, approximate=False).astype(jnp.bfloat16)
-    encoded = (
-        jnp.dot(enc_w2, hidden, preferred_element_type=jnp.float32) + enc_b2[:, None]
-    ).astype(jnp.bfloat16)
+    encoded = dense_encoder(
+        piece, sources, targets, weights, cells_dev, enc_w1, enc_b1, enc_w2, enc_b2
+    )
     blocked = encoded.reshape(width, lat_dev, 1, lon_dev)
     circles = lax.all_to_all(blocked, "lon", split_axis=0, concat_axis=2, tiled=True).reshape(
         ch_dev * lat_dev, NLON
@@ -89,15 +554,7 @@
     coeffs = jnp.einsum(
         "mrt,mlt->mrl", by_order, fwd_table, preferred_element_type=jnp.float32
     ).astype(jnp.bfloat16)
-    real_part = mix_weight[0]
-    imag_part = mix_weight[1]
-    mix_block = jnp.concatenate(
-        [
-            jnp.concatenate([real_part, -imag_part], axis=1),
-            jnp.concatenate([imag_part, real_part], axis=1),
-        ],
-        axis=0,
-    )
+    mix_block = mixing_matrix(mix_weight)
     mixed = jnp.einsum("gr,mrl->mgl", mix_block, coeffs, preferred_element_type=jnp.float32).astype(
         jnp.bfloat16
     )
@@ -138,6 +595,26 @@
         P(("lat", "lon"), None, None),
     )
     out_specs = P(None, ("lat", "lon"))
+    lon_count = mesh.shape["lon"]
+    lat_count = mesh.shape["lat"]
+
+    def on_device(*arrays):
+        slots = arrays[1].shape[0]
+        width = arrays[4].shape[0]
+        ord_dev, _, lat_total = arrays[9].shape
+        lat_dev = lat_total // lat_count
+        cells_dev = lat_dev * (NLON // lon_count)
+        halves = max(1, width // LANES)
+        fits = (
+            slots * 4 <= cells_dev
+            and width % LANES == 0
+            and lon_count % halves == 0
+            and lat_dev % (9 * lon_count // halves) == 0
+            and ord_dev % 8 == 0
+            and lat_total % TILE == 0
+        )
+        return listed_plan(*arrays) if fits else dense_plan(*arrays)
+
     return jax.shard_map(
         on_device, mesh=mesh, in_specs=in_specs, out_specs=out_specs, check_vma=False
     )

time: 2890 us -> 1320 us (0.46)
  blocking collectives: 1160 us -> 35.9 us
  local copies, waits for them, and re-layouts: 682 us -> 77.6 us
  Pallas kernels: 0 us -> 209 us
  matrix products: 163 us -> 83 us
    all_to_all x4 -> x0, blocking collectives: 1120 us -> none  [the longest x1 513 us: on_device(): lax.all_to_all(synthesis, 'lon', split_axis=2, concat_axis=0, tiled=True)]
    reshape x9 -> x1, local copies, waits for them, and re-layouts: 355 us -> 0.68 us  [listed_plan(): piece = source_all.transpose(1, 0, 2).reshape(channels, -1)]
    pallas_call x0 -> x4, Pallas kernels: none -> 209 us  [the longest x1 97.1 us: zonal_transform(): pl.pallas_call(functools.partial(zonal_kernel, channels=channels, blocks=...]
    all_to_all x9 -> x0, local copies, waits for them, and re-layouts: 191 us -> none  [the longest x2 71.3 us: on_device(): lax.all_to_all(blocked, 'lon', split_axis=0, concat_axis=2, tiled=True)]
    all_gather x0 -> x1, waiting for transfers between devices: none -> 118 us  [listed_plan(): band = lax.all_gather(listed, 'lon', axis=0, tiled=False)]
    all_to_all x2 -> x3, waiting for transfers between devices: 761 us -> 666 us  [the longest x1 322 us: listed_plan(): lax.all_to_all(grid_part, 'lon', split_axis=0, concat_axis=0, tiled=True)]
    dot_general x5 -> x1, matrix products: 163 us -> 83 us  [dense_encoder(): jnp.dot(enc_w2, hidden, preferred_element_type=jnp.float32)]
    convert_element_type x4 -> x3, local copies, waits for them, and re-layouts: 126 us -> 52.4 us  [the longest x1 46.2 us: listed_plan(): return (encoded.astype(F32) + spectral.astype(F32)).astype(BF16)]
  transfers between devices with their start and end apart: 2 -> 4, of which waited for: 2 -> 4; matrix products, arithmetic and copies ran while one was open for 1% -> 8% of each run, Pallas kernels for 0% -> 0%
where the time goes in v1:
time: 1320 us
  waiting for transfers between devices  784 us (59%)
  Pallas kernels  209 us (16%)
  other arithmetic  101 us (8%)
  matrix products  83 us (6%)
  local copies, waits for them, and re-layouts  77.6 us (6%)
  blocking collectives  35.9 us (3%)
  starting transfers between devices  18.8 us (1%)
  between operations  13.6 us (1%)
    all_to_all x1, waiting for transfers between devices, listed_plan(): lax.all_to_all(grid_part, 'lon', split_axis=0, concat_axis=0, tiled=True)  322 us
    all_to_all x1, waiting for transfers between devices, listed_plan(): lax.all_to_all(made, ('lat', 'lon'), split_axis=0, concat_axis=0, tiled=T...  233 us
    all_gather x1, waiting for transfers between devices, listed_plan(): band = lax.all_gather(listed, 'lon', axis=0, tiled=False)  118 us
    all_to_all x1, waiting for transfers between devices, listed_plan(): lax.all_to_all(spectra, 'lat', split_axis=0, concat_axis=0, tiled=True)  112 us
    pallas_call x1, Pallas kernels, zonal_transform(): pl.pallas_call(functools.partial(zonal_kernel, channels=channels, blocks=...  97.1 us
    dot_general x1, matrix products, dense_encoder(): jnp.dot(enc_w2, hidden, preferred_element_type=jnp.float32)  83 us
    pallas_call x1, Pallas kernels, order_steps(): pl.pallas_call(functools.partial(orders_kernel, group=group), grid=(ord_d...  63.2 us
    convert_element_type x1, local copies, waits for them, and re-layouts, listed_plan(): return (encoded.astype(F32) + spectral.astype(F32)).astype(BF16)  46.2 us
  transfers between devices with their start and end apart: 4, of which 4 were waited for; matrix products, arithmetic and copies ran while one was open for 8% of the time, Pallas kernels for 0%

profile of v1, /device:TPU:0, one launch (start us, length us, event | category | flops | bytes accessed | tf_op | source)
XLA Modules:
  0.0 1323.0 jit_solution(17603311595976463853)
XLA Ops:
  6.5 6.5 sort.15
  13.1 0.1 slice_compare_fusion
  13.2 0.1 broadcast_bitcast_fusion
  13.3 1.2 convert_reduce_fusion
  14.5 1.4 compare_select_fusion.1
  15.9 0.1 add_convert_fusion
  16.0 0.9 stack.39
  16.9 1.9 copy.76.cols_ref
  18.8 35.9 %all-gather.2.src_ref = bf16[8,73,512]{2,1,0:T(8,128)(2,1)} all-gather(bf16[1,73,512]{2,1,0:T(8,128)(2,1)} %bitcast.135), channel_id=2, replica_groups=mesh['lat'=4,'lon'=8] {'lon'}, dimensions={0}, use_global_device_ids=true | all-gather | bytes 672768 | tf_op jit(solution)/shard_map/all_gather | solution.py:429
  54.8 15.8 %shard_map.109 = bf16[4096,128]{1,0:T(8,128)(2,1)} custom-call(bf16[8,73,512]{2,1,0:T(8,128)(2,1)} %all-gather.2.src_ref, f32[4096,8]{1,0:T(8,128)} %copy.76.cols_ref, f32[1,4096]{1,0:T(1,128)} %bitcast.137), custom_call_target="tpu_custom_call" | custom-call | tf_op jit(solution)/shard_map/pallas_call | solution.py:138
  70.6 0.1 iota_add_fusion.2
  70.7 0.1 add.224
  70.8 0.1 iota_add_fusion.1
  70.9 2.6 cosine_multiply_fusion
  73.5 0.3 convert_reduce_fusion.1
  73.8 0.4 copy.79
  74.2 0.7 broadcast_in_dim.92.sums_ref
  74.9 1.6 copy.78
  76.6 1.4 scatter.9.w1_ref
  78.0 0.9 broadcast_select_fusion.1.basis_ref
  78.9 117.7 %all-gather.5.cloned.1.call-done.rows_ref = bf16[32768,128]{1,0:T(8,128)(2,1)} async-done(((bf16[4096,128]{1,0:T(8,128)(2,1)}), bf16[32768,128]{1,0:T(8,128)(2,1)}) %all-gather.5.cloned.1.call-update) | async-done | bytes 8388624 | tf_op jit(solution)/shard_map/all_gather | solution.py:433
  196.6 1.2 slice.57
  197.8 0.2 copy.88
  198.0 0.6 fusion.86.starts
  198.6 97.1 %shard_map.110 = bf16[4,180,32,256]{3,2,1,0:T(8,128)(2,1)} custom-call(s32[8,181]{1,0:T(8,128)} %fusion.86.starts, bf16[32768,128]{1,0:T(8,128)(2,1)} %all-gather.5.cloned.1.call-done.rows_ref, bf16[128,256]{1,0:T(8,128)(2,1)} %scatter.9.w1_ref, f32[1,256]{1,0:T(1,128)} %bitcast.144, bf16[256,256]{1,0:T(8,128)(2,1)} %bitcast.131, f32[1,256]{1,0:T(1,128)} %bitcast.145, ...), custom_call_target="tpu_custom_call" | custom-call | tf_op jit(solution)/shard_map/pallas_call | solution.py:259
  295.7 6.2 all-to-all-start
  302.0 0.1 copy.90
  302.1 0.1 copy.89
  302.2 16.2 %copy.83.fwd_ref = bf16[16,512,720]{2,1,0:T(8,128)(2,1)} copy(bf16[16,512,720]{1,2,0:T(8,128)(2,1)} %param.24) | data formatting | bytes 23592960 | tf_op args[9]
  318.5 0.8 maximum_bitcast_fusion.mix_ref
  319.3 0.7 fusion.77.swap_ref
  320.0 111.6 %all-to-all-done = bf16[4,180,32,256]{3,2,1,0:T(8,128)(2,1)} async-done(((bf16[4,180,32,256]{3,2,1,0:T(8,128)(2,1)}), bf16[4,180,32,256]{3,2,1,0:T(8,128)(2,1)}, u32[]{:S(2)}, u32[]{:S(2)}) %all-to-all-start) | async-done | bytes 11796512 | tf_op jit(solution)/shard_map/all_to_all | solution.py:463
  431.7 63.2 %shard_map.111 = bf16[16,2,45,32,128]{4,3,2,1,0:T(8,128)(2,1)} custom-call(bf16[720,32,256]{2,1,0:T(8,128)(2,1)} %bitcast.21.spec_ref, bf16[16,512,720]{2,1,0:T(8,128)(2,1)} %copy.83.fwd_ref, bf16[16,720,512]{2,1,0:T(8,128)(2,1)} %inv_ref.1, bf16[512,512]{1,0:T(8,128)(2,1)} %maximum_bitcast_fusion.mix_ref, bf16[256,256]{1,0:T(8,128)(2,1)} %fusion.77.swap_ref), custom_call_target="tpu_custom_call" | custom-call | tf_op jit(solution)/shard_map/pallas_call | solution.py:345
  494.9 3.9 all-to-all-start.1
  498.8 0.1 iota_add_fusion
  498.9 18.0 %multiply_convert_fusion.1 = (bf16[8,192,512,1]{1,0,3,2:T(8,128)(2,1)S(1)}, bf16[8,192,512,1]{1,0,3,2:T(8,128)(2,1)S(1)}) fusion(s32[8,192]{1,0:T(8,128)S(1)} %iota_add_fusion), kind=kLoop, calls=%fused_computation.72 | loop fusion | flops 10223616 | bytes 3151872 | tf_op jit(solution)/shard_map/convert.4
  516.9 2.7 pad_maximum_fusion
  519.6 5.7 copy.84
  525.3 1.9 broadcast_select_fusion.basis_ref
  527.3 232.9 %all-to-all-done.1.modes_ref = bf16[32,45,32,128]{3,2,1,0:T(8,128)(2,1)} async-done(((bf16[32,45,32,128]{3,2,1,0:T(8,128)(2,1)}), bf16[32,45,32,128]{3,2,1,0:T(8,128)(2,1)}, u32[]{:S(2)}, u32[]{:S(2)}) %all-to-all-start.1) | async-done | bytes 11796512 | tf_op jit(solution)/shard_map/all_to_all | solution.py:474
  760.1 32.6 %shard_map.112 = bf16[8,45,180,128]{3,2,1,0:T(8,128)(2,1)} custom-call(bf16[32,45,32,128]{3,2,1,0:T(8,128)(2,1)} %all-to-all-done.1.modes_ref, bf16[8,192,1024]{2,1,0:T(8,128)(2,1)} %broadcast_select_fusion.basis_ref), custom_call_target="tpu_custom_call" | custom-call | tf_op jit(solution)/shard_map/pallas_call | solution.py:389
  792.8 8.6 all-to-all-start.2
  801.4 0.7 copy.86
  802.2 44.4 %scatter_custom_fusion = f32[32400,73]{1,0:T(8,128)} fusion(s32[4096]{0:T(1024)S(1)} %get-tuple-element.38, f32[]{:T(128)} %constant.188.clone.1, f32[4096]{0:T(1024)S(1)} %copy-done.3, pred[4096]{0:T(1024)(128)(4,1)S(1)} %compare_and_fusion, bf16[]{:T(256)} %constant.194.clone.1, bf16[4096,73]{1,0:T(8,128)(2,1)S(1)} %bitcast.128, ...), kind=kCustom, calls=%fused_computation.65 | custom fusion | flops 1196032 | bytes 10546246 | tf_op jit(solution)/shard_map/scatter-add | solution.py:43
  846.6 321.9 %all-to-all-done.2 = bf16[8,45,180,128]{3,2,1,0:T(8,128)(2,1)} async-done(((bf16[8,45,180,128]{3,2,1,0:T(8,128)(2,1)}), bf16[8,45,180,128]{3,2,1,0:T(8,128)(2,1)}, u32[]{:S(2)}, u32[]{:S(2)}) %all-to-all-start.2) | async-done | bytes 16588832 | tf_op jit(solution)/shard_map/all_to_all | solution.py:484
  1168.5 18.4 %convert_bitcast_fusion = f32[2,128,4,45,180]{1,4,3,0,2:T(8,128)} fusion(bf16[4,2,45,180,128]{4,3,2,1,0:T(8,128)(2,1)} %bitcast.30), kind=kLoop, calls=%fused_computation.10 | loop fusion | flops 8294400 | bytes 49766400 | tf_op jit(solution)/shard_map/convert_element_type | solution.py:502
  1186.9 46.2 %copy.85 = f32[2,128,4,45,180]{1,0,4,3,2:T(2,128)} copy(f32[2,128,4,45,180]{1,4,3,0,2:T(8,128)} %convert_bitcast_fusion) | data formatting | bytes 66355200 | tf_op jit(solution)/shard_map/convert_element_type | solution.py:502
  1233.1 83.0 %fusion.4 = bf16[256,32400]{0,1:T(8,128)(2,1)} fusion(bf16[256,256]{1,0:T(8,128)(2,1)S(1)} %copy-done.2, f32[4050,8,2,128]{3,2,1,0:T(2,128)} %bitcast.124, f32[256]{0:T(256)S(1)} %copy-done.7, bf16[256,73]{0,1:T(8,128)(2,1)S(1)} %copy-done.5, f32[256]{0:T(256)S(1)} %copy-done.6, f32[32400,73]{1,0:T(8,128)} %scatter_custom_fusion), kind=kOutput, calls=%fused_computation.9 | convolution fusion | flops 6048983040 | bytes 59397696 | tf_op jit(solution)/shard_map/dot_general | solution.py:71
  (35 shorter events, 0.2 us)
Async XLA Ops:
  6.5 295.5 %copy-start.1 = (bf16[2,256,256]{2,1,0:T(8,128)(2,1)S(1)}, bf16[2,256,256]{2,1,0:T(8,128)(2,1)}, u32[]{:S(2)}) copy-start(bf16[2,256,256]{2,1,0:T(8,128)(2,1)} %param.23) | copy-start | bytes 786436
  6.5 190.1 %all-gather.5.cloned.1.call-start = ((), (), s32[]{:S(2)}) async-start(), calls=%async_computation.3 | async-start | bytes 9437184 | tf_op jit(solution)/shard_map/all_gather | solution.py:433
  295.7 135.9 %all-to-all-start = ((bf16[4,180,32,256]{3,2,1,0:T(8,128)(2,1)}), bf16[4,180,32,256]{3,2,1,0:T(8,128)(2,1)}, u32[]{:S(2)}, u32[]{:S(2)}) async-start(bf16[4,180,32,256]{3,2,1,0:T(8,128)(2,1)} %shard_map.110), calls=%async_computation | async-start | bytes 23592960 | tf_op jit(solution)/shard_map/all_to_all | solution.py:463
  494.9 265.3 %all-to-all-start.1 = ((bf16[32,45,32,128]{3,2,1,0:T(8,128)(2,1)}), bf16[32,45,32,128]{3,2,1,0:T(8,128)(2,1)}, u32[]{:S(2)}, u32[]{:S(2)}) async-start(bf16[32,45,32,128]{3,2,1,0:T(8,128)(2,1)} %bitcast.123), calls=%async_computation.1 | async-start | bytes 23592960 | tf_op jit(solution)/shard_map/all_to_all | solution.py:474
  527.3 274.1 %copy-start = (bf16[8,73,512]{2,1,0:T(8,128)(2,1)S(1)}, bf16[8,73,512]{2,1,0:T(8,128)(2,1)}, u32[]{:S(2)}) copy-start(bf16[8,73,512]{2,1,0:T(8,128)(2,1)} %all-gather.2.src_ref) | copy-start | bytes 1794052
  527.3 274.8 %copy-start.4 = (s32[4096]{0:T(1024)S(1)}, s32[4096]{0:T(1024)}, u32[]{:S(2)}) copy-start(s32[4096]{0:T(1024)} %param.16) | copy-start | bytes 49156
  527.3 274.9 %copy-start.3 = (f32[4096]{0:T(1024)S(1)}, f32[4096]{0:T(1024)}, u32[]{:S(2)}) copy-start(f32[4096]{0:T(1024)} %param.18) | copy-start | bytes 49156
  792.8 375.7 %all-to-all-start.2 = ((bf16[8,45,180,128]{3,2,1,0:T(8,128)(2,1)}), bf16[8,45,180,128]{3,2,1,0:T(8,128)(2,1)}, u32[]{:S(2)}, u32[]{:S(2)}) async-start(bf16[8,45,180,128]{3,2,1,0:T(8,128)(2,1)} %shard_map.112), calls=%async_computation.2 | async-start | bytes 33914880 | tf_op jit(solution)/shard_map/all_to_all | solution.py:484
  1186.9 46.2 %copy-start.2 = (bf16[256,256]{1,0:T(8,128)(2,1)S(1)}, bf16[256,256]{1,0:T(8,128)(2,1)}, u32[]{:S(2)}) copy-start(bf16[256,256]{1,0:T(8,128)(2,1)} %param.21) | copy-start | bytes 393220
  1186.9 46.2 %copy-start.5 = (bf16[256,73]{0,1:T(8,128)(2,1)S(1)}, bf16[256,73]{0,1:T(8,128)(2,1)}, u32[]{:S(2)}) copy-start(bf16[256,73]{0,1:T(8,128)(2,1)} %param.19) | copy-start | bytes 112132
  1186.9 46.3 %copy-start.6 = (f32[256]{0:T(256)S(1)}, f32[256]{0:T(256)}, u32[]{:S(2)}) copy-start(f32[256]{0:T(256)} %param.20) | copy-start | bytes 3076
  1186.9 46.3 %copy-start.7 = (f32[256]{0:T(256)S(1)}, f32[256]{0:T(256)}, u32[]{:S(2)}) copy-start(f32[256]{0:T(256)} %param.22) | copy-start | bytes 3076
Sparse Core Ops, SparseCore 0:
  70.7 125.8 all-gather.4

commit v2 on v1

--- a/solution.py
+++ b/solution.py
@@ -3,6 +3,7 @@
 
 import jax
 import jax.numpy as jnp
+import numpy as np
 from jax import lax
 from jax.experimental import pallas as pl
 from jax.experimental.pallas import tpu as pltpu
@@ -13,10 +14,17 @@
 LANES = 128
 TILE = 16
 WINDOW = 48
+LATS = 8
+CHUNK_RUNS = 2
+ORDER_GROUP = 8
 VMEM_BYTES = 60 * 1024 * 1024
 
 F32 = jnp.float32
 BF16 = jnp.bfloat16
+
+
+def work(flops, bytes_moved):
+    return pl.CostEstimate(flops=flops, bytes_accessed=bytes_moved, transcendentals=0)
 
 
 def build_basis(order_list, points_total):
@@ -74,7 +82,7 @@
 
 def regrid_kernel(src_ref, cols_ref, row_ref, out_ref, contrib, *, channels, shards, slots, src_rows):
     step = pl.program_id(0)
-    rows = out_ref.shape[0]
+    height, rows = out_ref.shape
 
     @pl.when(step == 0)
     def _():
@@ -108,7 +116,7 @@
     lane = lax.broadcasted_iota(jnp.int32, (rows, LANES), 1)
     for place in range(4):
         merged = jnp.where(lane == channels + place, cols_ref[here, 3 + place : 4 + place], merged)
-    out_ref[...] = merged.astype(BF16)
+    out_ref[...] = merged.T[:height].astype(BF16)
 
 
 def regrid_listed(source_all, recv_src, recv_cell, recv_weight, lat_dev, lon_dev, slot_count):
@@ -116,11 +124,9 @@
     total = recv_src.shape[0]
     ordered = jnp.sort(recv_cell)
     lead = jnp.concatenate([jnp.ones((1,), jnp.bool_), ordered[1:] != ordered[:-1]])
-    bounds = jnp.arange(total, dtype=jnp.int32) * lon_dev
     limits = jnp.arange(lat_dev + 1, dtype=jnp.int32) * lon_dev
     starts = jnp.sum((recv_cell[None, :] < limits[:, None]).astype(jnp.int32), axis=1)
     starts = jnp.zeros((total,), jnp.int32).at[: lat_dev + 1].set(starts)
-    del bounds
     cols = jnp.stack(
         [
             recv_src.astype(F32),
@@ -135,20 +141,22 @@
         axis=1,
     )
     rows = min(512, total)
+    height = -(-(channels + 4) // TILE) * TILE
     return pl.pallas_call(
         functools.partial(
             regrid_kernel, channels=channels, shards=shards, slots=slot_count, src_rows=src_rows
         ),
         grid=(total // rows,),
-        out_shape=jax.ShapeDtypeStruct((total, LANES), BF16),
+        out_shape=jax.ShapeDtypeStruct((height, total), BF16),
         in_specs=[
             pl.BlockSpec((shards, channels, src_rows), lambda i: (0, 0, 0)),
             pl.BlockSpec((total, 8), lambda i: (0, 0)),
             pl.BlockSpec((1, total), lambda i: (0, 0)),
         ],
-        out_specs=pl.BlockSpec((rows, LANES), lambda i: (i, 0)),
+        out_specs=pl.BlockSpec((height, rows), lambda i: (0, i)),
         scratch_shapes=[pltpu.VMEM((total, 2 * LANES), BF16)],
         compiler_params=pltpu.CompilerParams(vmem_limit_bytes=VMEM_BYTES),
+        cost_estimate=work(4 * total * total * LANES, 2 * total * LANES),
     )(source_all, cols, recv_cell.astype(F32)[None, :])
 
 
@@ -161,19 +169,16 @@
     b2_ref,
     basis_ref,
     sums_ref,
-    out_ref,
-    delta,
-    hots,
-    base,
-    *,
+    *rest,
     channels,
     blocks,
     block_rows,
 ):
+    *out_refs, delta, hots, base = rest
     step = pl.program_id(0)
     total = blocks * block_rows
-    groups, lats, height, width = out_ref.shape
-    columns = groups * height
+    groups, lats, height, width = out_refs[0].shape
+    columns = groups * height * len(out_refs)
     chunk = min(512, block_rows)
 
     def encode(values):
@@ -184,7 +189,7 @@
 
     @pl.when(step == 0)
     def _():
-        empty = encode(jnp.zeros((16, LANES), BF16))[0:1]
+        empty = encode(jnp.zeros((TILE, rows_ref.shape[1]), BF16))[0:1]
         base[...] = sums_ref[...] * empty
         delta[pl.ds(total, WINDOW), :] = jnp.zeros((WINDOW, width), BF16)
         hots[pl.ds(total, WINDOW), :] = jnp.zeros((WINDOW, columns), BF16)
@@ -193,13 +198,15 @@
 
         def one(j, carry):
             at = pl.ds(pl.multiple_of(j * chunk, chunk), chunk)
-            values = rows_ref[at, :]
-            delta[at, :] = (encode(values) - empty).astype(BF16)
-            point = values[:, channels : channels + 1].astype(F32)
-            lead = values[:, channels + 1 : channels + 2].astype(F32)
+            per_block = block_rows // chunk
+            part = pl.ds(pl.multiple_of((j % per_block) * chunk, chunk), chunk)
+            values = rows_ref[j // per_block, :, part].astype(F32).T
+            delta[at, :] = (encode(values.astype(BF16)) - empty).astype(BF16)
+            point = values[:, channels : channels + 1]
+            lead = values[:, channels + 1 : channels + 2]
             point = jnp.where(lead > 0.5, point, -1.0)
             hot = (point == lane).astype(BF16)
-            block = basis_ref[j // (block_rows // chunk)]
+            block = basis_ref[j // per_block]
             hots[at, :] = jnp.dot(hot, block, preferred_element_type=F32).astype(BF16)
             return carry
 
@@ -239,19 +246,21 @@
         result = window(0, base[...])
         result = lax.fori_loop(1, most, window, result).astype(BF16)
         for g in range(groups):
-            out_ref[g, tt] = result[g * height : (g + 1) * height, :]
+            for h, out_ref in enumerate(out_refs):
+                low = (g * len(out_refs) + h) * height
+                out_ref[g, tt] = result[low : low + height, :]
         return carry
 
     lax.fori_loop(0, lats, latitude, 0)
 
 
 def zonal_transform(
-    rows, starts, w1, b1, w2, b2, basis, sums, lat_dev, groups, channels, lats=15
+    rows, starts, w1, b1, w2, b2, basis, sums, lat_dev, groups, sets, channels, lats=15
 ):
-    blocks, block_rows, _ = rows.shape
+    blocks, depth, block_rows = rows.shape
     width = w2.shape[1]
     columns = basis.shape[2]
-    height = columns // groups
+    height = columns // (groups * sets)
     total = blocks * block_rows
     whole = lambda shape: pl.BlockSpec(
         shape, lambda i, s: (0,) * len(shape), pipeline_mode=pl.Buffered(1)
@@ -264,7 +273,7 @@
             num_scalar_prefetch=1,
             grid=(lat_dev // lats,),
             in_specs=[
-                whole((total, LANES)),
+                whole(rows.shape),
                 whole(w1.shape),
                 whole(b1.shape),
                 whole(w2.shape),
@@ -272,20 +281,22 @@
                 whole(basis.shape),
                 whole(sums.shape),
             ],
-            out_specs=pl.BlockSpec((groups, lats, height, width), lambda i, s: (0, i, 0, 0)),
+            out_specs=[pl.BlockSpec((groups, lats, height, width), lambda i, s: (0, i, 0, 0))]
+            * sets,
             scratch_shapes=[
                 pltpu.VMEM((total + WINDOW, width), BF16),
                 pltpu.VMEM((total + WINDOW, columns), BF16),
                 pltpu.VMEM((columns, width), F32),
             ],
         ),
-        out_shape=jax.ShapeDtypeStruct((groups, lat_dev, height, width), BF16),
+        out_shape=[jax.ShapeDtypeStruct((groups, lat_dev, height, width), BF16)] * sets,
         compiler_params=pltpu.CompilerParams(vmem_limit_bytes=VMEM_BYTES),
-    )(starts, rows.reshape(total, LANES), w1, b1, w2, b2, basis, sums)
-
-
-def orders_kernel(spec_ref, fwd_ref, inv_ref, mix_ref, swap_ref, out_ref, taken, made, *, group):
-    order = lax.rem(pl.program_id(0), group)
+        cost_estimate=work(50 * total * width * 2 * columns, 2 * total * width),
+    )(starts, rows, w1, b1, w2, b2, basis, sums)
+
+
+def orders_kernel(place, spec_ref, fwd_ref, inv_ref, mix_ref, swap_ref, out_ref, taken, made, *, group):
+    order = pl.program_id(0)
     lat_total, _, width = spec_ref.shape
     parts, halves, part_lats, _, lanes = out_ref.shape
     side = 2 * group
@@ -322,9 +333,9 @@
             block = jnp.concatenate(columns, axis=1)
             turned = jnp.dot(swap_ref[...], block, preferred_element_type=F32).astype(BF16)
             for i in range(side):
-                lat = first + i
+                spot = place[first + i]
                 for h in range(halves):
-                    out_ref[lat // part_lats, h, lat % part_lats] = turned[
+                    out_ref[spot // 64, h, spot % 64] = turned[
                         i * side : (i + 1) * side, h * lanes : (h + 1) * lanes
                     ]
             return carry
@@ -332,46 +343,54 @@
         lax.fori_loop(0, lat_total // side, one, 0)
 
 
-def order_steps(spectra, fwd_table, inv_table, mix_t, parts, halves):
-    lat_total, height, width = spectra.shape
-    ord_dev, degrees, _ = fwd_table.shape
-    group = 8
-    side = 2 * group
+def order_steps(place, spectra, fwd_table, inv_table, mix_t, first, parts, halves):
+    lat_total, side, width = spectra.shape
+    degrees = fwd_table.shape[1]
+    group = side // 2
     index = jnp.arange(side * side, dtype=jnp.int32)
     swapped = (index % side) * side + index // side
     swap = (swapped[:, None] == index[None, :]).astype(BF16)
     both = 2 * width
     part_lats = lat_total // parts
+    out_shape = (parts, halves, part_lats, side, width // halves)
     return pl.pallas_call(
         functools.partial(orders_kernel, group=group),
-        grid=(ord_dev,),
-        in_specs=[
-            pl.BlockSpec((lat_total, side, width), lambda r: (0, r // group, 0)),
-            pl.BlockSpec((1, degrees, lat_total), lambda r: (r, 0, 0)),
-            pl.BlockSpec((1, lat_total, degrees), lambda r: (r, 0, 0)),
-            pl.BlockSpec((both, both), lambda r: (0, 0)),
-            pl.BlockSpec((side * side, side * side), lambda r: (0, 0)),
-        ],
-        out_specs=pl.BlockSpec(
-            (parts, halves, part_lats, side, width // halves),
-            lambda r: (0, 0, 0, r // group, 0),
+        grid_spec=pltpu.PrefetchScalarGridSpec(
+            num_scalar_prefetch=1,
+            grid=(group,),
+            in_specs=[
+                pl.BlockSpec((lat_total, side, width), lambda r, s: (0, 0, 0)),
+                pl.BlockSpec((1, degrees, lat_total), lambda r, s: (first + r, 0, 0)),
+                pl.BlockSpec((1, lat_total, degrees), lambda r, s: (first + r, 0, 0)),
+                pl.BlockSpec((both, both), lambda r, s: (0, 0)),
+                pl.BlockSpec((side * side, side * side), lambda r, s: (0, 0)),
+            ],
+            out_specs=pl.BlockSpec(out_shape, lambda r, s: (0, 0, 0, 0, 0)),
+            scratch_shapes=[
+                pltpu.VMEM((side, lat_total, width), BF16),
+                pltpu.VMEM((group, lat_total, both), BF16),
+            ],
         ),
-        out_shape=jax.ShapeDtypeStruct(
-            (parts, halves, part_lats, height, width // halves), BF16
+        out_shape=jax.ShapeDtypeStruct(out_shape, BF16),
+        compiler_params=pltpu.CompilerParams(vmem_limit_bytes=VMEM_BYTES),
+        cost_estimate=work(
+            group * 2 * both * degrees * (2 * lat_total + both), 8 * group * degrees * lat_total
         ),
-        scratch_shapes=[
-            pltpu.VMEM((side, lat_total, width), BF16),
-            pltpu.VMEM((group, lat_total, both), BF16),
-        ],
-        compiler_params=pltpu.CompilerParams(vmem_limit_bytes=VMEM_BYTES),
-    )(spectra, fwd_table, inv_table, mix_t, swap)
-
-
-def synthesis_kernel(modes_ref, basis_ref, out_ref):
-    sources, lats, height, lanes = modes_ref.shape
+    )(place, spectra, fwd_table, inv_table, mix_t, swap)
+
+
+def synthesis_kernel(*refs):
+    *mode_refs, basis_ref, out_ref = refs
+    sources, lats, height, lanes = mode_refs[0].shape
     blocks, _, points, _ = out_ref.shape
     right = jnp.concatenate(
-        [modes_ref[:, t].reshape(sources * height, lanes) for t in range(lats)], axis=1
+        [
+            jnp.concatenate(
+                [ref[:, t].reshape(sources * height, lanes) for ref in mode_refs], axis=0
+            )
+            for t in range(lats)
+        ],
+        axis=1,
     )
 
     def one(k, carry):
@@ -383,20 +402,70 @@
     lax.fori_loop(0, blocks, one, 0)
 
 
-def synthesis_steps(modes, basis, points, lats):
-    sources, lat_part, height, lanes = modes.shape
+def synthesis_steps(modes, basis, points, lats, first, count):
+    sources, _, height, lanes = modes[0].shape
     blocks = basis.shape[0]
+    offset = first // lats
     return pl.pallas_call(
         synthesis_kernel,
-        grid=(lat_part // lats,),
+        grid=(-(-count // lats),),
         in_specs=[
-            pl.BlockSpec((sources, lats, height, lanes), lambda i: (0, i, 0, 0)),
-            pl.BlockSpec(basis.shape, lambda i: (0, 0, 0)),
+            pl.BlockSpec((sources, lats, height, lanes), lambda i: (0, i + offset, 0, 0))
+            for _ in modes
+        ]
+        + [pl.BlockSpec(basis.shape, lambda i: (0, 0, 0))],
+        out_specs=pl.BlockSpec((blocks, lats, points, lanes), lambda i: (0, i, 0, 0)),
+        out_shape=jax.ShapeDtypeStruct((blocks, count, points, lanes), BF16),
+        compiler_params=pltpu.CompilerParams(vmem_limit_bytes=VMEM_BYTES),
+        cost_estimate=work(2 * count * lanes * basis.size, 4 * blocks * count * points * lanes),
+    )(*modes, basis)
+
+
+def finish_kernel(part_ref, enc_ref, out_ref, flat, *, first, whole_groups, rest):
+    quarters, _, lats, points, lanes = part_ref.shape
+    group = pl.program_id(1) + first
+
+    def fill(count):
+        for q in range(quarters):
+            for t in range(count):
+                row = (q * count + t) * points
+                flat[row : row + points, :] = part_ref[q, 0, t].astype(F32)
+
+    @pl.when(group < whole_groups)
+    def _():
+        fill(lats)
+
+    @pl.when(group >= whole_groups)
+    def _():
+        fill(rest)
+
+    def one(j, carry):
+        at = pl.ds(pl.multiple_of(j * lanes, lanes), lanes)
+        out_ref[:, at] = (enc_ref[:, at].astype(F32) + flat[at, :].T).astype(BF16)
+        return carry
+
+    lax.fori_loop(0, out_ref.shape[1] // lanes, one, 0)
+
+
+def finish_steps(part, running, lats, first, whole_groups, rest):
+    quarters, halves, count, points, lanes = part.shape
+    span = quarters * lats * points
+    return pl.pallas_call(
+        functools.partial(
+            finish_kernel, first=first, whole_groups=whole_groups, rest=rest
+        ),
+        grid=(halves, -(-count // lats)),
+        in_specs=[
+            pl.BlockSpec((quarters, 1, lats, points, lanes), lambda h, i: (0, h, i, 0, 0)),
+            pl.BlockSpec((lanes, span), lambda h, i: (h, i + first)),
         ],
-        out_specs=pl.BlockSpec((blocks, lats, points, lanes), lambda i: (0, i, 0, 0)),
-        out_shape=jax.ShapeDtypeStruct((blocks, lat_part, points, lanes), BF16),
+        out_specs=pl.BlockSpec((lanes, span), lambda h, i: (h, i + first)),
+        out_shape=jax.ShapeDtypeStruct(running.shape, BF16),
+        scratch_shapes=[pltpu.VMEM((span, lanes), F32)],
+        input_output_aliases={1: 0},
         compiler_params=pltpu.CompilerParams(vmem_limit_bytes=VMEM_BYTES),
-    )(modes, basis)
+        cost_estimate=work(part.size * 40, 6 * part.size),
+    )(part, running)
 
 
 def listed_plan(
@@ -431,8 +500,8 @@
         source_all, recv_src, recv_cell, recv_weight, lat_dev, lon_dev, slot_count
     )
     band = lax.all_gather(listed, "lon", axis=0, tiled=False)
-    coded = band[:, : lat_dev + 1, channels + 2 : channels + 4].astype(jnp.int32)
-    starts = coded[:, :, 0] * 128 + coded[:, :, 1]
+    coded = band[:, channels + 2 : channels + 4, : lat_dev + 1].astype(jnp.int32)
+    starts = coded[:, 0] * 128 + coded[:, 1]
 
     mine = lax.axis_index("lon")
     owned = (
@@ -446,7 +515,8 @@
     inside = (jnp.arange(point_rows) < lon_dev)[None, :, None]
     basis_in = jnp.where(inside, basis_by_point(owned, at), 0)
     sums = jnp.sum(basis_in.astype(F32), axis=(0, 1))[:, None]
-    w1 = jnp.zeros((LANES, width), BF16).at[:channels].set(enc_w1.T)
+    w1 = jnp.zeros((band.shape[1], width), BF16).at[:channels].set(enc_w1.T)
+    sets = ord_dev // ORDER_GROUP
     spectra = zonal_transform(
         band,
         starts,
@@ -458,35 +528,48 @@
         sums,
         lat_dev,
         lat_count,
+        sets,
         channels,
     )
-    spectra = lax.all_to_all(spectra, "lat", split_axis=0, concat_axis=0, tiled=True)
-    spectra = spectra.reshape(lat_total, 2 * ord_dev, width)
-    made = order_steps(
-        spectra,
-        fwd_table,
-        inv_table,
-        mixing_matrix(mix_weight).T,
-        lat_count * quarters,
-        halves,
-    )
-    made = made.reshape(lat_count * lon_count, part_lats, 2 * ord_dev, LANES)
-    modes = lax.all_to_all(made, ("lat", "lon"), split_axis=0, concat_axis=0, tiled=True)
+
+    run = quarters * LATS
+    whole_groups = lat_dev // run
+    rest = (lat_dev - whole_groups * run) // quarters
+    lat = np.arange(lat_dev)
+    tail = lat - whole_groups * run
+    to_part = np.where(tail < 0, lat % run // LATS, tail // max(rest, 1))
+    to_row = np.where(tail < 0, lat // run * LATS + lat % LATS, whole_groups * LATS + tail % max(rest, 1))
+    place = (np.arange(lat_count)[:, None] * quarters + to_part) * 64 + to_row
+    place = jnp.asarray(place.reshape(-1), jnp.int32)
+
+    mix_t = mixing_matrix(mix_weight).T
+    modes = []
+    for g in range(sets):
+        got = lax.all_to_all(spectra[g], "lat", split_axis=0, concat_axis=0, tiled=True)
+        made = order_steps(
+            place,
+            got.reshape(lat_total, 2 * ORDER_GROUP, width),
+            fwd_table,
+            inv_table,
+            mix_t,
+            g * ORDER_GROUP,
+            lat_count * quarters,
+            halves,
+        )
+        made = made.reshape(lat_count * lon_count, part_lats, 2 * ORDER_GROUP, LANES)
+        modes.append(
+            lax.all_to_all(made, ("lat", "lon"), split_axis=0, concat_axis=0, tiled=True)
+        )
 
     pad_points = -(-lon_dev // TILE) * TILE
     at = jnp.arange(lon_count, dtype=jnp.int32)[:, None] * lon_dev + jnp.arange(
         pad_points, dtype=jnp.int32
     )
     inside = (jnp.arange(pad_points) < lon_dev)[None, :, None]
-    basis_out = basis_by_point(jnp.arange(ORDERS, dtype=jnp.int32), at)
+    listing = jnp.arange(ORDERS, dtype=jnp.int32).reshape(-1, sets, ORDER_GROUP)
+    basis_out = basis_by_point(listing.transpose(1, 0, 2).reshape(-1), at)
     basis_out = jnp.where(inside, basis_out, 0)
-    grid_part = synthesis_steps(modes, basis_out, lon_dev, 9)
-    grid_part = lax.all_to_all(grid_part, "lon", split_axis=0, concat_axis=0, tiled=True)
-    spectral = (
-        grid_part.reshape(quarters, halves, part_lats, lon_dev, LANES)
-        .transpose(1, 4, 0, 2, 3)
-        .reshape(width, cells_dev)
-    )
+
     piece = source_all.transpose(1, 0, 2).reshape(channels, -1)
     encoded = dense_encoder(
         piece,
@@ -499,7 +582,15 @@
         enc_w2,
         enc_b2,
     )
-    return (encoded.astype(F32) + spectral.astype(F32)).astype(BF16)
+    running = encoded
+    step = CHUNK_RUNS * LATS
+    for first in range(0, part_lats, step):
+        count = min(step, part_lats - first)
+        part = synthesis_steps(modes, basis_out, lon_dev, LATS, first, count)
+        part = lax.all_to_all(part, "lon", split_axis=0, concat_axis=0, tiled=True)
+        part = part.reshape(quarters, halves, count, lon_dev, LANES)
+        running = finish_steps(part, running, LATS, first // LATS, whole_groups, rest)
+    return running
 
 
 def dense_plan(
@@ -609,8 +700,11 @@
             slots * 4 <= cells_dev
             and width % LANES == 0
             and lon_count % halves == 0
-            and lat_dev % (9 * lon_count // halves) == 0
-            and ord_dev % 8 == 0
+            and lat_dev % (lon_count // halves) == 0
+            and lat_dev % 15 == 0
+            and (lon_count // halves) * LATS * (NLON // lon_count) % LANES == 0
+            and lat_dev // (lon_count // halves) < 64
+            and ord_dev % ORDER_GROUP == 0
             and lat_total % TILE == 0
         )
         return listed_plan(*arrays) if fits else dense_plan(*arrays)

time: 1320 us -> 1180 us (0.89)
  waiting for transfers between devices: 784 us -> 472 us
  Pallas kernels: 209 us -> 299 us
  blocking collectives: 35.9 us -> 109 us
  other arithmetic: 101 us -> 84.8 us
  matrix products: 83 us -> 96.5 us
    all_to_all x2 -> x4, waiting for transfers between devices: 434 us -> 193 us  [the longest x3 179 us: listed_plan(): part = lax.all_to_all(part, 'lon', split_axis=0, concat_axis=0, tiled=True)]
    pallas_call x2 -> x8, Pallas kernels: 95.9 us -> 178 us  [the longest x2 69.9 us: order_steps(): pl.pallas_call(functools.partial(orders_kernel, group=group), grid_spec=p...]
    all_to_all x0 -> x1, blocking collectives: none -> 73.2 us  [listed_plan(): lax.all_to_all(spectra[g], 'lat', split_axis=0, concat_axis=0, tiled=True)]
    convert_element_type x1 -> x0, local copies, waits for them, and re-layouts: 46.2 us -> none  [listed_plan(): return (encoded.astype(F32) + spectral.astype(F32)).astype(BF16)]
    all_gather x1, waiting for transfers between devices: 118 us -> 80.7 us  [listed_plan(): band = lax.all_gather(listed, 'lon', axis=0, tiled=False)]
    pallas_call x0 -> x3, local copies, waits for them, and re-layouts: none -> 34.7 us  [the longest x1 22.3 us: finish_steps(): pl.pallas_call(functools.partial(finish_kernel, first=first, whole_groups...]
    all_to_all x1 -> x2, waiting for transfers between devices: 233 us -> 198 us  [listed_plan(): lax.all_to_all(made, ('lat', 'lon'), split_axis=0, concat_axis=0, tiled=T...]
    convert_element_type x2 -> x1, other arithmetic: 18.4 us -> 0.77 us  [listed_plan(): coded = band[:, channels + 2:channels + 4, :lat_dev + 1].astype(jnp.int32)]
  transfers between devices with their start and end apart: 4 -> 7, of which waited for: 4 -> 6; matrix products, arithmetic and copies ran while one was open for 8% -> 18% of each run, Pallas kernels for 0% -> 12%
where the time goes in v2:
time: 1180 us
  waiting for transfers between devices  472 us (40%)
  Pallas kernels  299 us (25%)
  blocking collectives  109 us (9%)
  matrix products  96.5 us (8%)
  other arithmetic  84.8 us (7%)
  local copies, waits for them, and re-layouts  77.4 us (7%)
  starting transfers between devices  26.8 us (2%)
  between operations  14 us (1%)
    all_to_all x2, waiting for transfers between devices, listed_plan(): lax.all_to_all(made, ('lat', 'lon'), split_axis=0, concat_axis=0, tiled=T...  198 us
    all_to_all x3, waiting for transfers between devices, listed_plan(): part = lax.all_to_all(part, 'lon', split_axis=0, concat_axis=0, tiled=True)  179 us
    pallas_call x1, Pallas kernels, zonal_transform(): pl.pallas_call(functools.partial(zonal_kernel, channels=channels, blocks=...  104 us
    dot_general x1, matrix products, dense_encoder(): jnp.dot(enc_w2, hidden, preferred_element_type=jnp.float32)  96.5 us
    all_gather x1, waiting for transfers between devices, listed_plan(): band = lax.all_gather(listed, 'lon', axis=0, tiled=False)  80.7 us
    all_to_all x1, blocking collectives, listed_plan(): lax.all_to_all(spectra[g], 'lat', split_axis=0, concat_axis=0, tiled=True)  73.2 us
    pallas_call x2, Pallas kernels, order_steps(): pl.pallas_call(functools.partial(orders_kernel, group=group), grid_spec=p...  69.9 us
    pallas_call x3, Pallas kernels, finish_steps(): pl.pallas_call(functools.partial(finish_kernel, first=first, whole_groups...  66.8 us
  transfers between devices with their start and end apart: 7, of which 6 were waited for; matrix products, arithmetic and copies ran while one was open for 18% of the time, Pallas kernels for 12%

profile of v2, /device:TPU:0, one launch (start us, length us, event | category | flops | bytes accessed | tf_op | source)
XLA Modules:
  0.0 1178.9 jit_solution(14030946496571540659)
XLA Ops:
  6.5 6.5 sort.15
  13.1 1.2 convert_reduce_fusion
  14.4 35.9 %all-gather.2.src_ref = bf16[8,73,512]{2,1,0:T(8,128)(2,1)} all-gather(bf16[1,73,512]{2,1,0:T(8,128)(2,1)} %bitcast.128), channel_id=2, replica_groups=mesh['lat'=4,'lon'=8] {'lon'}, dimensions={0}, use_global_device_ids=true | all-gather | bytes 672768 | tf_op jit(solution)/shard_map/all_gather | solution.py:498
  50.5 1.4 compare_select_fusion.1
  51.9 0.9 stack.39
  52.8 1.9 copy.112.cols_ref
  54.8 16.3 %shard_map.118 = bf16[80,4096]{1,0:T(8,128)(2,1)} custom-call(bf16[8,73,512]{2,1,0:T(8,128)(2,1)} %all-gather.2.src_ref, f32[4096,8]{1,0:T(8,128)} %copy.112.cols_ref, f32[1,4096]{1,0:T(1,128)} %bitcast.136), custom_call_target="tpu_custom_call" | custom-call | flops 8589934592 | bytes 1048576 | tf_op jit(solution)/shard_map/pallas_call | solution.py:145
  71.3 0.8 copy.113
  72.1 2.6 cosine_multiply_fusion
  75.5 0.7 broadcast_in_dim.93.sums_ref
  76.8 0.9 broadcast_select_fusion.1.basis_ref
  77.7 80.7 %all-gather.5.cloned.1.call-done = bf16[640,4096]{1,0:T(8,128)(2,1)} async-done(((bf16[80,4096]{1,0:T(8,128)(2,1)}), bf16[640,4096]{1,0:T(8,128)(2,1)}) %all-gather.5.cloned.1.call-update) | async-done | bytes 5242896 | tf_op jit(solution)/shard_map/all_gather | solution.py:502
  158.5 0.8 slice_convert_fusion
  159.9 104.1 %shard_map.119 = (bf16[4,180,16,256]{3,2,1,0:T(8,128)(2,1)}, bf16[4,180,16,256]{3,2,1,0:T(8,128)(2,1)}) custom-call(s32[8,181]{1,0:T(8,128)} %bitcast.137, bf16[8,80,4096]{2,1,0:T(8,128)(2,1)} %bitcast.139, bf16[80,256]{1,0:T(8,128)(2,1)} %scatter.9.w1_ref, f32[1,256]{1,0:T(1,128)} %bitcast.140, bf16[256,256]{1,0:T(8,128)(2,1)} %bitcast.127, ...), custom_call_target="tpu_custom_call" | custom-call | flops 107374182400 | bytes 16777216 | tf_op jit(solution)/shard_map/pallas_call | solution.py:268
  264.0 73.2 %all_to_all.35 = bf16[4,180,16,256]{3,2,1,0:T(8,128)(2,1)} all-to-all(bf16[4,180,16,256]{3,2,1,0:T(8,128)(2,1)} %get-tuple-element.35), channel_id=1, replica_groups=mesh['lat'=4,'lon'=8] {'lat'}, dimensions={0} | all-to-all | bytes 11796480 | tf_op jit(solution)/shard_map/all_to_all | solution.py:548
  337.1 5.2 all-to-all-start
  342.5 16.2 %copy.118.fwd_ref = bf16[16,512,720]{2,1,0:T(8,128)(2,1)} copy(bf16[16,512,720]{1,2,0:T(8,128)(2,1)} %param.25) | data formatting | bytes 23592960 | tf_op args[9]
  358.8 0.8 maximum_bitcast_fusion.mix_ref
  359.6 0.7 fusion.44.swap_ref
  360.4 35.0 %shard_map.121 = bf16[16,2,45,16,128]{4,3,2,1,0:T(8,128)(2,1)} custom-call(s32[720]{0:T(1024)} %constant.250.clone.place, bf16[720,16,256]{2,1,0:T(8,128)(2,1)} %bitcast.117, bf16[16,512,720]{2,1,0:T(8,128)(2,1)} %copy.118.fwd_ref, bf16[16,720,512]{2,1,0:T(8,128)(2,1)} %inv_ref.3, bf16[512,512]{1,0:T(8,128)(2,1)} %maximum_bitcast_fusion.mix_ref, ...), custom_call_target="tpu_custom_call" | custom-call | flops 8187281408 | bytes 23592960 | tf_op jit(solution)/shard_map/pallas_call | solution.py:356
  395.3 13.4 %all-to-all-done = bf16[4,180,16,256]{3,2,1,0:T(8,128)(2,1)} async-done(((bf16[4,180,16,256]{3,2,1,0:T(8,128)(2,1)}), bf16[4,180,16,256]{3,2,1,0:T(8,128)(2,1)}, u32[]{:S(2)}, u32[]{:S(2)}) %all-to-all-start) | async-done | bytes 5898272 | tf_op jit(solution)/shard_map/all_to_all | solution.py:548
  408.8 3.6 all-to-all-start.3
  412.4 34.9 %shard_map.120 = bf16[16,2,45,16,128]{4,3,2,1,0:T(8,128)(2,1)} custom-call(s32[720]{0:T(1024)} %constant.250.clone.place, bf16[720,16,256]{2,1,0:T(8,128)(2,1)} %bitcast.14.spec_ref, bf16[16,512,720]{2,1,0:T(8,128)(2,1)} %copy.118.fwd_ref, bf16[16,720,512]{2,1,0:T(8,128)(2,1)} %inv_ref.3, bf16[512,512]{1,0:T(8,128)(2,1)} %maximum_bitcast_fusion.mix_ref, ...), custom_call_target="tpu_custom_call" | custom-call | flops 8187281408 | bytes 23592960 | tf_op jit(solution)/shard_map/pallas_call | solution.py:356
  447.3 96.8 %all-to-all-done.3.refs_1_ = bf16[32,45,16,128]{3,2,1,0:T(8,128)(2,1)} async-done(((bf16[32,45,16,128]{3,2,1,0:T(8,128)(2,1)}), bf16[32,45,16,128]{3,2,1,0:T(8,128)(2,1)}, u32[]{:S(2)}, u32[]{:S(2)}) %all-to-all-start.3) | async-done | bytes 5898272 | tf_op jit(solution)/shard_map/all_to_all | solution.py:561
  544.1 4.0 all-to-all-start.1
  548.2 19.5 %multiply_convert_fusion.1 = (bf16[8,192,512,1]{1,0,3,2:T(8,128)(2,1)S(1)}, bf16[8,192,512,1]{1,0,3,2:T(8,128)(2,1)S(1)}) fusion(s32[512]{0:T(512)S(1)} %reshape.378, s32[8,192]{1,0:T(8,128)S(1)} %iota_add_fusion), kind=kLoop, calls=%fused_computation.38 | loop fusion | flops 10223616 | bytes 3153920 | tf_op jit(solution)/shard_map/convert
  567.7 2.7 pad_maximum_fusion
  570.4 5.7 copy.120
  576.1 2.0 broadcast_select_fusion.refs_2_
  578.1 101.6 %all-to-all-done.1.refs_0_ = bf16[32,45,16,128]{3,2,1,0:T(8,128)(2,1)} async-done(((bf16[32,45,16,128]{3,2,1,0:T(8,128)(2,1)}), bf16[32,45,16,128]{3,2,1,0:T(8,128)(2,1)}, u32[]{:S(2)}, u32[]{:S(2)}) %all-to-all-start.1) | async-done | bytes 5898272 | tf_op jit(solution)/shard_map/all_to_all | solution.py:561
  679.7 13.9 %shard_map.124 = bf16[8,16,180,128]{3,2,1,0:T(8,128)(2,1)} custom-call(bf16[32,45,16,128]{3,2,1,0:T(8,128)(2,1)} %all-to-all-done.1.refs_0_, bf16[32,45,16,128]{3,2,1,0:T(8,128)(2,1)} %all-to-all-done.3.refs_1_, bf16[8,192,1024]{2,1,0:T(8,128)(2,1)} %broadcast_select_fusion.refs_2_), custom_call_target="tpu_custom_call" | custom-call | flops 6442450944 | bytes 11796480 | tf_op jit(solution)/shard_map/pallas_call | solution.py:409
  693.7 6.1 copy.123
  699.8 4.7 all-to-all-start.6
  704.5 14.0 %shard_map.123 = bf16[8,16,180,128]{3,2,1,0:T(8,128)(2,1)} custom-call(bf16[32,45,16,128]{3,2,1,0:T(8,128)(2,1)} %all-to-all-done.1.refs_0_, bf16[32,45,16,128]{3,2,1,0:T(8,128)(2,1)} %all-to-all-done.3.refs_1_, bf16[8,192,1024]{2,1,0:T(8,128)(2,1)} %broadcast_select_fusion.refs_2_), custom_call_target="tpu_custom_call" | custom-call | flops 6442450944 | bytes 11796480 | tf_op jit(solution)/shard_map/pallas_call | solution.py:409
  718.6 6.2 copy.121
  724.8 109.6 %all-to-all-done.6 = bf16[8,16,180,128]{3,1,2,0:T(8,128)(2,1)} async-done(((bf16[8,16,180,128]{3,1,2,0:T(8,128)(2,1)}), bf16[8,16,180,128]{3,1,2,0:T(8,128)(2,1)}, u32[]{:S(2)}, u32[]{:S(2)}) %all-to-all-start.6) | async-done | bytes 5898272 | tf_op jit(solution)/shard_map/all_to_all | solution.py:590
  834.3 4.7 all-to-all-start.5
  839.8 44.9 %scatter_custom_fusion = f32[32400,73]{1,0:T(8,128)} fusion(s32[4096]{0:T(1024)} %get-tuple-element.42, f32[]{:T(128)} %constant.205.clone.1, f32[4096]{0:T(1024)S(1)} %copy-done.6, pred[4096]{0:T(1024)(128)(4,1)S(1)} %compare_and_fusion, bf16[]{:T(256)} %constant.220.clone.1, bf16[4096,73]{1,0:T(8,128)(2,1)S(1)} %bitcast.120, s32[4096]{0:T(1024)S(1)} %copy-done.7), kind=kCustom, calls=%fused_computation.31 | custom fusion | flops 1196032 | bytes 10096704 | tf_op jit(solution)/shard_map/scatter-add | solution.py:51
  884.7 13.7 %shard_map.122 = bf16[8,13,180,128]{3,2,1,0:T(8,128)(2,1)} custom-call(bf16[32,45,16,128]{3,2,1,0:T(8,128)(2,1)} %all-to-all-done.1.refs_0_, bf16[32,45,16,128]{3,2,1,0:T(8,128)(2,1)} %all-to-all-done.3.refs_1_, bf16[8,192,1024]{2,1,0:T(8,128)(2,1)} %broadcast_select_fusion.refs_2_), custom_call_target="tpu_custom_call" | custom-call | flops 5234491392 | bytes 9584640 | tf_op jit(solution)/shard_map/pallas_call | solution.py:409
  898.4 69.6 %all-to-all-done.5 = bf16[8,16,180,128]{3,1,2,0:T(8,128)(2,1)} async-done(((bf16[8,16,180,128]{3,1,2,0:T(8,128)(2,1)}), bf16[8,16,180,128]{3,1,2,0:T(8,128)(2,1)}, u32[]{:S(2)}, u32[]{:S(2)}) %all-to-all-start.5) | async-done | bytes 5898272 | tf_op jit(solution)/shard_map/all_to_all | solution.py:590
  968.0 4.6 all-to-all-start.4
  972.7 96.5 %fusion.1.enc_ref = bf16[256,32400]{1,0:T(8,128)(2,1)} fusion(bf16[256,256]{1,0:T(8,128)(2,1)S(1)} %copy-done.5, f32[256]{0:T(256)S(1)} %copy-done.14, bf16[256,73]{0,1:T(8,128)(2,1)S(1)} %copy-done.10, f32[256]{0:T(256)S(1)} %copy-done.13, f32[32400,73]{1,0:T(8,128)} %scatter_custom_fusion), kind=kOutput, calls=%fused_computation.6 | convolution fusion | flops 6024099840 | bytes 26220096 | tf_op jit(solution)/shard_map/dot_general | solution.py:79
  1069.1 6.8 copy.122
  1075.9 6.8 copy.124
  1082.7 22.3 %shard_map.125.enc_ref = bf16[256,32400]{1,0:T(8,128)(2,1)} custom-call(bf16[4,2,16,180,128]{4,3,2,1,0:T(8,128)(2,1)} %bitcast.115, bf16[256,32400]{1,0:T(8,128)(2,1)} %fusion.1.enc_ref), custom_call_target="tpu_custom_call", output_to_operand_aliasing={{}: (1, {})} | custom-call | flops 117964800 | bytes 17694720 | tf_op jit(solution)/shard_map/pallas_call | solution.py:453
  1105.0 22.4 %shard_map.126.enc_ref = bf16[256,32400]{1,0:T(8,128)(2,1)} custom-call(bf16[4,2,16,180,128]{4,3,2,1,0:T(8,128)(2,1)} %bitcast.114, bf16[256,32400]{1,0:T(8,128)(2,1)} %shard_map.125.enc_ref), custom_call_target="tpu_custom_call", output_to_operand_aliasing={{}: (1, {})} | custom-call | flops 117964800 | bytes 17694720 | tf_op jit(solution)/shard_map/pallas_call | solution.py:453
  1127.4 22.1 %shard_map.127 = bf16[256,32400]{1,0:T(8,128)(2,1)} custom-call(bf16[4,2,13,180,128]{4,3,2,1,0:T(8,128)(2,1)} %bitcast.22.part_ref, bf16[256,32400]{1,0:T(8,128)(2,1)} %shard_map.126.enc_ref), custom_call_target="tpu_custom_call", output_to_operand_aliasing={{}: (1, {})} | custom-call | flops 95846400 | bytes 14376960 | tf_op jit(solution)/shard_map/pallas_call | solution.py:453
  1149.5 22.3 %copy.129 = bf16[256,32400]{0,1:T(8,128)(2,1)} copy(bf16[256,32400]{1,0:T(8,128)(2,1)} %shard_map.127) | data formatting | bytes 33177600 | tf_op jit(solution)/shard_map/pallas_call | solution.py:453
  (66 shorter events, 3.7 us)
Async XLA Ops:
  6.5 151.9 %all-gather.5.cloned.1.call-start = ((), (), s32[]{:S(2)}) async-start(), calls=%async_computation.7 | async-start | bytes 5898240 | tf_op jit(solution)/shard_map/all_gather | solution.py:502
  14.4 37.5 %copy-start.2 = (s32[1,4,8,128]{3,1,2,0:T(4,128)}, s32[1,4,8,128]{3,1,2,0:T(4,128)S(1)}, u32[]{:S(2)}) copy-start(s32[1,4,8,128]{3,1,2,0:T(4,128)S(1)} %copy.137) | copy-start | bytes 49156
  54.7 16.5 %copy-start.4 = (bf16[256,256]{1,0:T(8,128)(2,1)S(1)}, bf16[256,256]{1,0:T(8,128)(2,1)}, u32[]{:S(2)}) copy-start(bf16[256,256]{1,0:T(8,128)(2,1)} %param.22) | copy-start | bytes 393220
  54.8 21.5 %copy-start.9 = (bf16[256,73]{0,1:T(8,128)(2,1)S(1)}, bf16[256,73]{0,1:T(8,128)(2,1)}, u32[]{:S(2)}) copy-start(bf16[256,73]{0,1:T(8,128)(2,1)} %param.20) | copy-start | bytes 112132
  72.0 3.0 copy-start.11
  264.0 78.3 %copy-start.1 = (bf16[2,256,256]{2,1,0:T(8,128)(2,1)S(1)}, bf16[2,256,256]{2,1,0:T(8,128)(2,1)}, u32[]{:S(2)}) copy-start(bf16[2,256,256]{2,1,0:T(8,128)(2,1)} %param.24) | copy-start | bytes 786436
  337.1 71.7 %all-to-all-start = ((bf16[4,180,16,256]{3,2,1,0:T(8,128)(2,1)}), bf16[4,180,16,256]{3,2,1,0:T(8,128)(2,1)}, u32[]{:S(2)}, u32[]{:S(2)}) async-start(bf16[4,180,16,256]{3,2,1,0:T(8,128)(2,1)} %get-tuple-element.34), calls=%async_computation | async-start | bytes 11796480 | tf_op jit(solution)/shard_map/all_to_all | solution.py:548
  408.8 135.3 %all-to-all-start.3 = ((bf16[32,45,16,128]{3,2,1,0:T(8,128)(2,1)}), bf16[32,45,16,128]{3,2,1,0:T(8,128)(2,1)}, u32[]{:S(2)}, u32[]{:S(2)}) async-start(bf16[32,45,16,128]{3,2,1,0:T(8,128)(2,1)} %bitcast.118), calls=%async_computation.3 | async-start | bytes 11796480 | tf_op jit(solution)/shard_map/all_to_all | solution.py:561
  412.4 135.8 %copy-start.12 = (s32[8]{0:T(128)S(1)}, s32[8]{0:T(128)}, u32[]{:S(2)}) copy-start(s32[8]{0:T(128)} %copy-done.11) | copy-start | bytes 100
  544.1 135.7 %all-to-all-start.1 = ((bf16[32,45,16,128]{3,2,1,0:T(8,128)(2,1)}), bf16[32,45,16,128]{3,2,1,0:T(8,128)(2,1)}, u32[]{:S(2)}, u32[]{:S(2)}) async-start(bf16[32,45,16,128]{3,2,1,0:T(8,128)(2,1)} %bitcast.116), calls=%async_computation.1 | async-start | bytes 11796480 | tf_op jit(solution)/shard_map/all_to_all | solution.py:561
  699.8 134.5 %all-to-all-start.6 = ((bf16[8,16,180,128]{3,1,2,0:T(8,128)(2,1)}), bf16[8,16,180,128]{3,1,2,0:T(8,128)(2,1)}, u32[]{:S(2)}, u32[]{:S(2)}) async-start(bf16[8,16,180,128]{3,1,2,0:T(8,128)(2,1)} %copy.123), calls=%async_computation.6 | async-start | bytes 11796480 | tf_op jit(solution)/shard_map/all_to_all | solution.py:590
  718.5 120.5 %copy-start = (bf16[8,73,512]{2,1,0:T(8,128)(2,1)S(1)}, bf16[8,73,512]{2,1,0:T(8,128)(2,1)}, u32[]{:S(2)}) copy-start(bf16[8,73,512]{2,1,0:T(8,128)(2,1)} %all-gather.2.src_ref) | copy-start | bytes 1794052
  718.5 121.2 %copy-start.3 = (s32[1,4,8,128]{3,1,2,0:T(4,128)S(1)}, s32[1,4,8,128]{3,1,2,0:T(4,128)}, u32[]{:S(2)}) copy-start(s32[1,4,8,128]{3,1,2,0:T(4,128)} %copy-done.2) | copy-start | bytes 49156
  718.5 121.2 %copy-start.8 = (s32[4096]{0:T(1024)S(1)}, s32[4096]{0:T(1024)}, u32[]{:S(2)}) copy-start(s32[4096]{0:T(1024)} %param.17) | copy-start | bytes 49156
  718.5 121.3 %copy-start.6 = (f32[4096]{0:T(1024)S(1)}, f32[4096]{0:T(1024)}, u32[]{:S(2)}) copy-start(f32[4096]{0:T(1024)} %param.19) | copy-start | bytes 49156
  718.5 121.3 %copy-start.7 = (s32[4096]{0:T(1024)S(1)}, s32[4096]{0:T(1024)}, u32[]{:S(2)}) copy-start(s32[4096]{0:T(1024)} %get-tuple-element.53) | copy-start | bytes 49156
  834.3 133.6 %all-to-all-start.5 = ((bf16[8,16,180,128]{3,1,2,0:T(8,128)(2,1)}), bf16[8,16,180,128]{3,1,2,0:T(8,128)(2,1)}, u32[]{:S(2)}, u32[]{:S(2)}) async-start(bf16[8,16,180,128]{3,1,2,0:T(8,128)(2,1)} %copy.121), calls=%async_computation.5 | async-start | bytes 11796480 | tf_op jit(solution)/shard_map/all_to_all | solution.py:590
  884.7 87.9 %copy-start.5 = (bf16[256,256]{1,0:T(8,128)(2,1)S(1)}, bf16[256,256]{1,0:T(8,128)(2,1)}, u32[]{:S(2)}) copy-start(bf16[256,256]{1,0:T(8,128)(2,1)} %param.22) | copy-start | bytes 393220
  884.7 87.9 %copy-start.10 = (bf16[256,73]{0,1:T(8,128)(2,1)S(1)}, bf16[256,73]{0,1:T(8,128)(2,1)}, u32[]{:S(2)}) copy-start(bf16[256,73]{0,1:T(8,128)(2,1)} %param.20) | copy-start | bytes 112132
  884.7 88.0 %copy-start.13 = (f32[256]{0:T(256)S(1)}, f32[256]{0:T(256)}, u32[]{:S(2)}) copy-start(f32[256]{0:T(256)} %param.21) | copy-start | bytes 3076
  884.7 88.0 %copy-start.14 = (f32[256]{0:T(256)S(1)}, f32[256]{0:T(256)}, u32[]{:S(2)}) copy-start(f32[256]{0:T(256)} %param.23) | copy-start | bytes 3076
  968.0 159.4 %all-to-all-start.4 = ((bf16[8,13,180,128]{3,2,1,0:T(8,128)(2,1)}), bf16[8,13,180,128]{3,2,1,0:T(8,128)(2,1)}, u32[]{:S(2)}, u32[]{:S(2)}) async-start(bf16[8,13,180,128]{3,2,1,0:T(8,128)(2,1)} %shard_map.122), calls=%async_computation.4 | async-start | bytes 9797632 | tf_op jit(solution)/shard_map/all_to_all | solution.py:590
Sparse Core Ops, SparseCore 0:
  71.2 87.1 all-gather.4

commit v3 on v2

--- a/solution.py
+++ b/solution.py
@@ -13,7 +13,7 @@
 ORDERS = 512
 LANES = 128
 TILE = 16
-WINDOW = 48
+WINDOW = 32
 LATS = 8
 CHUNK_RUNS = 2
 ORDER_GROUP = 8
@@ -63,7 +63,7 @@
     )
 
 
-def dense_encoder(piece, sources, targets, weights, cells_dev, enc_w1, enc_b1, enc_w2, enc_b2):
+def regrid_all(piece, sources, targets, weights, cells_dev):
     shard_count, slot_count = sources.shape
     channels = piece.shape[0]
     src_rows = piece.shape[1] // shard_count
@@ -72,7 +72,10 @@
     picked = jnp.take(piece_rows, (offsets + sources).reshape(-1), axis=0)
     picked = picked.reshape(shard_count, slot_count, channels)
     empty = jnp.zeros((cells_dev, channels), jnp.float32)
-    regridded = spread(empty, picked, weights, targets).T.astype(jnp.bfloat16)
+    return spread(empty, picked, weights, targets).astype(jnp.bfloat16)
+
+
+def dense_encoder(regridded, enc_w1, enc_b1, enc_w2, enc_b2):
     hidden = jnp.dot(enc_w1, regridded, preferred_element_type=jnp.float32) + enc_b1[:, None]
     hidden = jax.nn.gelu(hidden, approximate=False).astype(jnp.bfloat16)
     return (
@@ -80,7 +83,13 @@
     ).astype(jnp.bfloat16)
 
 
-def regrid_kernel(src_ref, cols_ref, row_ref, out_ref, contrib, *, channels, shards, slots, src_rows):
+def encoder_by_cell(regridded, enc_w1, enc_b1, enc_w2, enc_b2):
+    hidden = jnp.dot(regridded, enc_w1.T, preferred_element_type=F32) + enc_b1
+    hidden = jax.nn.gelu(hidden, approximate=False).astype(BF16)
+    return (jnp.dot(hidden, enc_w2.T, preferred_element_type=F32) + enc_b2).astype(BF16)
+
+
+def regrid_kernel(live, src_ref, cols_ref, row_ref, out_ref, contrib, *, channels, shards, slots, src_rows):
     step = pl.program_id(0)
     height, rows = out_ref.shape
 
@@ -107,25 +116,39 @@
         lax.fori_loop(0, shards, one, 0)
 
     here = pl.ds(pl.multiple_of(step * rows, rows), rows)
-    cell = cols_ref[here, 2:3]
-    total = jnp.zeros((rows, 2 * LANES), F32)
-    for s in range(shards):
-        same = (cell == row_ref[:, s * slots : (s + 1) * slots]).astype(BF16)
-        total += jnp.dot(same, contrib[s * slots : (s + 1) * slots, :], preferred_element_type=F32)
-    merged = total[:, :LANES] + total[:, LANES:]
-    lane = lax.broadcasted_iota(jnp.int32, (rows, LANES), 1)
-    for place in range(4):
-        merged = jnp.where(lane == channels + place, cols_ref[here, 3 + place : 4 + place], merged)
-    out_ref[...] = merged.T[:height].astype(BF16)
+    used = jnp.logical_or(step == 0, step * rows < live[0])
+
+    @pl.when(used)
+    def _():
+        cell = cols_ref[here, 2:3]
+        total = jnp.zeros((rows, 2 * LANES), F32)
+        for s in range(shards):
+            same = (cell == row_ref[:, s * slots : (s + 1) * slots]).astype(BF16)
+            total += jnp.dot(
+                same, contrib[s * slots : (s + 1) * slots, :], preferred_element_type=F32
+            )
+        merged = total[:, :LANES] + total[:, LANES:]
+        lane = lax.broadcasted_iota(jnp.int32, (rows, LANES), 1)
+        for place in range(4):
+            merged = jnp.where(
+                lane == channels + place, cols_ref[here, 3 + place : 4 + place], merged
+            )
+        out_ref[...] = merged.T[:height].astype(BF16)
+
+    @pl.when(jnp.logical_not(used))
+    def _():
+        out_ref[...] = jnp.zeros_like(out_ref)
 
 
 def regrid_listed(source_all, recv_src, recv_cell, recv_weight, lat_dev, lon_dev, slot_count):
     shards, channels, src_rows = source_all.shape
     total = recv_src.shape[0]
-    ordered = jnp.sort(recv_cell)
+    keys = jnp.where(recv_weight != 0, recv_cell, lat_dev * lon_dev)
+    ordered = jnp.sort(keys)
     lead = jnp.concatenate([jnp.ones((1,), jnp.bool_), ordered[1:] != ordered[:-1]])
     limits = jnp.arange(lat_dev + 1, dtype=jnp.int32) * lon_dev
-    starts = jnp.sum((recv_cell[None, :] < limits[:, None]).astype(jnp.int32), axis=1)
+    starts = jnp.sum((keys[None, :] < limits[:, None]).astype(jnp.int32), axis=1)
+    live = starts[lat_dev:]
     starts = jnp.zeros((total,), jnp.int32).at[: lat_dev + 1].set(starts)
     cols = jnp.stack(
         [
@@ -146,18 +169,21 @@
         functools.partial(
             regrid_kernel, channels=channels, shards=shards, slots=slot_count, src_rows=src_rows
         ),
-        grid=(total // rows,),
+        grid_spec=pltpu.PrefetchScalarGridSpec(
+            num_scalar_prefetch=1,
+            grid=(total // rows,),
+            in_specs=[
+                pl.BlockSpec((shards, channels, src_rows), lambda i, n: (0, 0, 0)),
+                pl.BlockSpec((total, 8), lambda i, n: (0, 0)),
+                pl.BlockSpec((1, total), lambda i, n: (0, 0)),
+            ],
+            out_specs=pl.BlockSpec((height, rows), lambda i, n: (0, i)),
+            scratch_shapes=[pltpu.VMEM((total, 2 * LANES), BF16)],
+        ),
         out_shape=jax.ShapeDtypeStruct((height, total), BF16),
-        in_specs=[
-            pl.BlockSpec((shards, channels, src_rows), lambda i: (0, 0, 0)),
-            pl.BlockSpec((total, 8), lambda i: (0, 0)),
-            pl.BlockSpec((1, total), lambda i: (0, 0)),
-        ],
-        out_specs=pl.BlockSpec((height, rows), lambda i: (0, i)),
-        scratch_shapes=[pltpu.VMEM((total, 2 * LANES), BF16)],
         compiler_params=pltpu.CompilerParams(vmem_limit_bytes=VMEM_BYTES),
         cost_estimate=work(4 * total * total * LANES, 2 * total * LANES),
-    )(source_all, cols, recv_cell.astype(F32)[None, :])
+    )(live, source_all, cols, keys.astype(F32)[None, :])
 
 
 def zonal_kernel(
@@ -173,12 +199,13 @@
     channels,
     blocks,
     block_rows,
+    lat_dev,
 ):
     *out_refs, delta, hots, base = rest
     step = pl.program_id(0)
     total = blocks * block_rows
-    groups, lats, height, width = out_refs[0].shape
-    columns = groups * height * len(out_refs)
+    lats, height, width = out_refs[0].shape
+    columns = height * len(out_refs)
     chunk = min(512, block_rows)
 
     def encode(values):
@@ -196,21 +223,27 @@
         points = basis_ref.shape[1]
         lane = lax.broadcasted_iota(jnp.int32, (chunk, points), 1).astype(F32)
 
-        def one(j, carry):
-            at = pl.ds(pl.multiple_of(j * chunk, chunk), chunk)
-            per_block = block_rows // chunk
-            part = pl.ds(pl.multiple_of((j % per_block) * chunk, chunk), chunk)
-            values = rows_ref[j // per_block, :, part].astype(F32).T
-            delta[at, :] = (encode(values.astype(BF16)) - empty).astype(BF16)
-            point = values[:, channels : channels + 1]
-            lead = values[:, channels + 1 : channels + 2]
-            point = jnp.where(lead > 0.5, point, -1.0)
-            hot = (point == lane).astype(BF16)
-            block = basis_ref[j // per_block]
-            hots[at, :] = jnp.dot(hot, block, preferred_element_type=F32).astype(BF16)
-            return carry
-
-        lax.fori_loop(0, total // chunk, one, 0)
+        per_block = block_rows // chunk
+
+        def one_block(k, carry):
+            used = starts[k, lat_dev] + TILE + WINDOW
+            count = jnp.minimum((used + chunk - 1) // chunk, per_block)
+
+            def one(j, inner):
+                at = pl.ds(pl.multiple_of(k * block_rows + j * chunk, chunk), chunk)
+                part = pl.ds(pl.multiple_of(j * chunk, chunk), chunk)
+                values = rows_ref[k, :, part].astype(F32).T
+                delta[at, :] = (encode(values.astype(BF16)) - empty).astype(BF16)
+                point = values[:, channels : channels + 1]
+                lead = values[:, channels + 1 : channels + 2]
+                point = jnp.where(lead > 0.5, point, -1.0)
+                hot = (point == lane).astype(BF16)
+                hots[at, :] = jnp.dot(hot, basis_ref[k], preferred_element_type=F32).astype(BF16)
+                return inner
+
+            return lax.fori_loop(0, count, one, carry)
+
+        lax.fori_loop(0, blocks, one_block, 0)
 
     place = lax.broadcasted_iota(jnp.int32, (WINDOW, columns), 0)
 
@@ -230,7 +263,8 @@
         def window(j, running):
             left, right = [], []
             for k in range(blocks):
-                first = jnp.minimum(firsts[k] + j * WINDOW, total)
+                ceiling = (highs[k] + TILE - 1) // TILE * TILE
+                first = jnp.minimum(firsts[k] + j * WINDOW, ceiling)
                 first = pl.multiple_of(first, TILE)
                 at = pl.ds(first, WINDOW)
                 inside = (place >= lows[k] - first) & (place < highs[k] - first)
@@ -245,29 +279,31 @@
 
         result = window(0, base[...])
         result = lax.fori_loop(1, most, window, result).astype(BF16)
-        for g in range(groups):
-            for h, out_ref in enumerate(out_refs):
-                low = (g * len(out_refs) + h) * height
-                out_ref[g, tt] = result[low : low + height, :]
+        for g, out_ref in enumerate(out_refs):
+            out_ref[tt] = result[g * height : (g + 1) * height, :]
         return carry
 
     lax.fori_loop(0, lats, latitude, 0)
 
 
 def zonal_transform(
-    rows, starts, w1, b1, w2, b2, basis, sums, lat_dev, groups, sets, channels, lats=15
+    rows, starts, w1, b1, w2, b2, basis, sums, lat_dev, pieces, channels, lats=15
 ):
     blocks, depth, block_rows = rows.shape
     width = w2.shape[1]
     columns = basis.shape[2]
-    height = columns // (groups * sets)
+    height = columns // pieces
     total = blocks * block_rows
     whole = lambda shape: pl.BlockSpec(
         shape, lambda i, s: (0,) * len(shape), pipeline_mode=pl.Buffered(1)
     )
     return pl.pallas_call(
         functools.partial(
-            zonal_kernel, channels=channels, blocks=blocks, block_rows=block_rows
+            zonal_kernel,
+            channels=channels,
+            blocks=blocks,
+            block_rows=block_rows,
+            lat_dev=lat_dev,
         ),
         grid_spec=pltpu.PrefetchScalarGridSpec(
             num_scalar_prefetch=1,
@@ -281,31 +317,42 @@
                 whole(basis.shape),
                 whole(sums.shape),
             ],
-            out_specs=[pl.BlockSpec((groups, lats, height, width), lambda i, s: (0, i, 0, 0))]
-            * sets,
+            out_specs=[pl.BlockSpec((lats, height, width), lambda i, s: (i, 0, 0))] * pieces,
             scratch_shapes=[
                 pltpu.VMEM((total + WINDOW, width), BF16),
                 pltpu.VMEM((total + WINDOW, columns), BF16),
                 pltpu.VMEM((columns, width), F32),
             ],
         ),
-        out_shape=[jax.ShapeDtypeStruct((groups, lat_dev, height, width), BF16)] * sets,
+        out_shape=[jax.ShapeDtypeStruct((lat_dev, height, width), BF16)] * pieces,
         compiler_params=pltpu.CompilerParams(vmem_limit_bytes=VMEM_BYTES),
         cost_estimate=work(50 * total * width * 2 * columns, 2 * total * width),
     )(starts, rows, w1, b1, w2, b2, basis, sums)
 
 
-def orders_kernel(place, spec_ref, fwd_ref, inv_ref, mix_ref, swap_ref, out_ref, taken, made, *, group):
+def orders_kernel(place, bands, *refs, group, pieces):
+    spec_refs = refs[:pieces]
+    fwd_ref, inv_ref, mix_ref, swap_ref, out_ref, arrived, taken, made, sems = refs[pieces:]
     order = pl.program_id(0)
-    lat_total, _, width = spec_ref.shape
-    parts, halves, part_lats, _, lanes = out_ref.shape
+    lats = spec_refs[0].shape[0]
+    lat_total, _, width = arrived.shape
+    halves, lanes = out_ref.shape[1], out_ref.shape[4]
     side = 2 * group
 
     @pl.when(order == 0)
     def _():
+        copies = [
+            pltpu.make_async_copy(ref, arrived.at[pl.ds(bands[d] * lats, lats)], sems.at[d])
+            for d, ref in enumerate(spec_refs)
+        ]
+        for copy in copies:
+            copy.start()
+        for copy in copies:
+            copy.wait()
+
         def one(j, carry):
             at = pl.ds(pl.multiple_of(j * side, side), side)
-            block = spec_ref[at].reshape(side * side, width)
+            block = arrived[at].reshape(side * side, width)
             turned = jnp.dot(swap_ref[...], block, preferred_element_type=F32).astype(BF16)
             taken[:, at, :] = turned.reshape(side, side, width)
             return carry
@@ -313,7 +360,9 @@
         lax.fori_loop(0, lat_total // side, one, 0)
 
     spectrum = jnp.concatenate([taken[2 * order], taken[2 * order + 1]], axis=1)
-    coeffs = jnp.dot(fwd_ref[0], spectrum, preferred_element_type=F32).astype(BF16)
+    coeffs = lax.dot_general(
+        fwd_ref[0], spectrum, (((0,), (0,)), ((), ())), preferred_element_type=F32
+    ).astype(BF16)
     mixed = jnp.dot(coeffs, mix_ref[...], preferred_element_type=F32).astype(BF16)
     made[order] = jnp.dot(inv_ref[0], mixed, preferred_element_type=F32).astype(BF16)
 
@@ -343,9 +392,11 @@
         lax.fori_loop(0, lat_total // side, one, 0)
 
 
-def order_steps(place, spectra, fwd_table, inv_table, mix_t, first, parts, halves):
-    lat_total, side, width = spectra.shape
-    degrees = fwd_table.shape[1]
+def order_steps(place, bands, spectra, fwd_table, inv_table, mix_t, first, parts, halves):
+    pieces = len(spectra)
+    lats, side, width = spectra[0].shape
+    lat_total = lats * pieces
+    degrees = fwd_table.shape[2]
     group = side // 2
     index = jnp.arange(side * side, dtype=jnp.int32)
     swapped = (index % side) * side + index // side
@@ -354,21 +405,23 @@
     part_lats = lat_total // parts
     out_shape = (parts, halves, part_lats, side, width // halves)
     return pl.pallas_call(
-        functools.partial(orders_kernel, group=group),
+        functools.partial(orders_kernel, group=group, pieces=pieces),
         grid_spec=pltpu.PrefetchScalarGridSpec(
-            num_scalar_prefetch=1,
+            num_scalar_prefetch=2,
             grid=(group,),
-            in_specs=[
-                pl.BlockSpec((lat_total, side, width), lambda r, s: (0, 0, 0)),
-                pl.BlockSpec((1, degrees, lat_total), lambda r, s: (first + r, 0, 0)),
-                pl.BlockSpec((1, lat_total, degrees), lambda r, s: (first + r, 0, 0)),
-                pl.BlockSpec((both, both), lambda r, s: (0, 0)),
-                pl.BlockSpec((side * side, side * side), lambda r, s: (0, 0)),
+            in_specs=[pl.BlockSpec(memory_space=pl.ANY)] * pieces
+            + [
+                pl.BlockSpec((1, lat_total, degrees), lambda r, s, b: (first + r, 0, 0)),
+                pl.BlockSpec((1, lat_total, degrees), lambda r, s, b: (first + r, 0, 0)),
+                pl.BlockSpec((both, both), lambda r, s, b: (0, 0)),
+                pl.BlockSpec((side * side, side * side), lambda r, s, b: (0, 0)),
             ],
-            out_specs=pl.BlockSpec(out_shape, lambda r, s: (0, 0, 0, 0, 0)),
+            out_specs=pl.BlockSpec(out_shape, lambda r, s, b: (0, 0, 0, 0, 0)),
             scratch_shapes=[
+                pltpu.VMEM((lat_total, side, width), BF16),
                 pltpu.VMEM((side, lat_total, width), BF16),
                 pltpu.VMEM((group, lat_total, both), BF16),
+                pltpu.SemaphoreType.DMA((pieces,)),
             ],
         ),
         out_shape=jax.ShapeDtypeStruct(out_shape, BF16),
@@ -376,13 +429,15 @@
         cost_estimate=work(
             group * 2 * both * degrees * (2 * lat_total + both), 8 * group * degrees * lat_total
         ),
-    )(place, spectra, fwd_table, inv_table, mix_t, swap)
+    )(place, bands, *spectra, fwd_table, inv_table, mix_t, swap)
 
 
 def synthesis_kernel(*refs):
     *mode_refs, basis_ref, out_ref = refs
-    sources, lats, height, lanes = mode_refs[0].shape
-    blocks, _, points, _ = out_ref.shape
+    sources, _, height, lanes = mode_refs[0].shape
+    blocks = out_ref.shape[0]
+    lats = mode_refs[0].shape[1]
+    points = out_ref.shape[1] // lats
     right = jnp.concatenate(
         [
             jnp.concatenate(
@@ -394,9 +449,12 @@
     )
 
     def one(k, carry):
-        value = jnp.dot(basis_ref[k], right, preferred_element_type=F32).astype(BF16)
-        for t in range(lats):
-            out_ref[k, t] = value[:points, t * lanes : (t + 1) * lanes]
+        value = jnp.dot(basis_ref[k], right, preferred_element_type=F32)
+        span = 4 * points
+        for t in range(0, lats, 4):
+            rows = [value[:points, (t + i) * lanes : (t + i + 1) * lanes] for i in range(4)]
+            low = t * points
+            out_ref[k, low : low + span, :] = jnp.concatenate(rows, axis=0).astype(BF16)
         return carry
 
     lax.fori_loop(0, blocks, one, 0)
@@ -414,57 +472,53 @@
             for _ in modes
         ]
         + [pl.BlockSpec(basis.shape, lambda i: (0, 0, 0))],
-        out_specs=pl.BlockSpec((blocks, lats, points, lanes), lambda i: (0, i, 0, 0)),
-        out_shape=jax.ShapeDtypeStruct((blocks, count, points, lanes), BF16),
+        out_specs=pl.BlockSpec((blocks, lats * points, lanes), lambda i: (0, i, 0)),
+        out_shape=jax.ShapeDtypeStruct((blocks, count * points, lanes), BF16),
         compiler_params=pltpu.CompilerParams(vmem_limit_bytes=VMEM_BYTES),
         cost_estimate=work(2 * count * lanes * basis.size, 4 * blocks * count * points * lanes),
     )(*modes, basis)
 
 
-def finish_kernel(part_ref, enc_ref, out_ref, flat, *, first, whole_groups, rest):
-    quarters, _, lats, points, lanes = part_ref.shape
-    group = pl.program_id(1) + first
-
-    def fill(count):
-        for q in range(quarters):
-            for t in range(count):
-                row = (q * count + t) * points
-                flat[row : row + points, :] = part_ref[q, 0, t].astype(F32)
+def finish_kernel(part_ref, enc_ref, out_ref, *, first, whole_groups, rest_rows):
+    quarters, halves, rows, lanes = part_ref.shape
+    group = pl.program_id(0) + first
 
     @pl.when(group < whole_groups)
     def _():
-        fill(lats)
+        for q in range(quarters):
+            at = pl.ds(q * rows, rows)
+            for h in range(halves):
+                across = pl.ds(h * lanes, lanes)
+                total = enc_ref[at, across].astype(F32) + part_ref[q, h].astype(F32)
+                out_ref[at, across] = total.astype(BF16)
 
     @pl.when(group >= whole_groups)
     def _():
-        fill(rest)
-
-    def one(j, carry):
-        at = pl.ds(pl.multiple_of(j * lanes, lanes), lanes)
-        out_ref[:, at] = (enc_ref[:, at].astype(F32) + flat[at, :].T).astype(BF16)
-        return carry
-
-    lax.fori_loop(0, out_ref.shape[1] // lanes, one, 0)
-
-
-def finish_steps(part, running, lats, first, whole_groups, rest):
-    quarters, halves, count, points, lanes = part.shape
-    span = quarters * lats * points
+        count = quarters * rest_rows
+        for h in range(halves):
+            across = pl.ds(h * lanes, lanes)
+            pieces = [part_ref[q, h].astype(F32)[:rest_rows] for q in range(quarters)]
+            total = enc_ref[:count, across].astype(F32) + jnp.concatenate(pieces, axis=0)
+            out_ref[:count, across] = total.astype(BF16)
+
+
+def finish_steps(part, running, lats, points, first, whole_groups, rest):
+    quarters, halves, count, lanes = part.shape
+    rows = lats * points
     return pl.pallas_call(
         functools.partial(
-            finish_kernel, first=first, whole_groups=whole_groups, rest=rest
+            finish_kernel, first=first, whole_groups=whole_groups, rest_rows=rest * points
         ),
-        grid=(halves, -(-count // lats)),
+        grid=(-(-count // rows),),
         in_specs=[
-            pl.BlockSpec((quarters, 1, lats, points, lanes), lambda h, i: (0, h, i, 0, 0)),
-            pl.BlockSpec((lanes, span), lambda h, i: (h, i + first)),
+            pl.BlockSpec((quarters, halves, rows, lanes), lambda i: (0, 0, i, 0)),
+            pl.BlockSpec((quarters * rows, halves * lanes), lambda i: (i + first, 0)),
         ],
-        out_specs=pl.BlockSpec((lanes, span), lambda h, i: (h, i + first)),
+        out_specs=pl.BlockSpec((quarters * rows, halves * lanes), lambda i: (i + first, 0)),
         out_shape=jax.ShapeDtypeStruct(running.shape, BF16),
-        scratch_shapes=[pltpu.VMEM((span, lanes), F32)],
         input_output_aliases={1: 0},
         compiler_params=pltpu.CompilerParams(vmem_limit_bytes=VMEM_BYTES),
-        cost_estimate=work(part.size * 40, 6 * part.size),
+        cost_estimate=work(part.size * 4, 6 * part.size),
     )(part, running)
 
 
@@ -495,7 +549,8 @@
     quarters = lon_count // halves
     part_lats = lat_dev // quarters
 
-    source_all = lax.all_gather(source_cells, "lon", axis=0, tiled=False)
+    source_all = jnp.broadcast_to(source_cells[None], (lon_count,) + source_cells.shape)
+    source_all = lax.all_to_all(source_all, "lon", split_axis=0, concat_axis=0, tiled=True)
     listed = regrid_listed(
         source_all, recv_src, recv_cell, recv_weight, lat_dev, lon_dev, slot_count
     )
@@ -504,9 +559,11 @@
     starts = coded[:, 0] * 128 + coded[:, 1]
 
     mine = lax.axis_index("lon")
+    sets = ord_dev // ORDER_GROUP
+    bands = lax.axis_index("lat") ^ jnp.arange(lat_count, dtype=jnp.int32)
     owned = (
-        (jnp.arange(lat_count, dtype=jnp.int32)[:, None] * lon_count + mine) * ord_dev
-        + jnp.arange(ord_dev, dtype=jnp.int32)[None, :]
+        (bands[None, :, None] * lon_count + mine) * ord_dev
+        + jnp.arange(ord_dev, dtype=jnp.int32).reshape(sets, 1, ORDER_GROUP)
     ).reshape(-1)
     point_rows = -(-lon_dev // LANES) * LANES
     at = jnp.arange(lon_count, dtype=jnp.int32)[:, None] * lon_dev + jnp.arange(
@@ -516,7 +573,6 @@
     basis_in = jnp.where(inside, basis_by_point(owned, at), 0)
     sums = jnp.sum(basis_in.astype(F32), axis=(0, 1))[:, None]
     w1 = jnp.zeros((band.shape[1], width), BF16).at[:channels].set(enc_w1.T)
-    sets = ord_dev // ORDER_GROUP
     spectra = zonal_transform(
         band,
         starts,
@@ -527,8 +583,7 @@
         basis_in,
         sums,
         lat_dev,
-        lat_count,
-        sets,
+        sets * lat_count,
         channels,
     )
 
@@ -543,13 +598,23 @@
     place = jnp.asarray(place.reshape(-1), jnp.int32)
 
     mix_t = mixing_matrix(mix_weight).T
-    modes = []
+    fwd_by_lat = fwd_table.transpose(0, 2, 1)
+    modes, waiting, got = [], [], []
     for g in range(sets):
-        got = lax.all_to_all(spectra[g], "lat", split_axis=0, concat_axis=0, tiled=True)
+        sent = spectra[g * lat_count : (g + 1) * lat_count]
+        if got:
+            sent, got[1:] = lax.optimization_barrier((list(sent), got[1:]))
+        got = [sent[0]] + [
+            lax.ppermute(sent[d], "lat", [(i, i ^ d) for i in range(lat_count)])
+            for d in range(1, lat_count)
+        ]
+        waiting.append(got)
+    for g in range(sets):
         made = order_steps(
             place,
-            got.reshape(lat_total, 2 * ORDER_GROUP, width),
-            fwd_table,
+            bands,
+            waiting[g],
+            fwd_by_lat,
             inv_table,
             mix_t,
             g * ORDER_GROUP,
@@ -571,26 +636,24 @@
     basis_out = jnp.where(inside, basis_out, 0)
 
     piece = source_all.transpose(1, 0, 2).reshape(channels, -1)
-    encoded = dense_encoder(
+    regridded = regrid_all(
         piece,
         recv_src.reshape(lon_count, slot_count),
         recv_cell.reshape(lon_count, slot_count),
         recv_weight.reshape(lon_count, slot_count),
         cells_dev,
-        enc_w1,
-        enc_b1,
-        enc_w2,
-        enc_b2,
-    )
+    )
+    encoded = encoder_by_cell(regridded, enc_w1, enc_b1, enc_w2, enc_b2)
+    modes[-1], encoded = lax.optimization_barrier((modes[-1], encoded))
     running = encoded
     step = CHUNK_RUNS * LATS
     for first in range(0, part_lats, step):
         count = min(step, part_lats - first)
         part = synthesis_steps(modes, basis_out, lon_dev, LATS, first, count)
         part = lax.all_to_all(part, "lon", split_axis=0, concat_axis=0, tiled=True)
-        part = part.reshape(quarters, halves, count, lon_dev, LANES)
-        running = finish_steps(part, running, LATS, first // LATS, whole_groups, rest)
-    return running
+        part = part.reshape(quarters, halves, count * lon_dev, LANES)
+        running = finish_steps(part, running, LATS, lon_dev, first // LATS, whole_groups, rest)
+    return running.T
 
 
 def dense_plan(
@@ -621,9 +684,8 @@
     orders_total = ORDERS
     ord_dev = fwd_table.shape[0]
     piece = lax.all_gather(source_cells, "lon", axis=1, tiled=True)
-    encoded = dense_encoder(
-        piece, sources, targets, weights, cells_dev, enc_w1, enc_b1, enc_w2, enc_b2
-    )
+    regridded = regrid_all(piece, sources, targets, weights, cells_dev).T
+    encoded = dense_encoder(regridded, enc_w1, enc_b1, enc_w2, enc_b2)
     blocked = encoded.reshape(width, lat_dev, 1, lon_dev)
     circles = lax.all_to_all(blocked, "lon", split_axis=0, concat_axis=2, tiled=True).reshape(
         ch_dev * lat_dev, NLON
@@ -702,7 +764,8 @@
             and lon_count % halves == 0
             and lat_dev % (lon_count // halves) == 0
             and lat_dev % 15 == 0
-            and (lon_count // halves) * LATS * (NLON // lon_count) % LANES == 0
+            and lat_count & (lat_count - 1) == 0
+            and 4 * (NLON // lon_count) % TILE == 0
             and lat_dev // (lon_count // halves) < 64
             and ord_dev % ORDER_GROUP == 0
             and lat_total % TILE == 0

time: 1180 us -> 1110 us (0.941); the launches traced: 1180 us -> 1100 us
  waiting for transfers between devices: 472 us -> 606 us
  blocking collectives: 109 us -> 0 us
  local copies, waits for them, and re-layouts: 77.4 us -> 17 us
  Pallas kernels: 299 us -> 260 us
  matrix products: 96.5 us -> 80.4 us
    all_to_all x3, waiting for transfers between devices: 179 us -> 323 us  [listed_plan(): part = lax.all_to_all(part, 'lon', split_axis=0, concat_axis=0, tiled=True)]
    all_to_all x2, waiting for transfers between devices: 198 us -> 70.6 us  [listed_plan(): lax.all_to_all(made, ('lat', 'lon'), split_axis=0, concat_axis=0, tiled=T...]
    ppermute x0 -> x6, waiting for transfers between devices: none -> 126 us  [listed_plan(): lax.ppermute(sent[d], 'lat', [(i, i ^ d) for i in range(lat_count)])]
    all_to_all x1 -> x0, blocking collectives: 73.2 us -> none  [listed_plan(): lax.all_to_all(spectra[g], 'lat', split_axis=0, concat_axis=0, tiled=True)]
    pallas_call x3, Pallas kernels: 66.8 us -> 19.3 us  [finish_steps(): pl.pallas_call(functools.partial(finish_kernel, first=first, whole_groups...]
    all_gather x1 -> x0, blocking collectives: 35.9 us -> none  [listed_plan(): source_all = lax.all_gather(source_cells, 'lon', axis=0, tiled=False)]
    pallas_call x3 -> x0, local copies, waits for them, and re-layouts: 34.7 us -> none  [the longest x1 22.3 us: finish_steps(): pl.pallas_call(functools.partial(finish_kernel, first=first, whole_groups...]
    dot_general x1, matrix products: 96.5 us -> 80.4 us  [encoder_by_cell(): jnp.dot(hidden, enc_w2.T, preferred_element_type=F32) + enc_b2]
  transfers between devices with their start and end apart: 7 -> 13, of which waited for: 6 -> 11; matrix products, arithmetic and copies ran while one was open for 18% -> 16% of each run, Pallas kernels for 12% -> 7%
where the time goes in v3:
time: 1110 us; the launch traced here: 1100 us
  waiting for transfers between devices  606 us (55%)
  Pallas kernels  260 us (23%)
  other arithmetic  83.3 us (8%)
  matrix products  80.4 us (7%)
  starting transfers between devices  34.2 us (3%)
  local copies, waits for them, and re-layouts  17 us (2%)
  between operations  14.2 us (1%)
    all_to_all x3, waiting for transfers between devices, listed_plan(): part = lax.all_to_all(part, 'lon', split_axis=0, concat_axis=0, tiled=True)  323 us
    ppermute x6, waiting for transfers between devices, listed_plan(): lax.ppermute(sent[d], 'lat', [(i, i ^ d) for i in range(lat_count)])  126 us
    pallas_call x1, Pallas kernels, zonal_transform(): pl.pallas_call(functools.partial(zonal_kernel, channels=channels, blocks=...  113 us
    dot_general x1, matrix products, encoder_by_cell(): jnp.dot(hidden, enc_w2.T, preferred_element_type=F32) + enc_b2  80.4 us
    all_gather x1, waiting for transfers between devices, listed_plan(): band = lax.all_gather(listed, 'lon', axis=0, tiled=False)  80.2 us
    pallas_call x2, Pallas kernels, order_steps(): pl.pallas_call(functools.partial(orders_kernel, group=group, pieces=piece...  72.5 us
    all_to_all x2, waiting for transfers between devices, listed_plan(): lax.all_to_all(made, ('lat', 'lon'), split_axis=0, concat_axis=0, tiled=T...  70.6 us
    scatter-add x1, other arithmetic, spread(): return running.at[targets.reshape(-1)].add(contrib.reshape(-1, channels))  44.4 us
  transfers between devices with their start and end apart: 13, of which 11 were waited for; matrix products, arithmetic and copies ran while one was open for 16% of the time, Pallas kernels for 7%

profile of v3, /device:TPU:0, one launch (start us, length us, event | category | flops | bytes accessed | tf_op | source)
XLA Modules:
  0.0 1095.3 jit_solution(8555268861958516457)
XLA Ops:
  6.5 1.8 broadcast_in_dim.88
  8.3 7.3 all-to-all-start
  15.7 1.4 broadcast_clamp_fusion
  18.2 5.8 sort.15
  24.3 0.9 stack.39
  25.2 1.9 copy.63.cols_ref
  27.1 5.8 all-to-all-done.src_ref
  32.9 0.9 copy-done
  33.7 13.6 %shard_map.118 = bf16[80,4096]{1,0:T(8,128)(2,1)} custom-call(s32[1]{0:T(128)} %slice.51.live, bf16[8,73,512]{2,1,0:T(8,128)(2,1)} %copy-done, f32[4096,8]{1,0:T(8,128)} %copy.63.cols_ref, f32[1,4096]{1,0:T(1,128)} %bitcast.61), custom_call_target="tpu_custom_call" | custom-call | flops 8589934592 | bytes 1048576 | tf_op jit(solution)/shard_map/pallas_call | solution.py:168
  47.5 0.8 copy.64
  48.4 2.6 cosine_multiply_fusion
  53.1 0.9 broadcast_select_fusion.1.basis_ref
  54.0 80.2 %all-gather.3.cloned.1.call-done = bf16[640,4096]{1,0:T(8,128)(2,1)} async-done(((bf16[80,4096]{1,0:T(8,128)(2,1)}), bf16[640,4096]{1,0:T(8,128)(2,1)}) %all-gather.3.cloned.1.call-update) | async-done | bytes 5242896 | tf_op jit(solution)/shard_map/all_gather | solution.py:557
  134.2 0.8 slice_convert_fusion
  135.6 113.4 %shard_map.119 = (bf16[180,16,256]{2,1,0:T(8,128)(2,1)}, bf16[180,16,256]{2,1,0:T(8,128)(2,1)}, bf16[180,16,256]{2,1,0:T(8,128)(2,1)}, bf16[180,16,256]{2,1,0:T(...) custom-call(s32[8,181]{1,0:T(8,128)} %bitcast.62, ...), custom_call_target="tpu_custom_call" | custom-call | flops 107374182400 | bytes 16777216 | tf_op jit(solution)/shard_map/pallas_call | solution.py:300
  249.1 3.5 collective-permute-start.1
  252.7 33.4 %collective-permute-done.1.refs_2_ = bf16[180,16,256]{2,1,0:T(8,128)(2,1)} collective-permute-done((bf16[180,16,256]{2,1,0:T(8,128)(2,1)}, bf16[180,16,256]{2,1,0:T(8,128)(2,1)}, u32[]{:S(2)}, u32[]{:S(2)}) %collective-permute-start.1) | collective-permute-done | bytes 1474592 | tf_op jit(solution)/shard_map/ppermute | solution.py:608
  286.0 31.1 %collective-permute-done.2.refs_3_ = bf16[180,16,256]{2,1,0:T(8,128)(2,1)} collective-permute-done((bf16[180,16,256]{2,1,0:T(8,128)(2,1)}, bf16[180,16,256]{2,1,0:T(8,128)(2,1)}, u32[]{:S(2)}, u32[]{:S(2)}) %collective-permute-start.2) | collective-permute-done | bytes 1474592 | tf_op jit(solution)/shard_map/ppermute | solution.py:608
  317.2 1.7 collective-permute-start.4
  319.8 0.8 maximum_bitcast_fusion.refs_6_
  320.6 0.7 fusion.35.refs_7_
  321.4 31.2 %collective-permute-done.4.refs_2_ = bf16[180,16,256]{2,1,0:T(8,128)(2,1)S(1)} collective-permute-done((bf16[180,16,256]{2,1,0:T(8,128)(2,1)}, bf16[180,16,256]{2,1,0:T(8,128)(2,1)S(1)}, u32[]{:S(2)}, u32[]{:S(2)}) %collective-permute-start.4) | collective-permute-done | bytes 1474592 | tf_op jit(solution)/shard_map/ppermute | solution.py:608
  352.6 30.6 %collective-permute-done.5.refs_3_ = bf16[180,16,256]{2,1,0:T(8,128)(2,1)} collective-permute-done((bf16[180,16,256]{2,1,0:T(8,128)(2,1)}, bf16[180,16,256]{2,1,0:T(8,128)(2,1)}, u32[]{:S(2)}, u32[]{:S(2)}) %collective-permute-start.5) | collective-permute-done | bytes 1474592 | tf_op jit(solution)/shard_map/ppermute | solution.py:608
  383.2 36.2 %shard_map.121 = bf16[16,2,45,16,128]{4,3,2,1,0:T(8,128)(2,1)} custom-call(s32[720]{0:T(1024)} %constant.259.clone.place, s32[4]{0:T(128)} %iota_xor_fusion.bands, bf16[180,16,256]{2,1,0:T(8,128)(2,1)} %get-tuple-element.60.refs_0_, bf16[180,16,256]{2,1,0:T(8,128)(2,1)} %copy-done.1, bf16[180,16,256]{2,1,0:T(8,128)(2,1)} %copy-done.2, ...), custom_call_target="tpu_custom_call" | custom-call | flops 8187281408 | bytes 23592960 | tf_op jit(solution)/shard_map/pallas_call | solution.py:407
  419.4 3.8 all-to-all-start.2
  423.4 19.5 %multiply_convert_fusion.1 = (bf16[8,192,512,1]{1,0,3,2:T(8,128)(2,1)S(1)}, bf16[8,192,512,1]{1,0,3,2:T(8,128)(2,1)S(1)}) fusion(s32[512]{0:T(512)S(1)} %reshape.396, s32[8,192]{1,0:T(8,128)S(1)} %iota_add_fusion), kind=kLoop, calls=%fused_computation.32 | loop fusion | flops 10223616 | bytes 3153920 | tf_op jit(solution)/shard_map/convert
  442.8 2.6 pad_maximum_fusion
  445.5 5.7 copy.71
  451.2 2.0 broadcast_select_fusion.refs_2_
  453.2 1.6 copy.72
  454.8 44.4 %scatter_custom_fusion = f32[32400,73]{1,0:T(8,128)} fusion(s32[4096]{0:T(1024)S(1)} %get-tuple-element.83, f32[]{:T(128)} %constant.206.clone.1, f32[4096]{0:T(1024)S(1)} %copy-done.4, pred[4096]{0:T(1024)(128)(4,1)S(1)} %compare_and_fusion, bf16[]{:T(256)} %constant.229.clone.1, bf16[4096,73]{1,0:T(8,128)(2,1)S(1)} %bitcast.46, ...), kind=kCustom, calls=%fused_computation.25 | custom fusion | flops 1196032 | bytes 10546246 | tf_op jit(solution)/shard_map/scatter-add | solution.py:51
  499.2 36.3 %shard_map.120 = bf16[16,2,45,16,128]{4,3,2,1,0:T(8,128)(2,1)} custom-call(s32[720]{0:T(1024)} %constant.259.clone.place, s32[4]{0:T(128)} %iota_xor_fusion.bands, bf16[180,16,256]{2,1,0:T(8,128)(2,1)} %get-tuple-element.49.refs_0_, bf16[180,16,256]{2,1,0:T(8,128)(2,1)} %collective-permute-done.refs_1_, ...), custom_call_target="tpu_custom_call" | custom-call | flops 8187281408 | bytes 23592960 | tf_op jit(solution)/shard_map/pallas_call | solution.py:407
  535.5 19.4 %all-to-all-done.2.refs_1_ = bf16[32,45,16,128]{3,2,1,0:T(8,128)(2,1)} async-done(((bf16[32,45,16,128]{3,2,1,0:T(8,128)(2,1)}), bf16[32,45,16,128]{3,2,1,0:T(8,128)(2,1)}, u32[]{:S(2)}, u32[]{:S(2)}) %all-to-all-start.2) | async-done | bytes 5898272 | tf_op jit(solution)/shard_map/all_to_all | solution.py:626
  554.9 3.6 all-to-all-start.1
  558.5 80.4 %fusion.enc_ref = bf16[32400,256]{1,0:T(8,128)(2,1)} fusion(bf16[256,256]{1,0:T(8,128)(2,1)S(1)} %copy-done.6, f32[256]{0:T(256)S(1)} %copy-done.11, bf16[256,73]{0,1:T(8,128)(2,1)S(1)} %copy-done.9, f32[256]{0:T(256)S(1)} %copy-done.10, f32[32400,73]{1,0:T(8,128)} %scatter_custom_fusion), kind=kOutput, calls=%fused_computation.5 | convolution fusion | flops 6024099840 | bytes 26220096 | tf_op jit(solution)/shard_map/dot_general | solution.py:89
  638.9 51.3 %all-to-all-done.1.refs_0_ = bf16[32,45,16,128]{3,2,1,0:T(8,128)(2,1)} async-done(((bf16[32,45,16,128]{3,2,1,0:T(8,128)(2,1)}), bf16[32,45,16,128]{3,2,1,0:T(8,128)(2,1)}, u32[]{:S(2)}, u32[]{:S(2)}) %all-to-all-start.1) | async-done | bytes 5898272 | tf_op jit(solution)/shard_map/all_to_all | solution.py:626
  690.2 13.9 %shard_map.123 = bf16[8,2880,128]{2,1,0:T(8,128)(2,1)} custom-call(bf16[32,45,16,128]{3,2,1,0:T(8,128)(2,1)} %all-to-all-done.1.refs_0_, bf16[32,45,16,128]{3,2,1,0:T(8,128)(2,1)} %all-to-all-done.2.refs_1_, bf16[8,192,1024]{2,1,0:T(8,128)(2,1)} %broadcast_select_fusion.refs_2_), custom_call_target="tpu_custom_call" | custom-call | flops 6442450944 | bytes 11796480 | tf_op jit(solution)/shard_map/pallas_call | solution.py:467
  704.1 4.7 all-to-all-start.4
  708.8 14.0 %shard_map.124 = bf16[8,2880,128]{2,1,0:T(8,128)(2,1)} custom-call(bf16[32,45,16,128]{3,2,1,0:T(8,128)(2,1)} %all-to-all-done.1.refs_0_, bf16[32,45,16,128]{3,2,1,0:T(8,128)(2,1)} %all-to-all-done.2.refs_1_, bf16[8,192,1024]{2,1,0:T(8,128)(2,1)} %broadcast_select_fusion.refs_2_), custom_call_target="tpu_custom_call" | custom-call | flops 6442450944 | bytes 11796480 | tf_op jit(solution)/shard_map/pallas_call | solution.py:467
  722.8 115.8 %all-to-all-done.4 = bf16[8,2880,128]{2,1,0:T(8,128)(2,1)} async-done(((bf16[8,2880,128]{2,1,0:T(8,128)(2,1)}), bf16[8,2880,128]{2,1,0:T(8,128)(2,1)}, u32[]{:S(2)}, u32[]{:S(2)}) %all-to-all-start.4) | async-done | bytes 5898272 | tf_op jit(solution)/shard_map/all_to_all | solution.py:653
  838.6 4.7 all-to-all-start.5
  843.3 13.6 %shard_map.122 = bf16[8,2340,128]{2,1,0:T(8,128)(2,1)} custom-call(bf16[32,45,16,128]{3,2,1,0:T(8,128)(2,1)} %all-to-all-done.1.refs_0_, bf16[32,45,16,128]{3,2,1,0:T(8,128)(2,1)} %all-to-all-done.2.refs_1_, bf16[8,192,1024]{2,1,0:T(8,128)(2,1)} %broadcast_select_fusion.refs_2_), custom_call_target="tpu_custom_call" | custom-call | flops 5234491392 | bytes 9584640 | tf_op jit(solution)/shard_map/pallas_call | solution.py:467
  857.0 115.3 %all-to-all-done.5 = bf16[8,2880,128]{2,1,0:T(8,128)(2,1)} async-done(((bf16[8,2880,128]{2,1,0:T(8,128)(2,1)}), bf16[8,2880,128]{2,1,0:T(8,128)(2,1)}, u32[]{:S(2)}, u32[]{:S(2)}) %all-to-all-start.5) | async-done | bytes 5898272 | tf_op jit(solution)/shard_map/all_to_all | solution.py:653
  972.3 4.6 all-to-all-start.3
  976.9 6.8 shard_map.125.enc_ref
  983.7 6.8 shard_map.126.enc_ref
  990.5 91.8 %all-to-all-done.3 = bf16[8,2340,128]{2,1,0:T(8,128)(2,1)} async-done(((bf16[8,2340,128]{2,1,0:T(8,128)(2,1)}), bf16[8,2340,128]{2,1,0:T(8,128)(2,1)}, u32[]{:S(2)}, u32[]{:S(2)}) %all-to-all-start.3) | async-done | bytes 4792352 | tf_op jit(solution)/shard_map/all_to_all | solution.py:653
  1082.3 5.7 shard_map.127
  (68 shorter events, 5.6 us)
Async XLA Ops:
  8.3 24.5 %all-to-all-start = ((bf16[8,73,512]{2,1,0:T(8,128)(2,1)}), bf16[8,73,512]{2,1,0:T(8,128)(2,1)S(1)}, u32[]{:S(2)}, u32[]{:S(2)}) async-start(bf16[8,73,512]{2,1,0:T(8,128)(2,1)} %broadcast_in_dim.88), calls=%async_computation | async-start | bytes 1310720 | tf_op jit(solution)/shard_map/all_to_all | solution.py:553
  15.6 118.6 %all-gather.3.cloned.1.call-start = ((), (), s32[]{:S(2)}) async-start(), calls=%async_computation.6 | async-start | bytes 5898240 | tf_op jit(solution)/shard_map/all_gather | solution.py:557
  27.1 20.4 %copy-start.5 = (bf16[256,256]{1,0:T(8,128)(2,1)S(1)}, bf16[256,256]{1,0:T(8,128)(2,1)}, u32[]{:S(2)}) copy-start(bf16[256,256]{1,0:T(8,128)(2,1)} %param.22) | copy-start | bytes 393220
  32.9 0.9 copy-start
  33.7 18.7 %copy-start.8 = (bf16[256,73]{0,1:T(8,128)(2,1)S(1)}, bf16[256,73]{0,1:T(8,128)(2,1)}, u32[]{:S(2)}) copy-start(bf16[256,73]{0,1:T(8,128)(2,1)} %param.20) | copy-start | bytes 112132
  135.6 183.4 %copy-start.3 = (bf16[2,256,256]{2,1,0:T(8,128)(2,1)S(1)}, bf16[2,256,256]{2,1,0:T(8,128)(2,1)}, u32[]{:S(2)}) copy-start(bf16[2,256,256]{2,1,0:T(8,128)(2,1)} %param.24) | copy-start | bytes 786436
  249.0 3.7 collective-permute-start
  249.1 37.0 %collective-permute-start.1 = (bf16[180,16,256]{2,1,0:T(8,128)(2,1)}, bf16[180,16,256]{2,1,0:T(8,128)(2,1)}, u32[]{:S(2)}, u32[]{:S(2)}) collective-permute-start(bf16[180,16,256]{2,1,0:T(8,128)(2,1)} %get-tuple-element.55), channel_id=1, source_target_pairs={{0,16},{8,24},{16,0},{24,8},{1,17},{9,25},{17,1},{25,9},{2,18},{10... | collective-permute-start | bytes 4423688 | tf_op jit(solution)/shard_map/ppermute | solution.py:608
  252.6 64.5 %collective-permute-start.2 = (bf16[180,16,256]{2,1,0:T(8,128)(2,1)}, bf16[180,16,256]{2,1,0:T(8,128)(2,1)}, u32[]{:S(2)}, u32[]{:S(2)}) collective-permute-start(bf16[180,16,256]{2,1,0:T(8,128)(2,1)} %get-tuple-element.56), channel_id=1, source_target_pairs={{0,24},{8,16},{16,8},{24,0},{1,25},{9,17},{17,9},{25,1},{2,26},{10... | collective-permute-start | bytes 4423688 | tf_op jit(solution)/shard_map/ppermute | solution.py:608
  317.1 4.2 collective-permute-start.3
  317.2 35.3 %collective-permute-start.4 = (bf16[180,16,256]{2,1,0:T(8,128)(2,1)}, bf16[180,16,256]{2,1,0:T(8,128)(2,1)S(1)}, u32[]{:S(2)}, u32[]{:S(2)}) collective-permute-start(bf16[180,16,256]{2,1,0:T(8,128)(2,1)} %get-tuple-element.62), channel_id=1, source_target_pairs={{0,16},{8,24},{16,0},{24,8},{1,17},{9,25},{17,1},{25,9},{2,18},{10... | collective-permute-start | bytes 4423688 | tf_op jit(solution)/shard_map/ppermute | solution.py:608
  319.0 64.2 %collective-permute-start.5 = (bf16[180,16,256]{2,1,0:T(8,128)(2,1)}, bf16[180,16,256]{2,1,0:T(8,128)(2,1)}, u32[]{:S(2)}, u32[]{:S(2)}) collective-permute-start(bf16[180,16,256]{2,1,0:T(8,128)(2,1)} %get-tuple-element.63), channel_id=1, source_target_pairs={{0,24},{8,16},{16,8},{24,0},{1,25},{9,17},{17,9},{25,1},{2,26},{10... | collective-permute-start | bytes 4423688 | tf_op jit(solution)/shard_map/ppermute | solution.py:608
  321.4 61.8 %copy-start.1 = (bf16[180,16,256]{2,1,0:T(8,128)(2,1)}, bf16[180,16,256]{2,1,0:T(8,128)(2,1)S(1)}, u32[]{:S(2)}) copy-start(bf16[180,16,256]{2,1,0:T(8,128)(2,1)S(1)} %collective-permute-done.3.refs_1_) | copy-start | bytes 4423684
  352.6 30.6 %copy-start.2 = (bf16[180,16,256]{2,1,0:T(8,128)(2,1)}, bf16[180,16,256]{2,1,0:T(8,128)(2,1)S(1)}, u32[]{:S(2)}) copy-start(bf16[180,16,256]{2,1,0:T(8,128)(2,1)S(1)} %collective-permute-done.4.refs_2_) | copy-start | bytes 4423684
  419.4 31.8 %copy-start.7 = (s32[4096]{0:T(1024)S(1)}, s32[4096]{0:T(1024)}, u32[]{:S(2)}) copy-start(s32[4096]{0:T(1024)} %param.17) | copy-start | bytes 49156
  419.4 135.5 %all-to-all-start.2 = ((bf16[32,45,16,128]{3,2,1,0:T(8,128)(2,1)}), bf16[32,45,16,128]{3,2,1,0:T(8,128)(2,1)}, u32[]{:S(2)}, u32[]{:S(2)}) async-start(bf16[32,45,16,128]{3,2,1,0:T(8,128)(2,1)} %bitcast.43), calls=%async_computation.2 | async-start | bytes 11796480 | tf_op jit(solution)/shard_map/all_to_all | solution.py:626
  423.2 31.6 %copy-start.4 = (f32[4096]{0:T(1024)S(1)}, f32[4096]{0:T(1024)}, u32[]{:S(2)}) copy-start(f32[4096]{0:T(1024)} %param.19) | copy-start | bytes 49156
  499.2 59.3 %copy-start.6 = (bf16[256,256]{1,0:T(8,128)(2,1)S(1)}, bf16[256,256]{1,0:T(8,128)(2,1)}, u32[]{:S(2)}) copy-start(bf16[256,256]{1,0:T(8,128)(2,1)} %param.22) | copy-start | bytes 393220
  499.2 59.3 %copy-start.9 = (bf16[256,73]{0,1:T(8,128)(2,1)S(1)}, bf16[256,73]{0,1:T(8,128)(2,1)}, u32[]{:S(2)}) copy-start(bf16[256,73]{0,1:T(8,128)(2,1)} %param.20) | copy-start | bytes 112132
  499.2 59.3 %copy-start.10 = (f32[256]{0:T(256)S(1)}, f32[256]{0:T(256)}, u32[]{:S(2)}) copy-start(f32[256]{0:T(256)} %param.21) | copy-start | bytes 3076
  499.2 59.3 %copy-start.11 = (f32[256]{0:T(256)S(1)}, f32[256]{0:T(256)}, u32[]{:S(2)}) copy-start(f32[256]{0:T(256)} %param.23) | copy-start | bytes 3076
  554.9 135.3 %all-to-all-start.1 = ((bf16[32,45,16,128]{3,2,1,0:T(8,128)(2,1)}), bf16[32,45,16,128]{3,2,1,0:T(8,128)(2,1)}, u32[]{:S(2)}, u32[]{:S(2)}) async-start(bf16[32,45,16,128]{3,2,1,0:T(8,128)(2,1)} %bitcast.44), calls=%async_computation.1 | async-start | bytes 11796480 | tf_op jit(solution)/shard_map/all_to_all | solution.py:626
  704.1 134.5 %all-to-all-start.4 = ((bf16[8,2880,128]{2,1,0:T(8,128)(2,1)}), bf16[8,2880,128]{2,1,0:T(8,128)(2,1)}, u32[]{:S(2)}, u32[]{:S(2)}) async-start(bf16[8,2880,128]{2,1,0:T(8,128)(2,1)} %shard_map.123), calls=%async_computation.4 | async-start | bytes 11796480 | tf_op jit(solution)/shard_map/all_to_all | solution.py:653
  838.6 133.7 %all-to-all-start.5 = ((bf16[8,2880,128]{2,1,0:T(8,128)(2,1)}), bf16[8,2880,128]{2,1,0:T(8,128)(2,1)}, u32[]{:S(2)}, u32[]{:S(2)}) async-start(bf16[8,2880,128]{2,1,0:T(8,128)(2,1)} %shard_map.124), calls=%async_computation.5 | async-start | bytes 11796480 | tf_op jit(solution)/shard_map/all_to_all | solution.py:653
  972.3 110.1 %all-to-all-start.3 = ((bf16[8,2340,128]{2,1,0:T(8,128)(2,1)}), bf16[8,2340,128]{2,1,0:T(8,128)(2,1)}, u32[]{:S(2)}, u32[]{:S(2)}) async-start(bf16[8,2340,128]{2,1,0:T(8,128)(2,1)} %shard_map.122), calls=%async_computation.3 | async-start | bytes 9601024 | tf_op jit(solution)/shard_map/all_to_all | solution.py:653
Sparse Core Ops, SparseCore 0:
  47.5 86.6 all-gather.2

commit v4 on v3

--- a/solution.py
+++ b/solution.py
@@ -13,7 +13,8 @@
 ORDERS = 512
 LANES = 128
 TILE = 16
-WINDOW = 32
+WINDOW = 48
+UNROLL = 3
 LATS = 8
 CHUNK_RUNS = 2
 ORDER_GROUP = 8
@@ -186,7 +187,77 @@
     )(live, source_all, cols, keys.astype(F32)[None, :])
 
 
-def zonal_kernel(
+def transform_latitudes(starts, hots, delta, base, out_refs, first_lat, blocks):
+    step = pl.program_id(0)
+    groups, lats, _, _ = out_refs[0].shape
+    columns = hots.shape[1]
+    block_rows = (hots.shape[0] - WINDOW) // blocks
+    place = lax.broadcasted_iota(jnp.int32, (WINDOW, columns), 0)
+
+    def bounds(t):
+        lows = [starts[k, t] + k * block_rows for k in range(blocks)]
+        highs = [starts[k, t + 1] + k * block_rows for k in range(blocks)]
+        firsts = [(low // TILE) * TILE for low in lows]
+        most = jnp.int32(1)
+        for k in range(blocks):
+            most = jnp.maximum(most, (highs[k] - firsts[k] + WINDOW - 1) // WINDOW)
+        return lows, highs, firsts, most
+
+    def window(lows, highs, firsts):
+        left, right = [], []
+        for k in range(blocks):
+            first = pl.multiple_of(firsts[k], TILE)
+            at = pl.ds(first, WINDOW)
+            inside = (place >= lows[k] - first) & (place < highs[k] - first)
+            left.append(jnp.where(inside, hots[at, :].astype(F32), 0.0).astype(BF16))
+            right.append(delta[at, :])
+        return lax.dot_general(
+            jnp.concatenate(left, axis=0),
+            jnp.concatenate(right, axis=0),
+            (((0,), (0,)), ((), ())),
+            preferred_element_type=F32,
+        )
+
+    def store(tt, result):
+        result = result.astype(BF16)
+        low = 0
+        for g in range(groups):
+            for out_ref in out_refs:
+                height = out_ref.shape[2]
+                out_ref[g, tt] = result[low : low + height, :]
+                low += height
+
+    def several(b, carry):
+        chosen = [b * UNROLL + u for u in range(UNROLL)]
+        limits = [bounds(first_lat + step * lats + tt) for tt in chosen]
+        most = limits[0][3]
+        for limit in limits[1:]:
+            most = jnp.maximum(most, limit[3])
+
+        @pl.when(most == 1)
+        def _():
+            for tt, (lows, highs, firsts, _) in zip(chosen, limits):
+                store(tt, base[...] + window(lows, highs, firsts))
+
+        @pl.when(most > 1)
+        def _():
+            for tt, (lows, highs, firsts, count) in zip(chosen, limits):
+
+                def more(j, running):
+                    moved = [
+                        jnp.minimum(firsts[k] + j * WINDOW, (highs[k] + TILE - 1) // TILE * TILE)
+                        for k in range(blocks)
+                    ]
+                    return running + window(lows, highs, moved)
+
+                store(tt, lax.fori_loop(0, count, more, base[...]))
+
+        return carry
+
+    lax.fori_loop(0, lats // UNROLL, several, 0)
+
+
+def zonal_first_kernel(
     starts,
     rows_ref,
     w1_ref,
@@ -201,12 +272,16 @@
     block_rows,
     lat_dev,
 ):
-    *out_refs, delta, hots, base = rest
+    *out_refs, delta_out, hots_out, base, delta, hots, sems = rest
     step = pl.program_id(0)
     total = blocks * block_rows
-    lats, height, width = out_refs[0].shape
-    columns = height * len(out_refs)
+    width = delta.shape[1]
+    columns = hots.shape[1]
     chunk = min(512, block_rows)
+    copies = [
+        pltpu.make_async_copy(delta, delta_out, sems.at[0]),
+        pltpu.make_async_copy(hots, hots_out, sems.at[1]),
+    ]
 
     def encode(values):
         hidden = jnp.dot(values, w1_ref[...], preferred_element_type=F32) + b1_ref[...]
@@ -222,7 +297,6 @@
         hots[pl.ds(total, WINDOW), :] = jnp.zeros((WINDOW, columns), BF16)
         points = basis_ref.shape[1]
         lane = lax.broadcasted_iota(jnp.int32, (chunk, points), 1).astype(F32)
-
         per_block = block_rows // chunk
 
         def one_block(k, carry):
@@ -244,62 +318,51 @@
             return lax.fori_loop(0, count, one, carry)
 
         lax.fori_loop(0, blocks, one_block, 0)
-
-    place = lax.broadcasted_iota(jnp.int32, (WINDOW, columns), 0)
-
-    def latitude(tt, carry):
-        t = step * lats + tt
-        lows, highs, firsts = [], [], []
-        most = jnp.int32(1)
-        for k in range(blocks):
-            low = starts[k, t] + k * block_rows
-            high = starts[k, t + 1] + k * block_rows
-            first = (low // TILE) * TILE
-            most = jnp.maximum(most, (high - first + WINDOW - 1) // WINDOW)
-            lows.append(low)
-            highs.append(high)
-            firsts.append(first)
-
-        def window(j, running):
-            left, right = [], []
-            for k in range(blocks):
-                ceiling = (highs[k] + TILE - 1) // TILE * TILE
-                first = jnp.minimum(firsts[k] + j * WINDOW, ceiling)
-                first = pl.multiple_of(first, TILE)
-                at = pl.ds(first, WINDOW)
-                inside = (place >= lows[k] - first) & (place < highs[k] - first)
-                left.append(jnp.where(inside, hots[at, :].astype(F32), 0.0).astype(BF16))
-                right.append(delta[at, :])
-            return running + lax.dot_general(
-                jnp.concatenate(left, axis=0),
-                jnp.concatenate(right, axis=0),
-                (((0,), (0,)), ((), ())),
-                preferred_element_type=F32,
-            )
-
-        result = window(0, base[...])
-        result = lax.fori_loop(1, most, window, result).astype(BF16)
-        for g, out_ref in enumerate(out_refs):
-            out_ref[tt] = result[g * height : (g + 1) * height, :]
-        return carry
-
-    lax.fori_loop(0, lats, latitude, 0)
-
-
-def zonal_transform(
-    rows, starts, w1, b1, w2, b2, basis, sums, lat_dev, pieces, channels, lats=15
-):
-    blocks, depth, block_rows = rows.shape
+        for copy in copies:
+            copy.start()
+
+    transform_latitudes(starts, hots, delta, base, out_refs, 0, blocks)
+
+    @pl.when(step == pl.num_programs(0) - 1)
+    def _():
+        for copy in copies:
+            copy.wait()
+
+
+def zonal_second_kernel(starts, delta, hots, base, *out_refs, first_lat, blocks):
+    transform_latitudes(starts, hots, delta, base, out_refs, first_lat, blocks)
+
+
+def whole_block(shape):
+    return pl.BlockSpec(shape, lambda i, *_: (0,) * len(shape), pipeline_mode=pl.Buffered(1))
+
+
+def zonal_outputs(groups, lat_count, heights, lats, width):
+    shapes = [jax.ShapeDtypeStruct((groups, lat_count, h, width), BF16) for h in heights]
+    specs = [pl.BlockSpec((groups, lats, h, width), lambda i, *_: (0, i, 0, 0)) for h in heights]
+    return shapes, specs
+
+
+def zonal_transform(rows, starts, w1, b1, w2, b2, basis, sums, lat_dev, groups, sets, channels):
+    blocks, _, block_rows = rows.shape
     width = w2.shape[1]
     columns = basis.shape[2]
-    height = columns // pieces
+    height = columns // groups
     total = blocks * block_rows
-    whole = lambda shape: pl.BlockSpec(
-        shape, lambda i, s: (0,) * len(shape), pipeline_mode=pl.Buffered(1)
-    )
-    return pl.pallas_call(
+    lats = 15
+    early = lat_dev // 3 // lats * lats
+    late = lat_dev - early
+    flops = 25 * total * width * 2 * columns
+    shapes, specs = zonal_outputs(groups, early, [height], lats, width)
+    kept = [
+        jax.ShapeDtypeStruct((total + WINDOW, width), BF16),
+        jax.ShapeDtypeStruct((total + WINDOW, columns), BF16),
+        jax.ShapeDtypeStruct((columns, width), F32),
+    ]
+    inputs = (rows, w1, b1, w2, b2, basis, sums)
+    first, delta, hots, base = pl.pallas_call(
         functools.partial(
-            zonal_kernel,
+            zonal_first_kernel,
             channels=channels,
             blocks=blocks,
             block_rows=block_rows,
@@ -307,44 +370,61 @@
         ),
         grid_spec=pltpu.PrefetchScalarGridSpec(
             num_scalar_prefetch=1,
-            grid=(lat_dev // lats,),
-            in_specs=[
-                whole(rows.shape),
-                whole(w1.shape),
-                whole(b1.shape),
-                whole(w2.shape),
-                whole(b2.shape),
-                whole(basis.shape),
-                whole(sums.shape),
-            ],
-            out_specs=[pl.BlockSpec((lats, height, width), lambda i, s: (i, 0, 0))] * pieces,
+            grid=(early // lats,),
+            in_specs=[whole_block(a.shape) for a in inputs],
+            out_specs=specs
+            + [pl.BlockSpec(memory_space=pl.ANY)] * 2
+            + [whole_block((columns, width))],
             scratch_shapes=[
                 pltpu.VMEM((total + WINDOW, width), BF16),
                 pltpu.VMEM((total + WINDOW, columns), BF16),
-                pltpu.VMEM((columns, width), F32),
+                pltpu.SemaphoreType.DMA((2,)),
             ],
         ),
-        out_shape=[jax.ShapeDtypeStruct((lat_dev, height, width), BF16)] * pieces,
+        out_shape=shapes + kept,
         compiler_params=pltpu.CompilerParams(vmem_limit_bytes=VMEM_BYTES),
-        cost_estimate=work(50 * total * width * 2 * columns, 2 * total * width),
-    )(starts, rows, w1, b1, w2, b2, basis, sums)
-
-
-def orders_kernel(place, bands, *refs, group, pieces):
+        cost_estimate=work(flops, 4 * total * width),
+    )(starts, *inputs)
+    shapes, specs = zonal_outputs(groups, late, [height // sets] * sets, lats, width)
+    second = pl.pallas_call(
+        functools.partial(zonal_second_kernel, first_lat=early, blocks=blocks),
+        grid_spec=pltpu.PrefetchScalarGridSpec(
+            num_scalar_prefetch=1,
+            grid=(late // lats,),
+            in_specs=[whole_block(a.shape) for a in (delta, hots, base)],
+            out_specs=specs,
+        ),
+        out_shape=shapes,
+        compiler_params=pltpu.CompilerParams(vmem_limit_bytes=VMEM_BYTES),
+        cost_estimate=work(flops, 4 * total * width),
+    )(starts, delta, hots, base)
+    return first, second
+
+
+def orders_kernel(place, *refs, group, pieces, rows):
     spec_refs = refs[:pieces]
     fwd_ref, inv_ref, mix_ref, swap_ref, out_ref, arrived, taken, made, sems = refs[pieces:]
     order = pl.program_id(0)
-    lats = spec_refs[0].shape[0]
     lat_total, _, width = arrived.shape
     halves, lanes = out_ref.shape[1], out_ref.shape[4]
     side = 2 * group
+    count = spec_refs[0].shape[0]
 
     @pl.when(order == 0)
     def _():
-        copies = [
-            pltpu.make_async_copy(ref, arrived.at[pl.ds(bands[d] * lats, lats)], sems.at[d])
-            for d, ref in enumerate(spec_refs)
-        ]
+        copies = []
+        for i in range(count):
+            low = i * lat_total // count
+            for ref, row in zip(spec_refs, rows):
+                lats = ref.shape[1]
+                copies.append(
+                    pltpu.make_async_copy(
+                        ref.at[i, :, pl.ds(row, side)],
+                        arrived.at[pl.ds(low, lats)],
+                        sems.at[len(copies)],
+                    )
+                )
+                low += lats
         for copy in copies:
             copy.start()
         for copy in copies:
@@ -392,10 +472,11 @@
         lax.fori_loop(0, lat_total // side, one, 0)
 
 
-def order_steps(place, bands, spectra, fwd_table, inv_table, mix_t, first, parts, halves):
+def order_steps(place, spectra, rows, fwd_table, inv_table, mix_t, first, parts, halves):
     pieces = len(spectra)
-    lats, side, width = spectra[0].shape
-    lat_total = lats * pieces
+    count, width = spectra[0].shape[0], spectra[0].shape[3]
+    side = 2 * ORDER_GROUP
+    lat_total = fwd_table.shape[1]
     degrees = fwd_table.shape[2]
     group = side // 2
     index = jnp.arange(side * side, dtype=jnp.int32)
@@ -405,23 +486,23 @@
     part_lats = lat_total // parts
     out_shape = (parts, halves, part_lats, side, width // halves)
     return pl.pallas_call(
-        functools.partial(orders_kernel, group=group, pieces=pieces),
+        functools.partial(orders_kernel, group=group, pieces=pieces, rows=rows),
         grid_spec=pltpu.PrefetchScalarGridSpec(
-            num_scalar_prefetch=2,
+            num_scalar_prefetch=1,
             grid=(group,),
             in_specs=[pl.BlockSpec(memory_space=pl.ANY)] * pieces
             + [
-                pl.BlockSpec((1, lat_total, degrees), lambda r, s, b: (first + r, 0, 0)),
-                pl.BlockSpec((1, lat_total, degrees), lambda r, s, b: (first + r, 0, 0)),
-                pl.BlockSpec((both, both), lambda r, s, b: (0, 0)),
-                pl.BlockSpec((side * side, side * side), lambda r, s, b: (0, 0)),
+                pl.BlockSpec((1, lat_total, degrees), lambda r, s: (first + r, 0, 0)),
+                pl.BlockSpec((1, lat_total, degrees), lambda r, s: (first + r, 0, 0)),
+                pl.BlockSpec((both, both), lambda r, s: (0, 0)),
+                pl.BlockSpec((side * side, side * side), lambda r, s: (0, 0)),
             ],
-            out_specs=pl.BlockSpec(out_shape, lambda r, s, b: (0, 0, 0, 0, 0)),
+            out_specs=pl.BlockSpec(out_shape, lambda r, s: (0, 0, 0, 0, 0)),
             scratch_shapes=[
                 pltpu.VMEM((lat_total, side, width), BF16),
                 pltpu.VMEM((side, lat_total, width), BF16),
                 pltpu.VMEM((group, lat_total, both), BF16),
-                pltpu.SemaphoreType.DMA((pieces,)),
+                pltpu.SemaphoreType.DMA((pieces * count,)),
             ],
         ),
         out_shape=jax.ShapeDtypeStruct(out_shape, BF16),
@@ -429,7 +510,7 @@
         cost_estimate=work(
             group * 2 * both * degrees * (2 * lat_total + both), 8 * group * degrees * lat_total
         ),
-    )(place, bands, *spectra, fwd_table, inv_table, mix_t, swap)
+    )(place, *spectra, fwd_table, inv_table, mix_t, swap)
 
 
 def synthesis_kernel(*refs):
@@ -560,10 +641,9 @@
 
     mine = lax.axis_index("lon")
     sets = ord_dev // ORDER_GROUP
-    bands = lax.axis_index("lat") ^ jnp.arange(lat_count, dtype=jnp.int32)
     owned = (
-        (bands[None, :, None] * lon_count + mine) * ord_dev
-        + jnp.arange(ord_dev, dtype=jnp.int32).reshape(sets, 1, ORDER_GROUP)
+        (jnp.arange(lat_count, dtype=jnp.int32)[:, None] * lon_count + mine) * ord_dev
+        + jnp.arange(ord_dev, dtype=jnp.int32)[None, :]
     ).reshape(-1)
     point_rows = -(-lon_dev // LANES) * LANES
     at = jnp.arange(lon_count, dtype=jnp.int32)[:, None] * lon_dev + jnp.arange(
@@ -573,7 +653,7 @@
     basis_in = jnp.where(inside, basis_by_point(owned, at), 0)
     sums = jnp.sum(basis_in.astype(F32), axis=(0, 1))[:, None]
     w1 = jnp.zeros((band.shape[1], width), BF16).at[:channels].set(enc_w1.T)
-    spectra = zonal_transform(
+    first, second = zonal_transform(
         band,
         starts,
         w1,
@@ -583,7 +663,8 @@
         basis_in,
         sums,
         lat_dev,
-        sets * lat_count,
+        lat_count,
+        sets,
         channels,
     )
 
@@ -599,21 +680,21 @@
 
     mix_t = mixing_matrix(mix_weight).T
     fwd_by_lat = fwd_table.transpose(0, 2, 1)
-    modes, waiting, got = [], [], []
+    def exchange(piece):
+        return lax.all_to_all(piece, "lat", split_axis=0, concat_axis=0, tiled=True)
+
+    early = exchange(first)
+    modes, waiting = [], []
     for g in range(sets):
-        sent = spectra[g * lat_count : (g + 1) * lat_count]
-        if got:
-            sent, got[1:] = lax.optimization_barrier((list(sent), got[1:]))
-        got = [sent[0]] + [
-            lax.ppermute(sent[d], "lat", [(i, i ^ d) for i in range(lat_count)])
-            for d in range(1, lat_count)
-        ]
-        waiting.append(got)
+        piece = second[g]
+        if waiting:
+            piece, waiting[-1] = lax.optimization_barrier((piece, waiting[-1]))
+        waiting.append(exchange(piece))
     for g in range(sets):
         made = order_steps(
             place,
-            bands,
-            waiting[g],
+            [early, waiting[g]],
+            [g * 2 * ORDER_GROUP, 0],
             fwd_by_lat,
             inv_table,
             mix_t,
@@ -622,6 +703,8 @@
             halves,
         )
         made = made.reshape(lat_count * lon_count, part_lats, 2 * ORDER_GROUP, LANES)
+        if g + 1 < sets:
+            made, waiting[g + 1] = lax.optimization_barrier((made, waiting[g + 1]))
         modes.append(
             lax.all_to_all(made, ("lat", "lon"), split_axis=0, concat_axis=0, tiled=True)
         )
@@ -763,8 +846,7 @@
             and width % LANES == 0
             and lon_count % halves == 0
             and lat_dev % (lon_count // halves) == 0
-            and lat_dev % 15 == 0
-            and lat_count & (lat_count - 1) == 0
+            and lat_dev % 45 == 0
             and 4 * (NLON // lon_count) % TILE == 0
             and lat_dev // (lon_count // halves) < 64
             and ord_dev % ORDER_GROUP == 0

time: 1110 us -> 1090 us (0.982)
  blocking collectives: 0 us -> 51.1 us
  waiting for transfers between devices: 606 us -> 556 us
  Pallas kernels: 260 us -> 234 us
    ppermute x6 -> x0, waiting for transfers between devices: 126 us -> none  [listed_plan(): lax.ppermute(sent[d], 'lat', [(i, i ^ d) for i in range(lat_count)])]
    all_to_all x0 -> x2, waiting for transfers between devices: none -> 52.8 us  [exchange(): return lax.all_to_all(piece, 'lat', split_axis=0, concat_axis=0, tiled=True)]
    all_to_all x0 -> x1, blocking collectives: none -> 51.1 us  [exchange(): return lax.all_to_all(piece, 'lat', split_axis=0, concat_axis=0, tiled=True)]
    pallas_call x1 -> x2, Pallas kernels: 113 us -> 85.1 us  [the longest x1 48 us: zonal_transform(): pl.pallas_call(functools.partial(zonal_first_kernel, channels=channels, b...]
    all_to_all x2, waiting for transfers between devices: 70.6 us -> 97.5 us  [listed_plan(): lax.all_to_all(made, ('lat', 'lon'), split_axis=0, concat_axis=0, tiled=T...]
  transfers between devices with their start and end apart: 13 -> 9, of which waited for: 11 -> 9; matrix products, arithmetic and copies ran while one was open for 16% -> 17% of each run, Pallas kernels for 7% -> 7%
where the time goes in v4:
time: 1090 us; the launch traced here: 1080 us
  waiting for transfers between devices  556 us (51%)
  Pallas kernels  234 us (21%)
  matrix products  89.7 us (8%)
  other arithmetic  82.8 us (8%)
  blocking collectives  51.1 us (5%)
  starting transfers between devices  38.5 us (4%)
  local copies, waits for them, and re-layouts  17.8 us (2%)
  between operations  14 us (1%)
    all_to_all x3, waiting for transfers between devices, listed_plan(): part = lax.all_to_all(part, 'lon', split_axis=0, concat_axis=0, tiled=True)  323 us
    all_to_all x2, waiting for transfers between devices, listed_plan(): lax.all_to_all(made, ('lat', 'lon'), split_axis=0, concat_axis=0, tiled=T...  97.5 us
    dot_general x1, matrix products, encoder_by_cell(): jnp.dot(hidden, enc_w2.T, preferred_element_type=F32) + enc_b2  89.7 us
    all_gather x1, waiting for transfers between devices, listed_plan(): band = lax.all_gather(listed, 'lon', axis=0, tiled=False)  77.7 us
    pallas_call x2, Pallas kernels, order_steps(): pl.pallas_call(functools.partial(orders_kernel, group=group, pieces=piece...  72.4 us
    all_to_all x2, waiting for transfers between devices, exchange(): return lax.all_to_all(piece, 'lat', split_axis=0, concat_axis=0, tiled=True)  52.8 us
    all_to_all x1, blocking collectives, exchange(): return lax.all_to_all(piece, 'lat', split_axis=0, concat_axis=0, tiled=True)  51.1 us
    pallas_call x1, Pallas kernels, zonal_transform(): pl.pallas_call(functools.partial(zonal_first_kernel, channels=channels, b...  48 us
  transfers between devices with their start and end apart: 9, of which 9 were waited for; matrix products, arithmetic and copies ran while one was open for 17% of the time, Pallas kernels for 7%

profile of v4, /device:TPU:0, one launch (start us, length us, event | category | flops | bytes accessed | tf_op | source)
XLA Modules:
  0.0 1083.9 jit_solution(9816409139640087154)
XLA Ops:
  6.5 1.8 broadcast_in_dim.89
  8.3 7.3 all-to-all-start
  16.3 1.4 broadcast_clamp_fusion
  18.8 5.8 sort.15
  24.9 0.9 stack.39
  25.8 1.9 copy.68.cols_ref
  27.7 5.2 all-to-all-done.src_ref
  32.9 0.8 copy-done
  33.7 15.6 %shard_map.118 = bf16[80,4096]{1,0:T(8,128)(2,1)} custom-call(s32[1]{0:T(128)} %slice.51.live, bf16[8,73,512]{2,1,0:T(8,128)(2,1)} %copy-done, f32[4096,8]{1,0:T(8,128)} %copy.68.cols_ref, f32[1,4096]{1,0:T(1,128)} %bitcast.60), custom_call_target="tpu_custom_call" | custom-call | flops 8589934592 | bytes 1048576 | tf_op jit(solution)/shard_map/pallas_call | solution.py:169
  49.3 0.8 copy.70
  50.4 2.6 cosine_multiply_fusion
  55.1 0.9 broadcast_select_fusion.1.basis_ref
  56.0 77.7 %all-gather.3.cloned.1.call-done = bf16[640,4096]{1,0:T(8,128)(2,1)} async-done(((bf16[80,4096]{1,0:T(8,128)(2,1)}), bf16[640,4096]{1,0:T(8,128)(2,1)}) %all-gather.3.cloned.1.call-update) | async-done | bytes 5242896 | tf_op jit(solution)/shard_map/all_gather | solution.py:638
  133.7 0.8 slice.61
  135.1 48.0 %shard_map.119 = (bf16[4,60,32,256]{3,2,1,0:T(8,128)(2,1)}, bf16[32816,256]{1,0:T(8,128)(2,1)}, bf16[32816,128]{1,0:T(8,128)(2,1)}, f32[128,256]{1,0:T(8,128)}) custom-call(s32[8,181]{1,0:T(8,128)} %fusion.44.starts, bf16[8,80,4096]{2,1,0:T(8,128)(2,1)} %bitcast.62, bf16[80,256]{1,0:T(8,128)(2,1)} %scatter.9.w1_ref, f32[1,256]{1,0:T(1,128)} %bitcast.63, ...), custom_call_target="tpu_custom_call" | custom-call | flops 53687091200 | bytes 33554432 | tf_op jit(solution)/shard_map/pallas_call | solution.py:363
  183.1 37.1 %shard_map.120 = (bf16[4,120,16,256]{3,2,1,0:T(8,128)(2,1)}, bf16[4,120,16,256]{3,2,1,0:T(8,128)(2,1)}) custom-call(s32[8,181]{1,0:T(8,128)} %fusion.44.starts, bf16[32816,256]{1,0:T(8,128)(2,1)} %get-tuple-element.45.delta, bf16[32816,128]{1,0:T(8,128)(2,1)} %get-tuple-element.46.hots, f32[128,256]{1,0:T(8,128)} %get-tuple-element.47.base), custom_call_target="tpu_custom_call" | custom-call | flops 53687091200 | bytes 33554432 | tf_op jit(solution)/shard_map/pallas_call | solution.py:389
  220.2 51.1 %all_to_all.45.refs_1_ = bf16[4,120,16,256]{3,2,1,0:T(8,128)(2,1)} all-to-all(bf16[4,120,16,256]{3,2,1,0:T(8,128)(2,1)} %get-tuple-element.49), channel_id=1, replica_groups=mesh['lat'=4,'lon'=8] {'lat'}, dimensions={0} | all-to-all | bytes 7864320 | tf_op jit(solution)/shard_map/all_to_all | solution.py:684
  271.3 4.8 all-to-all-start.1
  276.1 45.4 %all-to-all-done.1.refs_0_ = bf16[4,60,32,256]{3,2,1,0:T(8,128)(2,1)} async-done(((bf16[4,60,32,256]{3,2,1,0:T(8,128)(2,1)}), bf16[4,60,32,256]{3,2,1,0:T(8,128)(2,1)}, u32[]{:S(2)}, u32[]{:S(2)}) %all-to-all-start.1) | async-done | bytes 3932192 | tf_op jit(solution)/shard_map/all_to_all | solution.py:684
  321.5 5.1 all-to-all-start.3
  326.9 0.8 maximum_bitcast_fusion.refs_4_
  327.8 0.7 fusion.35.refs_5_
  328.5 36.2 %shard_map.121 = bf16[16,2,45,16,128]{4,3,2,1,0:T(8,128)(2,1)} custom-call(s32[720]{0:T(1024)} %constant.252.clone.place, bf16[4,60,32,256]{3,2,1,0:T(8,128)(2,1)} %all-to-all-done.1.refs_0_, bf16[4,120,16,256]{3,2,1,0:T(8,128)(2,1)} %all_to_all.45.refs_1_, bf16[16,720,512]{2,1,0:T(8,128)(2,1)} %bitcast.40, bf16[16,720,512]{2,1,0:T(8,128)(2,1)} %refs_3_.3, ...), custom_call_target="tpu_custom_call" | custom-call | flops 8187281408 | bytes 23592960 | tf_op jit(solution)/shard_map/pallas_call | solution.py:488
  364.7 7.3 all-to-all-done.3.refs_1_
  372.1 36.2 %shard_map.122 = bf16[16,2,45,16,128]{4,3,2,1,0:T(8,128)(2,1)} custom-call(s32[720]{0:T(1024)} %constant.252.clone.place, bf16[4,60,32,256]{3,2,1,0:T(8,128)(2,1)} %all-to-all-done.1.refs_0_, bf16[4,120,16,256]{3,2,1,0:T(8,128)(2,1)} %all-to-all-done.3.refs_1_, bf16[16,720,512]{2,1,0:T(8,128)(2,1)} %bitcast.41, bf16[16,720,512]{2,1,0:T(8,128)(2,1)} %refs_3_.3, ...), custom_call_target="tpu_custom_call" | custom-call | flops 8187281408 | bytes 23592960 | tf_op jit(solution)/shard_map/pallas_call | solution.py:488
  408.3 3.6 all-to-all-start.5
  412.1 19.5 %multiply_convert_fusion.1 = (bf16[8,192,512,1]{1,0,3,2:T(8,128)(2,1)S(1)}, bf16[8,192,512,1]{1,0,3,2:T(8,128)(2,1)S(1)}) fusion(s32[512]{0:T(512)S(1)} %reshape.372, s32[8,192]{1,0:T(8,128)S(1)} %iota_add_fusion), kind=kLoop, calls=%fused_computation.32 | loop fusion | flops 10223616 | bytes 3153920 | tf_op jit(solution)/shard_map/convert
  431.6 2.6 pad_maximum_fusion
  434.2 5.7 copy.77
  440.0 2.0 broadcast_select_fusion.refs_2_
  442.0 1.6 copy.78
  443.7 44.5 %scatter_custom_fusion = f32[32400,73]{1,0:T(8,128)} fusion(s32[4096]{0:T(1024)} %get-tuple-element.73, f32[]{:T(128)} %constant.199.clone.1, f32[4096]{0:T(1024)S(1)} %copy-done.2, pred[4096]{0:T(1024)(128)(4,1)S(1)} %compare_and_fusion, bf16[]{:T(256)} %constant.222.clone.1, bf16[4096,73]{1,0:T(8,128)(2,1)S(1)} %bitcast.45, s32[4096]{0:T(1024)S(1)} %copy-done.7), kind=kCustom, calls=%fused_computation.25 | custom fusion | flops 1196032 | bytes 10096704 | tf_op jit(solution)/shard_map/scatter-add | solution.py:52
  488.1 55.5 %all-to-all-done.5.refs_1_ = bf16[32,45,16,128]{3,2,1,0:T(8,128)(2,1)} async-done(((bf16[32,45,16,128]{3,2,1,0:T(8,128)(2,1)}), bf16[32,45,16,128]{3,2,1,0:T(8,128)(2,1)}, u32[]{:S(2)}, u32[]{:S(2)}) %all-to-all-start.5) | async-done | bytes 5898272 | tf_op jit(solution)/shard_map/all_to_all | solution.py:709
  543.6 3.6 all-to-all-start.4
  547.3 89.7 %fusion.enc_ref = bf16[32400,256]{1,0:T(8,128)(2,1)} fusion(bf16[256,256]{1,0:T(8,128)(2,1)S(1)} %copy-done.6, f32[256]{0:T(256)S(1)} %copy-done.12, bf16[256,73]{0,1:T(8,128)(2,1)S(1)} %copy-done.10, f32[256]{0:T(256)S(1)} %copy-done.11, f32[32400,73]{1,0:T(8,128)} %scatter_custom_fusion), kind=kOutput, calls=%fused_computation.5 | convolution fusion | flops 6024099840 | bytes 26220096 | tf_op jit(solution)/shard_map/dot_general | solution.py:90
  636.9 42.0 %all-to-all-done.4.refs_0_ = bf16[32,45,16,128]{3,2,1,0:T(8,128)(2,1)} async-done(((bf16[32,45,16,128]{3,2,1,0:T(8,128)(2,1)}), bf16[32,45,16,128]{3,2,1,0:T(8,128)(2,1)}, u32[]{:S(2)}, u32[]{:S(2)}) %all-to-all-start.4) | async-done | bytes 5898272 | tf_op jit(solution)/shard_map/all_to_all | solution.py:709
  678.9 13.9 %shard_map.124 = bf16[8,2880,128]{2,1,0:T(8,128)(2,1)} custom-call(bf16[32,45,16,128]{3,2,1,0:T(8,128)(2,1)} %all-to-all-done.4.refs_0_, bf16[32,45,16,128]{3,2,1,0:T(8,128)(2,1)} %all-to-all-done.5.refs_1_, bf16[8,192,1024]{2,1,0:T(8,128)(2,1)} %broadcast_select_fusion.refs_2_), custom_call_target="tpu_custom_call" | custom-call | flops 6442450944 | bytes 11796480 | tf_op jit(solution)/shard_map/pallas_call | solution.py:548
  692.9 4.7 all-to-all-start.7
  697.6 13.9 %shard_map.125 = bf16[8,2880,128]{2,1,0:T(8,128)(2,1)} custom-call(bf16[32,45,16,128]{3,2,1,0:T(8,128)(2,1)} %all-to-all-done.4.refs_0_, bf16[32,45,16,128]{3,2,1,0:T(8,128)(2,1)} %all-to-all-done.5.refs_1_, bf16[8,192,1024]{2,1,0:T(8,128)(2,1)} %broadcast_select_fusion.refs_2_), custom_call_target="tpu_custom_call" | custom-call | flops 6442450944 | bytes 11796480 | tf_op jit(solution)/shard_map/pallas_call | solution.py:548
  711.5 115.8 %all-to-all-done.7 = bf16[8,2880,128]{2,1,0:T(8,128)(2,1)} async-done(((bf16[8,2880,128]{2,1,0:T(8,128)(2,1)}), bf16[8,2880,128]{2,1,0:T(8,128)(2,1)}, u32[]{:S(2)}, u32[]{:S(2)}) %all-to-all-start.7) | async-done | bytes 5898272 | tf_op jit(solution)/shard_map/all_to_all | solution.py:736
  827.4 4.7 all-to-all-start.8
  832.1 13.6 %shard_map.123 = bf16[8,2340,128]{2,1,0:T(8,128)(2,1)} custom-call(bf16[32,45,16,128]{3,2,1,0:T(8,128)(2,1)} %all-to-all-done.4.refs_0_, bf16[32,45,16,128]{3,2,1,0:T(8,128)(2,1)} %all-to-all-done.5.refs_1_, bf16[8,192,1024]{2,1,0:T(8,128)(2,1)} %broadcast_select_fusion.refs_2_), custom_call_target="tpu_custom_call" | custom-call | flops 5234491392 | bytes 9584640 | tf_op jit(solution)/shard_map/pallas_call | solution.py:548
  845.7 115.3 %all-to-all-done.8 = bf16[8,2880,128]{2,1,0:T(8,128)(2,1)} async-done(((bf16[8,2880,128]{2,1,0:T(8,128)(2,1)}), bf16[8,2880,128]{2,1,0:T(8,128)(2,1)}, u32[]{:S(2)}, u32[]{:S(2)}) %all-to-all-start.8) | async-done | bytes 5898272 | tf_op jit(solution)/shard_map/all_to_all | solution.py:736
  961.0 4.6 all-to-all-start.6
  965.6 6.8 shard_map.126.enc_ref
  972.5 6.8 shard_map.127.enc_ref
  979.3 91.8 %all-to-all-done.6 = bf16[8,2340,128]{2,1,0:T(8,128)(2,1)} async-done(((bf16[8,2340,128]{2,1,0:T(8,128)(2,1)}), bf16[8,2340,128]{2,1,0:T(8,128)(2,1)}, u32[]{:S(2)}, u32[]{:S(2)}) %all-to-all-start.6) | async-done | bytes 4792352 | tf_op jit(solution)/shard_map/all_to_all | solution.py:736
  1071.1 5.7 shard_map.128
  (62 shorter events, 5.4 us)
Async XLA Ops:
  8.3 24.5 %all-to-all-start = ((bf16[8,73,512]{2,1,0:T(8,128)(2,1)}), bf16[8,73,512]{2,1,0:T(8,128)(2,1)S(1)}, u32[]{:S(2)}, u32[]{:S(2)}) async-start(bf16[8,73,512]{2,1,0:T(8,128)(2,1)} %broadcast_in_dim.89), calls=%async_computation | async-start | bytes 1310720 | tf_op jit(solution)/shard_map/all_to_all | solution.py:634
  15.6 118.1 %all-gather.3.cloned.1.call-start = ((), (), s32[]{:S(2)}) async-start(), calls=%async_computation.9 | async-start | bytes 5898240 | tf_op jit(solution)/shard_map/all_gather | solution.py:638
  15.7 0.6 copy-start.3
  25.8 23.6 %copy-start.5 = (bf16[256,256]{1,0:T(8,128)(2,1)S(1)}, bf16[256,256]{1,0:T(8,128)(2,1)}, u32[]{:S(2)}) copy-start(bf16[256,256]{1,0:T(8,128)(2,1)} %param.22) | copy-start | bytes 393220
  32.9 0.8 copy-start
  33.7 20.7 %copy-start.9 = (bf16[256,73]{0,1:T(8,128)(2,1)S(1)}, bf16[256,73]{0,1:T(8,128)(2,1)}, u32[]{:S(2)}) copy-start(bf16[256,73]{0,1:T(8,128)(2,1)} %param.20) | copy-start | bytes 112132
  220.2 106.4 %copy-start.1 = (bf16[2,256,256]{2,1,0:T(8,128)(2,1)S(1)}, bf16[2,256,256]{2,1,0:T(8,128)(2,1)}, u32[]{:S(2)}) copy-start(bf16[2,256,256]{2,1,0:T(8,128)(2,1)} %param.24) | copy-start | bytes 786436
  271.3 50.2 %all-to-all-start.1 = ((bf16[4,60,32,256]{3,2,1,0:T(8,128)(2,1)}), bf16[4,60,32,256]{3,2,1,0:T(8,128)(2,1)}, u32[]{:S(2)}, u32[]{:S(2)}) async-start(bf16[4,60,32,256]{3,2,1,0:T(8,128)(2,1)} %get-tuple-element.44), calls=%async_computation.1 | async-start | bytes 7864320 | tf_op jit(solution)/shard_map/all_to_all | solution.py:684
  321.5 50.5 %all-to-all-start.3 = ((bf16[4,120,16,256]{3,2,1,0:T(8,128)(2,1)}), bf16[4,120,16,256]{3,2,1,0:T(8,128)(2,1)}, u32[]{:S(2)}, u32[]{:S(2)}) async-start(bf16[4,120,16,256]{3,2,1,0:T(8,128)(2,1)} %get-tuple-element.51), calls=%async_computation.3 | async-start | bytes 7864320 | tf_op jit(solution)/shard_map/all_to_all | solution.py:684
  408.3 31.7 %copy-start.4 = (s32[1,4,8,128]{3,1,2,0:T(4,128)S(1)}, s32[1,4,8,128]{3,1,2,0:T(4,128)}, u32[]{:S(2)}) copy-start(s32[1,4,8,128]{3,1,2,0:T(4,128)} %copy-done.3) | copy-start | bytes 49156
  408.3 31.7 %copy-start.8 = (s32[4096]{0:T(1024)S(1)}, s32[4096]{0:T(1024)}, u32[]{:S(2)}) copy-start(s32[4096]{0:T(1024)} %param.17) | copy-start | bytes 49156
  408.3 135.3 %all-to-all-start.5 = ((bf16[32,45,16,128]{3,2,1,0:T(8,128)(2,1)}), bf16[32,45,16,128]{3,2,1,0:T(8,128)(2,1)}, u32[]{:S(2)}, u32[]{:S(2)}) async-start(bf16[32,45,16,128]{3,2,1,0:T(8,128)(2,1)} %bitcast.43), calls=%async_computation.5 | async-start | bytes 11796480 | tf_op jit(solution)/shard_map/all_to_all | solution.py:709
  411.9 31.7 %copy-start.2 = (f32[4096]{0:T(1024)S(1)}, f32[4096]{0:T(1024)}, u32[]{:S(2)}) copy-start(f32[4096]{0:T(1024)} %param.19) | copy-start | bytes 49156
  412.0 31.7 %copy-start.7 = (s32[4096]{0:T(1024)S(1)}, s32[4096]{0:T(1024)}, u32[]{:S(2)}) copy-start(s32[4096]{0:T(1024)} %get-tuple-element.62) | copy-start | bytes 49156
  442.0 105.2 %copy-start.6 = (bf16[256,256]{1,0:T(8,128)(2,1)S(1)}, bf16[256,256]{1,0:T(8,128)(2,1)}, u32[]{:S(2)}) copy-start(bf16[256,256]{1,0:T(8,128)(2,1)} %param.22) | copy-start | bytes 393220
  442.0 105.2 %copy-start.10 = (bf16[256,73]{0,1:T(8,128)(2,1)S(1)}, bf16[256,73]{0,1:T(8,128)(2,1)}, u32[]{:S(2)}) copy-start(bf16[256,73]{0,1:T(8,128)(2,1)} %param.20) | copy-start | bytes 112132
  442.0 105.2 %copy-start.11 = (f32[256]{0:T(256)S(1)}, f32[256]{0:T(256)}, u32[]{:S(2)}) copy-start(f32[256]{0:T(256)} %param.21) | copy-start | bytes 3076
  442.0 105.3 %copy-start.12 = (f32[256]{0:T(256)S(1)}, f32[256]{0:T(256)}, u32[]{:S(2)}) copy-start(f32[256]{0:T(256)} %param.23) | copy-start | bytes 3076
  543.6 135.3 %all-to-all-start.4 = ((bf16[32,45,16,128]{3,2,1,0:T(8,128)(2,1)}), bf16[32,45,16,128]{3,2,1,0:T(8,128)(2,1)}, u32[]{:S(2)}, u32[]{:S(2)}) async-start(bf16[32,45,16,128]{3,2,1,0:T(8,128)(2,1)} %bitcast.42), calls=%async_computation.4 | async-start | bytes 11796480 | tf_op jit(solution)/shard_map/all_to_all | solution.py:709
  692.9 134.5 %all-to-all-start.7 = ((bf16[8,2880,128]{2,1,0:T(8,128)(2,1)}), bf16[8,2880,128]{2,1,0:T(8,128)(2,1)}, u32[]{:S(2)}, u32[]{:S(2)}) async-start(bf16[8,2880,128]{2,1,0:T(8,128)(2,1)} %shard_map.124), calls=%async_computation.7 | async-start | bytes 11796480 | tf_op jit(solution)/shard_map/all_to_all | solution.py:736
  827.4 133.6 %all-to-all-start.8 = ((bf16[8,2880,128]{2,1,0:T(8,128)(2,1)}), bf16[8,2880,128]{2,1,0:T(8,128)(2,1)}, u32[]{:S(2)}, u32[]{:S(2)}) async-start(bf16[8,2880,128]{2,1,0:T(8,128)(2,1)} %shard_map.125), calls=%async_computation.8 | async-start | bytes 11796480 | tf_op jit(solution)/shard_map/all_to_all | solution.py:736
  961.0 110.1 %all-to-all-start.6 = ((bf16[8,2340,128]{2,1,0:T(8,128)(2,1)}), bf16[8,2340,128]{2,1,0:T(8,128)(2,1)}, u32[]{:S(2)}, u32[]{:S(2)}) async-start(bf16[8,2340,128]{2,1,0:T(8,128)(2,1)} %shard_map.123), calls=%async_computation.6 | async-start | bytes 9601024 | tf_op jit(solution)/shard_map/all_to_all | solution.py:736
Sparse Core Ops, SparseCore 0:
  49.5 84.2 all-gather.2

commit v5 on v4

--- a/solution.py
+++ b/solution.py
@@ -16,7 +16,7 @@
 WINDOW = 48
 UNROLL = 3
 LATS = 8
-CHUNK_RUNS = 2
+CHUNK_CUTS = (1, 4)
 ORDER_GROUP = 8
 VMEM_BYTES = 60 * 1024 * 1024
 
@@ -636,6 +636,15 @@
         source_all, recv_src, recv_cell, recv_weight, lat_dev, lon_dev, slot_count
     )
     band = lax.all_gather(listed, "lon", axis=0, tiled=False)
+    pad_points = -(-lon_dev // TILE) * TILE
+    at = jnp.arange(lon_count, dtype=jnp.int32)[:, None] * lon_dev + jnp.arange(
+        pad_points, dtype=jnp.int32
+    )
+    inside = (jnp.arange(pad_points) < lon_dev)[None, :, None]
+    listing = jnp.arange(ORDERS, dtype=jnp.int32).reshape(-1, ord_dev // ORDER_GROUP, ORDER_GROUP)
+    basis_out = basis_by_point(listing.transpose(1, 0, 2).reshape(-1), at)
+    basis_out = jnp.where(inside, basis_out, 0)
+    band, basis_out = lax.optimization_barrier((band, basis_out))
     coded = band[:, channels + 2 : channels + 4, : lat_dev + 1].astype(jnp.int32)
     starts = coded[:, 0] * 128 + coded[:, 1]
 
@@ -689,6 +698,8 @@
         piece = second[g]
         if waiting:
             piece, waiting[-1] = lax.optimization_barrier((piece, waiting[-1]))
+        else:
+            piece, early = lax.optimization_barrier((piece, early))
         waiting.append(exchange(piece))
     for g in range(sets):
         made = order_steps(
@@ -709,15 +720,6 @@
             lax.all_to_all(made, ("lat", "lon"), split_axis=0, concat_axis=0, tiled=True)
         )
 
-    pad_points = -(-lon_dev // TILE) * TILE
-    at = jnp.arange(lon_count, dtype=jnp.int32)[:, None] * lon_dev + jnp.arange(
-        pad_points, dtype=jnp.int32
-    )
-    inside = (jnp.arange(pad_points) < lon_dev)[None, :, None]
-    listing = jnp.arange(ORDERS, dtype=jnp.int32).reshape(-1, sets, ORDER_GROUP)
-    basis_out = basis_by_point(listing.transpose(1, 0, 2).reshape(-1), at)
-    basis_out = jnp.where(inside, basis_out, 0)
-
     piece = source_all.transpose(1, 0, 2).reshape(channels, -1)
     regridded = regrid_all(
         piece,
@@ -726,13 +728,16 @@
         recv_weight.reshape(lon_count, slot_count),
         cells_dev,
     )
-    encoded = encoder_by_cell(regridded, enc_w1, enc_b1, enc_w2, enc_b2)
-    modes[-1], encoded = lax.optimization_barrier((modes[-1], encoded))
-    running = encoded
-    step = CHUNK_RUNS * LATS
-    for first in range(0, part_lats, step):
-        count = min(step, part_lats - first)
-        part = synthesis_steps(modes, basis_out, lon_dev, LATS, first, count)
+    modes[-1], regridded = lax.optimization_barrier((modes[-1], regridded))
+    running = encoder_by_cell(regridded, enc_w1, enc_b1, enc_w2, enc_b2)
+    cuts = [0] + [c * LATS for c in CHUNK_CUTS if c * LATS < part_lats] + [part_lats]
+    parts = []
+    for first, last in zip(cuts[:-1], cuts[1:]):
+        parts.append(synthesis_steps(modes, basis_out, lon_dev, LATS, first, last - first))
+    if len(parts) > 1:
+        parts[1], running = lax.optimization_barrier((parts[1], running))
+    for first, last, part in zip(cuts[:-1], cuts[1:], parts):
+        count = last - first
         part = lax.all_to_all(part, "lon", split_axis=0, concat_axis=0, tiled=True)
         part = part.reshape(quarters, halves, count * lon_dev, LANES)
         running = finish_steps(part, running, LATS, lon_dev, first // LATS, whole_groups, rest)

time: 1090 us -> 1090 us (level)
  waiting for transfers between devices: 556 us -> 413 us
  blocking collectives: 51.1 us -> 186 us
    all_to_all x0 -> x1, blocking collectives: none -> 135 us  [listed_plan(): lax.all_to_all(made, ('lat', 'lon'), split_axis=0, concat_axis=0, tiled=T...]
    all_to_all x3, waiting for transfers between devices: 323 us -> 268 us  [listed_plan(): part = lax.all_to_all(part, 'lon', split_axis=0, concat_axis=0, tiled=True)]
    all_to_all x2, waiting for transfers between devices: 52.8 us -> 15.4 us  [exchange(): return lax.all_to_all(piece, 'lat', split_axis=0, concat_axis=0, tiled=True)]
    all_gather x1, waiting for transfers between devices: 77.7 us -> 46.7 us  [listed_plan(): band = lax.all_gather(listed, 'lon', axis=0, tiled=False)]
    all_to_all x2 -> x1, waiting for transfers between devices: 97.5 us -> 77.2 us  [listed_plan(): lax.all_to_all(made, ('lat', 'lon'), split_axis=0, concat_axis=0, tiled=T...]
  transfers between devices with their start and end apart: 9 -> 8, of which waited for: 9 -> 7; matrix products, arithmetic and copies ran while one was open for 17% -> 17% of each run, Pallas kernels for 7% -> 11%
where the time goes in v5:
time: 1090 us; the launch traced here: 1080 us
  waiting for transfers between devices  413 us (38%)
  Pallas kernels  237 us (22%)
  blocking collectives  186 us (17%)
  other arithmetic  93.2 us (9%)
  matrix products  81 us (7%)
  starting transfers between devices  35.9 us (3%)
  local copies, waits for them, and re-layouts  22.2 us (2%)
  between operations  14 us (1%)
    all_to_all x3, waiting for transfers between devices, listed_plan(): part = lax.all_to_all(part, 'lon', split_axis=0, concat_axis=0, tiled=True)  268 us
    all_to_all x1, blocking collectives, listed_plan(): lax.all_to_all(made, ('lat', 'lon'), split_axis=0, concat_axis=0, tiled=T...  135 us
    dot_general x1, matrix products, encoder_by_cell(): jnp.dot(hidden, enc_w2.T, preferred_element_type=F32) + enc_b2  81 us
    all_to_all x1, waiting for transfers between devices, listed_plan(): lax.all_to_all(made, ('lat', 'lon'), split_axis=0, concat_axis=0, tiled=T...  77.2 us
    pallas_call x2, Pallas kernels, order_steps(): pl.pallas_call(functools.partial(orders_kernel, group=group, pieces=piece...  72.4 us
    all_to_all x1, blocking collectives, exchange(): return lax.all_to_all(piece, 'lat', split_axis=0, concat_axis=0, tiled=True)  50.9 us
    pallas_call x1, Pallas kernels, zonal_transform(): pl.pallas_call(functools.partial(zonal_first_kernel, channels=channels, b...  49.3 us
    all_gather x1, waiting for transfers between devices, listed_plan(): band = lax.all_gather(listed, 'lon', axis=0, tiled=False)  46.7 us
  transfers between devices with their start and end apart: 8, of which 7 were waited for; matrix products, arithmetic and copies ran while one was open for 17% of the time, Pallas kernels for 11%

profile of v5, /device:TPU:0, one launch (start us, length us, event | category | flops | bytes accessed | tf_op | source)
XLA Modules:
  0.0 1082.4 jit_solution(3052891906894106038)
XLA Ops:
  6.5 1.8 broadcast_in_dim.89
  8.3 7.3 all-to-all-start
  16.3 1.4 broadcast_clamp_fusion
  18.8 5.8 sort.15
  24.9 0.9 stack.39
  25.8 1.9 copy.68.cols_ref
  27.7 5.2 all-to-all-done.src_ref
  32.9 0.8 copy-done
  33.7 15.0 %shard_map.118 = bf16[80,4096]{1,0:T(8,128)(2,1)} custom-call(s32[1]{0:T(128)} %slice.51.live, bf16[8,73,512]{2,1,0:T(8,128)(2,1)} %copy-done, f32[4096,8]{1,0:T(8,128)} %copy.68.cols_ref, f32[1,4096]{1,0:T(1,128)} %bitcast.65), custom_call_target="tpu_custom_call" | custom-call | flops 8589934592 | bytes 1048576 | tf_op jit(solution)/shard_map/pallas_call | solution.py:169
  49.1 0.8 copy.71
  49.9 2.6 cosine_multiply_fusion
  52.9 1.2 copy.72
  54.1 0.7 broadcast_in_dim.105.sums_ref
  54.8 19.5 %multiply_convert_fusion.1 = (bf16[8,192,512,1]{1,0,3,2:T(8,128)(2,1)S(1)}, bf16[8,192,512,1]{1,0,3,2:T(8,128)(2,1)S(1)}) fusion(s32[512]{0:T(512)S(1)} %reshape.369, s32[8,192]{1,0:T(8,128)S(1)} %iota_add_fusion.1), kind=kLoop, calls=%fused_computation.31 | loop fusion | flops 10223616 | bytes 3153920 | tf_op jit(solution)/shard_map/convert
  74.3 2.7 pad_maximum_fusion
  77.0 5.7 copy.69
  83.3 1.9 broadcast_select_fusion.1.basis_ref
  85.3 2.0 broadcast_select_fusion.refs_2_
  87.3 46.7 %all-gather.3.cloned.1.call-done = bf16[640,4096]{1,0:T(8,128)(2,1)} async-done(((bf16[80,4096]{1,0:T(8,128)(2,1)}), bf16[640,4096]{1,0:T(8,128)(2,1)}) %all-gather.3.cloned.1.call-update) | async-done | bytes 5242896 | tf_op jit(solution)/shard_map/all_gather | solution.py:638
  133.9 5.4 copy.70
  139.9 49.3 %shard_map.119 = (bf16[4,60,32,256]{3,2,1,0:T(8,128)(2,1)}, bf16[32816,256]{1,0:T(8,128)(2,1)}, bf16[32816,128]{1,0:T(8,128)(2,1)}, f32[128,256]{1,0:T(8,128)}) custom-call(s32[8,181]{1,0:T(8,128)} %fusion.39.starts, bf16[8,80,4096]{2,1,0:T(8,128)(2,1)} %bitcast.49, bf16[80,256]{1,0:T(8,128)(2,1)} %scatter.9.w1_ref, f32[1,256]{1,0:T(1,128)} %bitcast.66, ...), custom_call_target="tpu_custom_call" | custom-call | flops 53687091200 | bytes 33554432 | tf_op jit(solution)/shard_map/pallas_call | solution.py:363
  189.2 5.2 all-to-all-start.1
  194.5 37.3 %shard_map.120 = (bf16[4,120,16,256]{3,2,1,0:T(8,128)(2,1)}, bf16[4,120,16,256]{3,2,1,0:T(8,128)(2,1)}) custom-call(s32[8,181]{1,0:T(8,128)} %fusion.39.starts, bf16[32816,256]{1,0:T(8,128)(2,1)} %get-tuple-element.51.delta, bf16[32816,128]{1,0:T(8,128)(2,1)} %get-tuple-element.52.hots, f32[128,256]{1,0:T(8,128)} %get-tuple-element.53.base), custom_call_target="tpu_custom_call" | custom-call | flops 53687091200 | bytes 33554432 | tf_op jit(solution)/shard_map/pallas_call | solution.py:389
  231.8 8.1 all-to-all-done.1.refs_0_
  239.9 50.9 %all_to_all.45.refs_1_ = bf16[4,120,16,256]{3,2,1,0:T(8,128)(2,1)} all-to-all(bf16[4,120,16,256]{3,2,1,0:T(8,128)(2,1)} %get-tuple-element.58), channel_id=1, replica_groups=mesh['lat'=4,'lon'=8] {'lat'}, dimensions={0} | all-to-all | bytes 7864320 | tf_op jit(solution)/shard_map/all_to_all | solution.py:693
  290.8 4.8 all-to-all-start.3
  295.9 0.9 maximum_bitcast_fusion.refs_4_
  296.8 0.7 fusion.30.refs_5_
  297.5 36.2 %shard_map.121 = bf16[16,2,45,16,128]{4,3,2,1,0:T(8,128)(2,1)} custom-call(s32[720]{0:T(1024)} %constant.252.clone.place, bf16[4,60,32,256]{3,2,1,0:T(8,128)(2,1)} %all-to-all-done.1.refs_0_, bf16[4,120,16,256]{3,2,1,0:T(8,128)(2,1)} %all_to_all.45.refs_1_, bf16[16,720,512]{2,1,0:T(8,128)(2,1)} %bitcast.43, bf16[16,720,512]{2,1,0:T(8,128)(2,1)} %refs_3_.3, ...), custom_call_target="tpu_custom_call" | custom-call | flops 8187281408 | bytes 23592960 | tf_op jit(solution)/shard_map/pallas_call | solution.py:488
  333.7 7.3 all-to-all-done.3.refs_1_
  341.1 36.2 %shard_map.122 = bf16[16,2,45,16,128]{4,3,2,1,0:T(8,128)(2,1)} custom-call(s32[720]{0:T(1024)} %constant.252.clone.place, bf16[4,60,32,256]{3,2,1,0:T(8,128)(2,1)} %all-to-all-done.1.refs_0_, bf16[4,120,16,256]{3,2,1,0:T(8,128)(2,1)} %all-to-all-done.3.refs_1_, bf16[16,720,512]{2,1,0:T(8,128)(2,1)} %bitcast.44, bf16[16,720,512]{2,1,0:T(8,128)(2,1)} %refs_3_.3, ...), custom_call_target="tpu_custom_call" | custom-call | flops 8187281408 | bytes 23592960 | tf_op jit(solution)/shard_map/pallas_call | solution.py:488
  377.3 135.3 %all_to_all.46.refs_1_ = bf16[32,45,16,128]{3,2,1,0:T(8,128)(2,1)} all-to-all(bf16[32,45,16,128]{3,2,1,0:T(8,128)(2,1)} %bitcast.46), channel_id=1, replica_groups=mesh['lat'=4,'lon'=8] {'lat','lon'}, dimensions={0} | all-to-all | bytes 11796480 | tf_op jit(solution)/shard_map/all_to_all | solution.py:720
  512.6 3.6 all-to-all-start.4
  517.0 44.9 %scatter_custom_fusion = f32[32400,73]{1,0:T(8,128)} fusion(s32[4096]{0:T(1024)} %get-tuple-element.85, f32[]{:T(128)} %constant.199.clone.1, f32[4096]{0:T(1024)S(1)} %copy-done.3, pred[4096]{0:T(1024)(128)(4,1)S(1)} %compare_and_fusion, bf16[]{:T(256)} %constant.222.clone.1, bf16[4096,73]{1,0:T(8,128)(2,1)S(1)} %bitcast.50, s32[4096]{0:T(1024)S(1)} %copy-done.8), kind=kCustom, calls=%fused_computation.24 | custom fusion | flops 1196032 | bytes 10096704 | tf_op jit(solution)/shard_map/scatter-add | solution.py:52
  561.9 8.8 convert_element_type.121
  570.7 77.2 %all-to-all-done.4.refs_0_ = bf16[32,45,16,128]{3,2,1,0:T(8,128)(2,1)} async-done(((bf16[32,45,16,128]{3,2,1,0:T(8,128)(2,1)}), bf16[32,45,16,128]{3,2,1,0:T(8,128)(2,1)}, u32[]{:S(2)}, u32[]{:S(2)}) %all-to-all-start.4) | async-done | bytes 5898272 | tf_op jit(solution)/shard_map/all_to_all | solution.py:720
  647.9 9.0 shard_map.125
  656.9 4.4 all-to-all-start.8
  661.3 81.0 %fusion.enc_ref = bf16[32400,256]{1,0:T(8,128)(2,1)} fusion(bf16[256,256]{1,0:T(8,128)(2,1)S(1)} %copy-done.7, f32[256]{0:T(256)S(1)} %copy-done.13, bf16[32400,73]{1,0:T(8,128)(2,1)} %convert_element_type.121, bf16[256,73]{0,1:T(8,128)(2,1)S(1)} %copy-done.11, f32[256]{0:T(256)S(1)} %copy-done.12), kind=kOutput, calls=%fused_computation.5 | convolution fusion | flops 6021734400 | bytes 21489696 | tf_op jit(solution)/shard_map/dot_general | solution.py:90
  742.4 18.9 %shard_map.124 = bf16[8,4320,128]{2,1,0:T(8,128)(2,1)} custom-call(bf16[32,45,16,128]{3,2,1,0:T(8,128)(2,1)} %all-to-all-done.4.refs_0_, bf16[32,45,16,128]{3,2,1,0:T(8,128)(2,1)} %all_to_all.46.refs_1_, bf16[8,192,1024]{2,1,0:T(8,128)(2,1)} %broadcast_select_fusion.refs_2_), custom_call_target="tpu_custom_call" | custom-call | flops 9663676416 | bytes 17694720 | tf_op jit(solution)/shard_map/pallas_call | solution.py:548
  761.2 5.9 all-to-all-start.7
  767.1 13.6 %shard_map.123 = bf16[8,2340,128]{2,1,0:T(8,128)(2,1)} custom-call(bf16[32,45,16,128]{3,2,1,0:T(8,128)(2,1)} %all-to-all-done.4.refs_0_, bf16[32,45,16,128]{3,2,1,0:T(8,128)(2,1)} %all_to_all.46.refs_1_, bf16[8,192,1024]{2,1,0:T(8,128)(2,1)} %broadcast_select_fusion.refs_2_), custom_call_target="tpu_custom_call" | custom-call | flops 5234491392 | bytes 9584640 | tf_op jit(solution)/shard_map/pallas_call | solution.py:548
  780.7 179.0 %all-to-all-done.7 = bf16[8,4320,128]{2,1,0:T(8,128)(2,1)} async-done(((bf16[8,4320,128]{2,1,0:T(8,128)(2,1)}), bf16[8,4320,128]{2,1,0:T(8,128)(2,1)}, u32[]{:S(2)}, u32[]{:S(2)}) %all-to-all-start.7) | async-done | bytes 8847392 | tf_op jit(solution)/shard_map/all_to_all | solution.py:741
  959.7 4.6 all-to-all-start.6
  964.3 5.1 shard_map.126.enc_ref
  969.4 10.9 %shard_map.127.enc_ref = bf16[32400,256]{1,0:T(8,128)(2,1)} custom-call(bf16[4,2,4320,128]{3,2,1,0:T(8,128)(2,1)} %bitcast.25.part_ref, bf16[32400,256]{1,0:T(8,128)(2,1)} %shard_map.126.enc_ref), custom_call_target="tpu_custom_call", output_to_operand_aliasing={{}: (1, {})} | custom-call | flops 17694720 | bytes 26542080 | tf_op jit(solution)/shard_map/pallas_call | solution.py:589
  980.3 89.4 %all-to-all-done.6 = bf16[8,2340,128]{2,1,0:T(8,128)(2,1)} async-done(((bf16[8,2340,128]{2,1,0:T(8,128)(2,1)}), bf16[8,2340,128]{2,1,0:T(8,128)(2,1)}, u32[]{:S(2)}, u32[]{:S(2)}) %all-to-all-start.6) | async-done | bytes 4792352 | tf_op jit(solution)/shard_map/all_to_all | solution.py:741
  1069.7 5.7 shard_map.128
  (64 shorter events, 5.0 us)
Async XLA Ops:
  8.3 24.5 %all-to-all-start = ((bf16[8,73,512]{2,1,0:T(8,128)(2,1)}), bf16[8,73,512]{2,1,0:T(8,128)(2,1)S(1)}, u32[]{:S(2)}, u32[]{:S(2)}) async-start(bf16[8,73,512]{2,1,0:T(8,128)(2,1)} %broadcast_in_dim.89), calls=%async_computation | async-start | bytes 1310720 | tf_op jit(solution)/shard_map/all_to_all | solution.py:634
  15.6 118.3 %all-gather.3.cloned.1.call-start = ((), (), s32[]{:S(2)}) async-start(), calls=%async_computation.9 | async-start | bytes 5898240 | tf_op jit(solution)/shard_map/all_gather | solution.py:638
  15.7 0.6 copy-start.4
  27.7 21.3 %copy-start.6 = (bf16[256,256]{1,0:T(8,128)(2,1)S(1)}, bf16[256,256]{1,0:T(8,128)(2,1)}, u32[]{:S(2)}) copy-start(bf16[256,256]{1,0:T(8,128)(2,1)} %param.22) | copy-start | bytes 393220
  32.9 0.8 copy-start
  48.8 33.9 %copy-start.10 = (bf16[256,73]{0,1:T(8,128)(2,1)S(1)}, bf16[256,73]{0,1:T(8,128)(2,1)}, u32[]{:S(2)}) copy-start(bf16[256,73]{0,1:T(8,128)(2,1)} %param.20) | copy-start | bytes 112132
  189.2 50.6 %all-to-all-start.1 = ((bf16[4,60,32,256]{3,2,1,0:T(8,128)(2,1)}), bf16[4,60,32,256]{3,2,1,0:T(8,128)(2,1)}, u32[]{:S(2)}, u32[]{:S(2)}) async-start(bf16[4,60,32,256]{3,2,1,0:T(8,128)(2,1)} %get-tuple-element.55), calls=%async_computation.1 | async-start | bytes 7864320 | tf_op jit(solution)/shard_map/all_to_all | solution.py:693
  194.5 101.2 %copy-start.2 = (bf16[2,256,256]{2,1,0:T(8,128)(2,1)S(1)}, bf16[2,256,256]{2,1,0:T(8,128)(2,1)}, u32[]{:S(2)}) copy-start(bf16[2,256,256]{2,1,0:T(8,128)(2,1)} %param.24) | copy-start | bytes 786436
  290.8 50.2 %all-to-all-start.3 = ((bf16[4,120,16,256]{3,2,1,0:T(8,128)(2,1)}), bf16[4,120,16,256]{3,2,1,0:T(8,128)(2,1)}, u32[]{:S(2)}, u32[]{:S(2)}) async-start(bf16[4,120,16,256]{3,2,1,0:T(8,128)(2,1)} %get-tuple-element.60), calls=%async_computation.3 | async-start | bytes 7864320 | tf_op jit(solution)/shard_map/all_to_all | solution.py:693
  377.3 139.0 %copy-start.5 = (s32[1,4,8,128]{3,1,2,0:T(4,128)S(1)}, s32[1,4,8,128]{3,1,2,0:T(4,128)}, u32[]{:S(2)}) copy-start(s32[1,4,8,128]{3,1,2,0:T(4,128)} %copy-done.4) | copy-start | bytes 49156
  377.3 139.0 %copy-start.9 = (s32[4096]{0:T(1024)S(1)}, s32[4096]{0:T(1024)}, u32[]{:S(2)}) copy-start(s32[4096]{0:T(1024)} %param.17) | copy-start | bytes 49156
  377.3 139.0 %copy-start.1 = (bf16[8,73,512]{2,1,0:T(8,128)(2,1)S(1)}, bf16[8,73,512]{2,1,0:T(8,128)(2,1)}, u32[]{:S(2)}) copy-start(bf16[8,73,512]{2,1,0:T(8,128)(2,1)} %copy-done) | copy-start | bytes 1794052
  377.3 139.7 %copy-start.3 = (f32[4096]{0:T(1024)S(1)}, f32[4096]{0:T(1024)}, u32[]{:S(2)}) copy-start(f32[4096]{0:T(1024)} %param.19) | copy-start | bytes 49156
  377.3 139.7 %copy-start.8 = (s32[4096]{0:T(1024)S(1)}, s32[4096]{0:T(1024)}, u32[]{:S(2)}) copy-start(s32[4096]{0:T(1024)} %get-tuple-element.74) | copy-start | bytes 49156
  512.6 135.3 %all-to-all-start.4 = ((bf16[32,45,16,128]{3,2,1,0:T(8,128)(2,1)}), bf16[32,45,16,128]{3,2,1,0:T(8,128)(2,1)}, u32[]{:S(2)}, u32[]{:S(2)}) async-start(bf16[32,45,16,128]{3,2,1,0:T(8,128)(2,1)} %bitcast.45), calls=%async_computation.4 | async-start | bytes 11796480 | tf_op jit(solution)/shard_map/all_to_all | solution.py:720
  570.7 90.6 %copy-start.7 = (bf16[256,256]{1,0:T(8,128)(2,1)S(1)}, bf16[256,256]{1,0:T(8,128)(2,1)}, u32[]{:S(2)}) copy-start(bf16[256,256]{1,0:T(8,128)(2,1)} %param.22) | copy-start | bytes 393220
  570.7 90.6 %copy-start.11 = (bf16[256,73]{0,1:T(8,128)(2,1)S(1)}, bf16[256,73]{0,1:T(8,128)(2,1)}, u32[]{:S(2)}) copy-start(bf16[256,73]{0,1:T(8,128)(2,1)} %param.20) | copy-start | bytes 112132
  570.7 90.6 %copy-start.12 = (f32[256]{0:T(256)S(1)}, f32[256]{0:T(256)}, u32[]{:S(2)}) copy-start(f32[256]{0:T(256)} %param.21) | copy-start | bytes 3076
  570.7 90.6 %copy-start.13 = (f32[256]{0:T(256)S(1)}, f32[256]{0:T(256)}, u32[]{:S(2)}) copy-start(f32[256]{0:T(256)} %param.23) | copy-start | bytes 3076
  656.9 104.4 %all-to-all-start.8 = ((bf16[8,1440,128]{2,1,0:T(8,128)(2,1)}), bf16[8,1440,128]{2,1,0:T(8,128)(2,1)}, u32[]{:S(2)}, u32[]{:S(2)}) async-start(bf16[8,1440,128]{2,1,0:T(8,128)(2,1)} %shard_map.125), calls=%async_computation.8 | async-start | bytes 5898240 | tf_op jit(solution)/shard_map/all_to_all | solution.py:741
  761.2 198.4 %all-to-all-start.7 = ((bf16[8,4320,128]{2,1,0:T(8,128)(2,1)}), bf16[8,4320,128]{2,1,0:T(8,128)(2,1)}, u32[]{:S(2)}, u32[]{:S(2)}) async-start(bf16[8,4320,128]{2,1,0:T(8,128)(2,1)} %shard_map.124), calls=%async_computation.7 | async-start | bytes 17694720 | tf_op jit(solution)/shard_map/all_to_all | solution.py:741
  959.7 110.0 %all-to-all-start.6 = ((bf16[8,2340,128]{2,1,0:T(8,128)(2,1)}), bf16[8,2340,128]{2,1,0:T(8,128)(2,1)}, u32[]{:S(2)}, u32[]{:S(2)}) async-start(bf16[8,2340,128]{2,1,0:T(8,128)(2,1)} %shard_map.123), calls=%async_computation.6 | async-start | bytes 9601024 | tf_op jit(solution)/shard_map/all_to_all | solution.py:741
Sparse Core Ops, SparseCore 0:
  48.9 84.9 all-gather.2

commit v6 on v5

--- a/solution.py
+++ b/solution.py
@@ -14,7 +14,7 @@
 LANES = 128
 TILE = 16
 WINDOW = 48
-UNROLL = 3
+UNROLL = 5
 LATS = 8
 CHUNK_CUTS = (1, 4)
 ORDER_GROUP = 8
@@ -437,7 +437,7 @@
             taken[:, at, :] = turned.reshape(side, side, width)
             return carry
 
-        lax.fori_loop(0, lat_total // side, one, 0)
+        lax.fori_loop(0, lat_total // side, one, 0, unroll=5)
 
     spectrum = jnp.concatenate([taken[2 * order], taken[2 * order + 1]], axis=1)
     coeffs = lax.dot_general(
@@ -469,7 +469,7 @@
                     ]
             return carry
 
-        lax.fori_loop(0, lat_total // side, one, 0)
+        lax.fori_loop(0, lat_total // side, one, 0, unroll=5)
 
 
 def order_steps(place, spectra, rows, fwd_table, inv_table, mix_t, first, parts, halves):
@@ -644,9 +644,9 @@
     listing = jnp.arange(ORDERS, dtype=jnp.int32).reshape(-1, ord_dev // ORDER_GROUP, ORDER_GROUP)
     basis_out = basis_by_point(listing.transpose(1, 0, 2).reshape(-1), at)
     basis_out = jnp.where(inside, basis_out, 0)
-    band, basis_out = lax.optimization_barrier((band, basis_out))
     coded = band[:, channels + 2 : channels + 4, : lat_dev + 1].astype(jnp.int32)
     starts = coded[:, 0] * 128 + coded[:, 1]
+    starts, basis_out = lax.optimization_barrier((starts, basis_out))
 
     mine = lax.axis_index("lon")
     sets = ord_dev // ORDER_GROUP
@@ -692,6 +692,14 @@
     def exchange(piece):
         return lax.all_to_all(piece, "lat", split_axis=0, concat_axis=0, tiled=True)
 
+    piece = source_all.transpose(1, 0, 2).reshape(channels, -1)
+    regridded = regrid_all(
+        piece,
+        recv_src.reshape(lon_count, slot_count),
+        recv_cell.reshape(lon_count, slot_count),
+        recv_weight.reshape(lon_count, slot_count),
+        cells_dev,
+    )
     early = exchange(first)
     modes, waiting = [], []
     for g in range(sets):
@@ -701,6 +709,7 @@
         else:
             piece, early = lax.optimization_barrier((piece, early))
         waiting.append(exchange(piece))
+    waiting[0], regridded = lax.optimization_barrier((waiting[0], regridded))
     for g in range(sets):
         made = order_steps(
             place,
@@ -716,26 +725,18 @@
         made = made.reshape(lat_count * lon_count, part_lats, 2 * ORDER_GROUP, LANES)
         if g + 1 < sets:
             made, waiting[g + 1] = lax.optimization_barrier((made, waiting[g + 1]))
+        if modes:
+            made, modes[-1] = lax.optimization_barrier((made, modes[-1]))
         modes.append(
             lax.all_to_all(made, ("lat", "lon"), split_axis=0, concat_axis=0, tiled=True)
         )
 
-    piece = source_all.transpose(1, 0, 2).reshape(channels, -1)
-    regridded = regrid_all(
-        piece,
-        recv_src.reshape(lon_count, slot_count),
-        recv_cell.reshape(lon_count, slot_count),
-        recv_weight.reshape(lon_count, slot_count),
-        cells_dev,
-    )
-    modes[-1], regridded = lax.optimization_barrier((modes[-1], regridded))
     running = encoder_by_cell(regridded, enc_w1, enc_b1, enc_w2, enc_b2)
+    modes[-1], running = lax.optimization_barrier((modes[-1], running))
     cuts = [0] + [c * LATS for c in CHUNK_CUTS if c * LATS < part_lats] + [part_lats]
     parts = []
     for first, last in zip(cuts[:-1], cuts[1:]):
         parts.append(synthesis_steps(modes, basis_out, lon_dev, LATS, first, last - first))
-    if len(parts) > 1:
-        parts[1], running = lax.optimization_barrier((parts[1], running))
     for first, last, part in zip(cuts[:-1], cuts[1:], parts):
         count = last - first
         part = lax.all_to_all(part, "lon", split_axis=0, concat_axis=0, tiled=True)

time: 1090 us -> 1050 us (0.963)
  blocking collectives: 186 us -> 50.9 us
  waiting for transfers between devices: 413 us -> 537 us
  Pallas kernels: 237 us -> 211 us
    all_to_all x1 -> x0, blocking collectives: 135 us -> none  [listed_plan(): lax.all_to_all(made, ('lat', 'lon'), split_axis=0, concat_axis=0, tiled=T...]
    all_to_all x1 -> x2, waiting for transfers between devices: 77.2 us -> 155 us  [listed_plan(): lax.all_to_all(made, ('lat', 'lon'), split_axis=0, concat_axis=0, tiled=T...]
    all_to_all x3, waiting for transfers between devices: 268 us -> 316 us  [listed_plan(): part = lax.all_to_all(part, 'lon', split_axis=0, concat_axis=0, tiled=True)]
    pallas_call x2, Pallas kernels: 72.4 us -> 54.6 us  [order_steps(): pl.pallas_call(functools.partial(orders_kernel, group=group, pieces=piece...]
  transfers between devices with their start and end apart: 8 -> 9, of which waited for: 7 -> 8; matrix products, arithmetic and copies ran while one was open for 17% -> 18% of each run, Pallas kernels for 11% -> 13%
where the time goes in v6:
time: 1050 us; the launch traced here: 1040 us
  waiting for transfers between devices  537 us (51%)
  Pallas kernels  211 us (20%)
  other arithmetic  92.9 us (9%)
  matrix products  81 us (8%)
  blocking collectives  50.9 us (5%)
  starting transfers between devices  38.7 us (4%)
  local copies, waits for them, and re-layouts  17.1 us (2%)
  between operations  14 us (1%)
    all_to_all x3, waiting for transfers between devices, listed_plan(): part = lax.all_to_all(part, 'lon', split_axis=0, concat_axis=0, tiled=True)  316 us
    all_to_all x2, waiting for transfers between devices, listed_plan(): lax.all_to_all(made, ('lat', 'lon'), split_axis=0, concat_axis=0, tiled=T...  155 us
    dot_general x1, matrix products, encoder_by_cell(): jnp.dot(hidden, enc_w2.T, preferred_element_type=F32) + enc_b2  81 us
    pallas_call x2, Pallas kernels, order_steps(): pl.pallas_call(functools.partial(orders_kernel, group=group, pieces=piece...  54.6 us
    all_to_all x1, blocking collectives, exchange(): return lax.all_to_all(piece, 'lat', split_axis=0, concat_axis=0, tiled=True)  50.9 us
    all_gather x1, waiting for transfers between devices, listed_plan(): band = lax.all_gather(listed, 'lon', axis=0, tiled=False)  48.4 us
    pallas_call x1, Pallas kernels, zonal_transform(): pl.pallas_call(functools.partial(zonal_first_kernel, channels=channels, b...  46.2 us
    scatter-add x1, other arithmetic, spread(): return running.at[targets.reshape(-1)].add(contrib.reshape(-1, channels))  44.8 us
  transfers between devices with their start and end apart: 9, of which 8 were waited for; matrix products, arithmetic and copies ran while one was open for 18% of the time, Pallas kernels for 13%

profile of v6, /device:TPU:0, one launch (start us, length us, event | category | flops | bytes accessed | tf_op | source)
XLA Modules:
  0.0 1042.7 jit_solution(9824498817025647549)
XLA Ops:
  6.5 1.8 broadcast_in_dim.89
  8.3 7.3 all-to-all-start
  15.7 1.4 broadcast_clamp_fusion
  18.2 5.8 sort.15
  24.2 0.9 stack.39
  25.2 1.9 copy.68.cols_ref
  27.1 5.8 all-to-all-done.src_ref
  32.9 0.8 copy-done.1
  33.7 13.7 %shard_map.118 = bf16[80,4096]{1,0:T(8,128)(2,1)} custom-call(s32[1]{0:T(128)} %slice.51.live, bf16[8,73,512]{2,1,0:T(8,128)(2,1)} %copy-done.1, f32[4096,8]{1,0:T(8,128)} %copy.68.cols_ref, f32[1,4096]{1,0:T(1,128)} %bitcast.64), custom_call_target="tpu_custom_call" | custom-call | flops 8589934592 | bytes 1048576 | tf_op jit(solution)/shard_map/pallas_call | solution.py:169
  47.7 0.8 copy.71
  48.5 2.6 cosine_multiply_fusion
  51.5 1.2 copy.72
  53.5 19.5 %multiply_convert_fusion.1 = (bf16[8,192,512,1]{1,0,3,2:T(8,128)(2,1)S(1)}, bf16[8,192,512,1]{1,0,3,2:T(8,128)(2,1)S(1)}) fusion(s32[512]{0:T(512)S(1)} %reshape.369, s32[8,192]{1,0:T(8,128)S(1)} %iota_add_fusion.1), kind=kLoop, calls=%fused_computation.31 | loop fusion | flops 10223616 | bytes 3153920 | tf_op jit(solution)/shard_map/convert
  72.9 2.7 pad_maximum_fusion
  75.6 5.7 copy.70
  82.0 1.9 broadcast_select_fusion.1.basis_ref
  83.9 2.0 broadcast_select_fusion.refs_2_
  85.9 48.4 %all-gather.3.cloned.1.call-done = bf16[640,4096]{1,0:T(8,128)(2,1)} async-done(((bf16[80,4096]{1,0:T(8,128)(2,1)}), bf16[640,4096]{1,0:T(8,128)(2,1)}) %all-gather.3.cloned.1.call-update) | async-done | bytes 5242896 | tf_op jit(solution)/shard_map/all_gather | solution.py:638
  134.3 0.8 slice.61
  135.7 46.2 %shard_map.119 = (bf16[4,60,32,256]{3,2,1,0:T(8,128)(2,1)}, bf16[32816,256]{1,0:T(8,128)(2,1)}, bf16[32816,128]{1,0:T(8,128)(2,1)}, f32[128,256]{1,0:T(8,128)}) custom-call(s32[8,181]{1,0:T(8,128)} %fusion.39.starts, bf16[8,80,4096]{2,1,0:T(8,128)(2,1)} %bitcast.66, bf16[80,256]{1,0:T(8,128)(2,1)} %scatter.9.w1_ref, f32[1,256]{1,0:T(1,128)} %bitcast.67, ...), custom_call_target="tpu_custom_call" | custom-call | flops 53687091200 | bytes 33554432 | tf_op jit(solution)/shard_map/pallas_call | solution.py:363
  181.9 5.7 all-to-all-start.1
  187.6 33.4 %shard_map.120 = (bf16[4,120,16,256]{3,2,1,0:T(8,128)(2,1)}, bf16[4,120,16,256]{3,2,1,0:T(8,128)(2,1)}) custom-call(s32[8,181]{1,0:T(8,128)} %fusion.39.starts, bf16[32816,256]{1,0:T(8,128)(2,1)} %get-tuple-element.53.delta, bf16[32816,128]{1,0:T(8,128)(2,1)} %get-tuple-element.54.hots, f32[128,256]{1,0:T(8,128)} %get-tuple-element.55.base), custom_call_target="tpu_custom_call" | custom-call | flops 53687091200 | bytes 33554432 | tf_op jit(solution)/shard_map/pallas_call | solution.py:389
  221.0 12.0 %all-to-all-done.1.refs_0_ = bf16[4,60,32,256]{3,2,1,0:T(8,128)(2,1)} async-done(((bf16[4,60,32,256]{3,2,1,0:T(8,128)(2,1)}), bf16[4,60,32,256]{3,2,1,0:T(8,128)(2,1)}, u32[]{:S(2)}, u32[]{:S(2)}) %all-to-all-start.1) | async-done | bytes 3932192 | tf_op jit(solution)/shard_map/all_to_all | solution.py:693
  233.0 50.9 %all_to_all.45.refs_1_ = bf16[4,120,16,256]{3,2,1,0:T(8,128)(2,1)} all-to-all(bf16[4,120,16,256]{3,2,1,0:T(8,128)(2,1)} %get-tuple-element.60), channel_id=1, replica_groups=mesh['lat'=4,'lon'=8] {'lat'}, dimensions={0} | all-to-all | bytes 7864320 | tf_op jit(solution)/shard_map/all_to_all | solution.py:693
  284.0 5.2 all-to-all-start.3
  289.4 0.8 maximum_bitcast_fusion.refs_4_
  290.3 0.8 fusion.30.refs_5_
  291.8 44.8 %scatter_custom_fusion = f32[32400,73]{1,0:T(8,128)} fusion(s32[4096]{0:T(1024)S(1)} %get-tuple-element.89, f32[]{:T(128)} %constant.199.clone.1, f32[4096]{0:T(1024)S(1)} %copy-done.4, pred[4096]{0:T(1024)(128)(4,1)S(1)} %compare_and_fusion, bf16[]{:T(256)} %constant.220.clone.1, bf16[4096,73]{1,0:T(8,128)(2,1)S(1)} %bitcast.49, ...), kind=kCustom, calls=%fused_computation.24 | custom fusion | flops 1196032 | bytes 10546246 | tf_op jit(solution)/shard_map/scatter-add | solution.py:52
  336.5 8.8 convert_element_type.120
  345.4 27.2 %shard_map.121 = bf16[16,2,45,16,128]{4,3,2,1,0:T(8,128)(2,1)} custom-call(s32[720]{0:T(1024)} %constant.252.clone.place, bf16[4,60,32,256]{3,2,1,0:T(8,128)(2,1)} %all-to-all-done.1.refs_0_, bf16[4,120,16,256]{3,2,1,0:T(8,128)(2,1)} %all_to_all.45.refs_1_, bf16[16,720,512]{2,1,0:T(8,128)(2,1)} %bitcast.43, bf16[16,720,512]{2,1,0:T(8,128)(2,1)} %refs_3_.3, ...), custom_call_target="tpu_custom_call" | custom-call | flops 8187281408 | bytes 23592960 | tf_op jit(solution)/shard_map/pallas_call | solution.py:488
  372.6 3.6 all-to-all-start.4
  376.3 27.4 %shard_map.122 = bf16[16,2,45,16,128]{4,3,2,1,0:T(8,128)(2,1)} custom-call(s32[720]{0:T(1024)} %constant.252.clone.place, bf16[4,60,32,256]{3,2,1,0:T(8,128)(2,1)} %all-to-all-done.1.refs_0_, bf16[4,120,16,256]{3,2,1,0:T(8,128)(2,1)} %all-to-all-done.3.refs_1_, bf16[16,720,512]{2,1,0:T(8,128)(2,1)} %bitcast.44, bf16[16,720,512]{2,1,0:T(8,128)(2,1)} %refs_3_.3, ...), custom_call_target="tpu_custom_call" | custom-call | flops 8187281408 | bytes 23592960 | tf_op jit(solution)/shard_map/pallas_call | solution.py:488
  403.7 104.3 %all-to-all-done.4.refs_0_ = bf16[32,45,16,128]{3,2,1,0:T(8,128)(2,1)} async-done(((bf16[32,45,16,128]{3,2,1,0:T(8,128)(2,1)}), bf16[32,45,16,128]{3,2,1,0:T(8,128)(2,1)}, u32[]{:S(2)}, u32[]{:S(2)}) %all-to-all-start.4) | async-done | bytes 5898272 | tf_op jit(solution)/shard_map/all_to_all | solution.py:731
  507.9 3.6 all-to-all-start.5
  511.6 81.0 %fusion.enc_ref = bf16[32400,256]{1,0:T(8,128)(2,1)} fusion(bf16[256,256]{1,0:T(8,128)(2,1)S(1)} %copy-done.6, f32[256]{0:T(256)S(1)} %copy-done.11, bf16[32400,73]{1,0:T(8,128)(2,1)} %convert_element_type.120, bf16[256,73]{0,1:T(8,128)(2,1)S(1)} %copy-done.9, f32[256]{0:T(256)S(1)} %copy-done.10), kind=kOutput, calls=%fused_computation.5 | convolution fusion | flops 6021734400 | bytes 21489696 | tf_op jit(solution)/shard_map/dot_general | solution.py:90
  592.6 50.6 %all-to-all-done.5.refs_1_ = bf16[32,45,16,128]{3,2,1,0:T(8,128)(2,1)} async-done(((bf16[32,45,16,128]{3,2,1,0:T(8,128)(2,1)}), bf16[32,45,16,128]{3,2,1,0:T(8,128)(2,1)}, u32[]{:S(2)}, u32[]{:S(2)}) %all-to-all-start.5) | async-done | bytes 5898272 | tf_op jit(solution)/shard_map/all_to_all | solution.py:731
  643.3 9.0 shard_map.125
  652.2 3.6 all-to-all-start.8
  655.9 18.9 %shard_map.124 = bf16[8,4320,128]{2,1,0:T(8,128)(2,1)} custom-call(bf16[32,45,16,128]{3,2,1,0:T(8,128)(2,1)} %all-to-all-done.4.refs_0_, bf16[32,45,16,128]{3,2,1,0:T(8,128)(2,1)} %all-to-all-done.5.refs_1_, bf16[8,192,1024]{2,1,0:T(8,128)(2,1)} %broadcast_select_fusion.refs_2_), custom_call_target="tpu_custom_call" | custom-call | flops 9663676416 | bytes 17694720 | tf_op jit(solution)/shard_map/pallas_call | solution.py:548
  674.7 47.8 %all-to-all-done.8 = bf16[8,1440,128]{2,1,0:T(8,128)(2,1)S(1)} async-done(((bf16[8,1440,128]{2,1,0:T(8,128)(2,1)}), bf16[8,1440,128]{2,1,0:T(8,128)(2,1)S(1)}, u32[]{:S(2)}, u32[]{:S(2)}) %all-to-all-start.8) | async-done | bytes 2949152 | tf_op jit(solution)/shard_map/all_to_all | solution.py:742
  722.5 5.0 all-to-all-start.7
  727.5 13.6 %shard_map.123 = bf16[8,2340,128]{2,1,0:T(8,128)(2,1)} custom-call(bf16[32,45,16,128]{3,2,1,0:T(8,128)(2,1)} %all-to-all-done.4.refs_0_, bf16[32,45,16,128]{3,2,1,0:T(8,128)(2,1)} %all-to-all-done.5.refs_1_, bf16[8,192,1024]{2,1,0:T(8,128)(2,1)} %broadcast_select_fusion.refs_2_), custom_call_target="tpu_custom_call" | custom-call | flops 5234491392 | bytes 9584640 | tf_op jit(solution)/shard_map/pallas_call | solution.py:548
  741.1 178.7 %all-to-all-done.7 = bf16[8,4320,128]{2,1,0:T(8,128)(2,1)} async-done(((bf16[8,4320,128]{2,1,0:T(8,128)(2,1)}), bf16[8,4320,128]{2,1,0:T(8,128)(2,1)}, u32[]{:S(2)}, u32[]{:S(2)}) %all-to-all-start.7) | async-done | bytes 8847392 | tf_op jit(solution)/shard_map/all_to_all | solution.py:742
  919.8 4.6 all-to-all-start.6
  924.5 5.1 shard_map.126.enc_ref
  929.6 10.9 %shard_map.127.enc_ref = bf16[32400,256]{1,0:T(8,128)(2,1)} custom-call(bf16[4,2,4320,128]{3,2,1,0:T(8,128)(2,1)} %bitcast.25.part_ref, bf16[32400,256]{1,0:T(8,128)(2,1)} %shard_map.126.enc_ref), custom_call_target="tpu_custom_call", output_to_operand_aliasing={{}: (1, {})} | custom-call | flops 17694720 | bytes 26542080 | tf_op jit(solution)/shard_map/pallas_call | solution.py:589
  940.5 89.4 %all-to-all-done.6 = bf16[8,2340,128]{2,1,0:T(8,128)(2,1)} async-done(((bf16[8,2340,128]{2,1,0:T(8,128)(2,1)}), bf16[8,2340,128]{2,1,0:T(8,128)(2,1)}, u32[]{:S(2)}, u32[]{:S(2)}) %all-to-all-start.6) | async-done | bytes 4792352 | tf_op jit(solution)/shard_map/all_to_all | solution.py:742
  1029.9 5.7 shard_map.128
  (61 shorter events, 5.1 us)
Async XLA Ops:
  8.3 24.5 %all-to-all-start = ((bf16[8,73,512]{2,1,0:T(8,128)(2,1)}), bf16[8,73,512]{2,1,0:T(8,128)(2,1)S(1)}, u32[]{:S(2)}, u32[]{:S(2)}) async-start(bf16[8,73,512]{2,1,0:T(8,128)(2,1)} %broadcast_in_dim.89), calls=%async_computation | async-start | bytes 1310720 | tf_op jit(solution)/shard_map/all_to_all | solution.py:634
  15.6 118.7 %all-gather.3.cloned.1.call-start = ((), (), s32[]{:S(2)}) async-start(), calls=%async_computation.9 | async-start | bytes 5898240 | tf_op jit(solution)/shard_map/all_gather | solution.py:638
  27.1 20.6 %copy-start.5 = (bf16[256,256]{1,0:T(8,128)(2,1)S(1)}, bf16[256,256]{1,0:T(8,128)(2,1)}, u32[]{:S(2)}) copy-start(bf16[256,256]{1,0:T(8,128)(2,1)} %param.22) | copy-start | bytes 393220
  32.9 0.8 copy-start.1
  47.4 33.9 %copy-start.8 = (bf16[256,73]{0,1:T(8,128)(2,1)S(1)}, bf16[256,73]{0,1:T(8,128)(2,1)}, u32[]{:S(2)}) copy-start(bf16[256,73]{0,1:T(8,128)(2,1)} %param.20) | copy-start | bytes 112132
  181.9 51.1 %all-to-all-start.1 = ((bf16[4,60,32,256]{3,2,1,0:T(8,128)(2,1)}), bf16[4,60,32,256]{3,2,1,0:T(8,128)(2,1)}, u32[]{:S(2)}, u32[]{:S(2)}) async-start(bf16[4,60,32,256]{3,2,1,0:T(8,128)(2,1)} %get-tuple-element.57), calls=%async_computation.1 | async-start | bytes 7864320 | tf_op jit(solution)/shard_map/all_to_all | solution.py:693
  187.6 101.6 %copy-start.3 = (bf16[2,256,256]{2,1,0:T(8,128)(2,1)S(1)}, bf16[2,256,256]{2,1,0:T(8,128)(2,1)}, u32[]{:S(2)}) copy-start(bf16[2,256,256]{2,1,0:T(8,128)(2,1)} %param.24) | copy-start | bytes 786436
  221.0 69.3 %copy-start.7 = (s32[4096]{0:T(1024)S(1)}, s32[4096]{0:T(1024)}, u32[]{:S(2)}) copy-start(s32[4096]{0:T(1024)} %param.17) | copy-start | bytes 49156
  221.0 70.0 %copy-start.2 = (bf16[8,73,512]{2,1,0:T(8,128)(2,1)S(1)}, bf16[8,73,512]{2,1,0:T(8,128)(2,1)}, u32[]{:S(2)}) copy-start(bf16[8,73,512]{2,1,0:T(8,128)(2,1)} %copy-done.1) | copy-start | bytes 1794052
  221.0 70.7 %copy-start.4 = (f32[4096]{0:T(1024)S(1)}, f32[4096]{0:T(1024)}, u32[]{:S(2)}) copy-start(f32[4096]{0:T(1024)} %param.19) | copy-start | bytes 49156
  284.0 88.6 %all-to-all-start.3 = ((bf16[4,120,16,256]{3,2,1,0:T(8,128)(2,1)}), bf16[4,120,16,256]{3,2,1,0:T(8,128)(2,1)}, u32[]{:S(2)}, u32[]{:S(2)}) async-start(bf16[4,120,16,256]{3,2,1,0:T(8,128)(2,1)} %get-tuple-element.63), calls=%async_computation.3 | async-start | bytes 7864320 | tf_op jit(solution)/shard_map/all_to_all | solution.py:693
  372.6 135.3 %all-to-all-start.4 = ((bf16[32,45,16,128]{3,2,1,0:T(8,128)(2,1)}), bf16[32,45,16,128]{3,2,1,0:T(8,128)(2,1)}, u32[]{:S(2)}, u32[]{:S(2)}) async-start(bf16[32,45,16,128]{3,2,1,0:T(8,128)(2,1)} %bitcast.45), calls=%async_computation.4 | async-start | bytes 11796480 | tf_op jit(solution)/shard_map/all_to_all | solution.py:731
  376.2 135.3 %copy-start.6 = (bf16[256,256]{1,0:T(8,128)(2,1)S(1)}, bf16[256,256]{1,0:T(8,128)(2,1)}, u32[]{:S(2)}) copy-start(bf16[256,256]{1,0:T(8,128)(2,1)} %param.22) | copy-start | bytes 393220
  376.3 135.3 %copy-start.9 = (bf16[256,73]{0,1:T(8,128)(2,1)S(1)}, bf16[256,73]{0,1:T(8,128)(2,1)}, u32[]{:S(2)}) copy-start(bf16[256,73]{0,1:T(8,128)(2,1)} %param.20) | copy-start | bytes 112132
  376.3 135.3 %copy-start.10 = (f32[256]{0:T(256)S(1)}, f32[256]{0:T(256)}, u32[]{:S(2)}) copy-start(f32[256]{0:T(256)} %param.21) | copy-start | bytes 3076
  376.3 135.3 %copy-start.11 = (f32[256]{0:T(256)S(1)}, f32[256]{0:T(256)}, u32[]{:S(2)}) copy-start(f32[256]{0:T(256)} %param.23) | copy-start | bytes 3076
  507.9 135.3 %all-to-all-start.5 = ((bf16[32,45,16,128]{3,2,1,0:T(8,128)(2,1)}), bf16[32,45,16,128]{3,2,1,0:T(8,128)(2,1)}, u32[]{:S(2)}, u32[]{:S(2)}) async-start(bf16[32,45,16,128]{3,2,1,0:T(8,128)(2,1)} %bitcast.46), calls=%async_computation.5 | async-start | bytes 11796480 | tf_op jit(solution)/shard_map/all_to_all | solution.py:731
  652.2 70.3 %all-to-all-start.8 = ((bf16[8,1440,128]{2,1,0:T(8,128)(2,1)}), bf16[8,1440,128]{2,1,0:T(8,128)(2,1)S(1)}, u32[]{:S(2)}, u32[]{:S(2)}) async-start(bf16[8,1440,128]{2,1,0:T(8,128)(2,1)} %shard_map.125), calls=%async_computation.8 | async-start | bytes 5898240 | tf_op jit(solution)/shard_map/all_to_all | solution.py:742
  722.5 18.6 %copy-start = (bf16[8,1440,128]{2,1,0:T(8,128)(2,1)}, bf16[8,1440,128]{2,1,0:T(8,128)(2,1)S(1)}, u32[]{:S(2)}) copy-start(bf16[8,1440,128]{2,1,0:T(8,128)(2,1)S(1)} %all-to-all-done.8) | copy-start | bytes 8847364
  722.5 197.3 %all-to-all-start.7 = ((bf16[8,4320,128]{2,1,0:T(8,128)(2,1)}), bf16[8,4320,128]{2,1,0:T(8,128)(2,1)}, u32[]{:S(2)}, u32[]{:S(2)}) async-start(bf16[8,4320,128]{2,1,0:T(8,128)(2,1)} %shard_map.124), calls=%async_computation.7 | async-start | bytes 17694720 | tf_op jit(solution)/shard_map/all_to_all | solution.py:742
  919.8 110.1 %all-to-all-start.6 = ((bf16[8,2340,128]{2,1,0:T(8,128)(2,1)}), bf16[8,2340,128]{2,1,0:T(8,128)(2,1)}, u32[]{:S(2)}, u32[]{:S(2)}) async-start(bf16[8,2340,128]{2,1,0:T(8,128)(2,1)} %shard_map.123), calls=%async_computation.6 | async-start | bytes 9601024 | tf_op jit(solution)/shard_map/all_to_all | solution.py:742
Sparse Core Ops, SparseCore 0:
  47.5 86.6 all-gather.2

commit v7 on v6

--- a/solution.py
+++ b/solution.py
@@ -709,7 +709,6 @@
         else:
             piece, early = lax.optimization_barrier((piece, early))
         waiting.append(exchange(piece))
-    waiting[0], regridded = lax.optimization_barrier((waiting[0], regridded))
     for g in range(sets):
         made = order_steps(
             place,
@@ -726,7 +725,7 @@
         if g + 1 < sets:
             made, waiting[g + 1] = lax.optimization_barrier((made, waiting[g + 1]))
         if modes:
-            made, modes[-1] = lax.optimization_barrier((made, modes[-1]))
+            made, modes[-1], regridded = lax.optimization_barrier((made, modes[-1], regridded))
         modes.append(
             lax.all_to_all(made, ("lat", "lon"), split_axis=0, concat_axis=0, tiled=True)
         )

time: 1050 us -> 1010 us (0.962)
  waiting for transfers between devices: 537 us -> 497 us
    all_to_all x2, waiting for transfers between devices: 155 us -> 100 us  [listed_plan(): lax.all_to_all(made, ('lat', 'lon'), split_axis=0, concat_axis=0, tiled=T...]
    all_to_all x2, waiting for transfers between devices: 12 us -> 28.2 us  [exchange(): return lax.all_to_all(piece, 'lat', split_axis=0, concat_axis=0, tiled=True)]
  transfers between devices with their start and end apart: 9 -> 9, of which waited for: 8 -> 9; matrix products, arithmetic and copies ran while one was open for 18% -> 19% of each run, Pallas kernels for 13% -> 14%
where the time goes in v7:
time: 1010 us; the launch traced here: 1000 us
  waiting for transfers between devices  497 us (49%)
  Pallas kernels  213 us (21%)
  other arithmetic  92.9 us (9%)
  matrix products  81 us (8%)
  blocking collectives  51 us (5%)
  starting transfers between devices  37.8 us (4%)
  local copies, waits for them, and re-layouts  17.6 us (2%)
  between operations  14 us (1%)
    all_to_all x3, waiting for transfers between devices, listed_plan(): part = lax.all_to_all(part, 'lon', split_axis=0, concat_axis=0, tiled=True)  316 us
    all_to_all x2, waiting for transfers between devices, listed_plan(): lax.all_to_all(made, ('lat', 'lon'), split_axis=0, concat_axis=0, tiled=T...  100 us
    dot_general x1, matrix products, encoder_by_cell(): jnp.dot(hidden, enc_w2.T, preferred_element_type=F32) + enc_b2  81 us
    pallas_call x2, Pallas kernels, order_steps(): pl.pallas_call(functools.partial(orders_kernel, group=group, pieces=piece...  54.7 us
    all_to_all x1, blocking collectives, exchange(): return lax.all_to_all(piece, 'lat', split_axis=0, concat_axis=0, tiled=True)  51 us
    all_gather x1, waiting for transfers between devices, listed_plan(): band = lax.all_gather(listed, 'lon', axis=0, tiled=False)  47.2 us
    pallas_call x1, Pallas kernels, zonal_transform(): pl.pallas_call(functools.partial(zonal_first_kernel, channels=channels, b...  46.8 us
    scatter-add x1, other arithmetic, spread(): return running.at[targets.reshape(-1)].add(contrib.reshape(-1, channels))  44.9 us
  transfers between devices with their start and end apart: 9, of which 9 were waited for; matrix products, arithmetic and copies ran while one was open for 19% of the time, Pallas kernels for 14%

profile of v7, /device:TPU:0, one launch (start us, length us, event | category | flops | bytes accessed | tf_op | source)
XLA Modules:
  0.0 1004.4 jit_solution(14810821846249434657)
XLA Ops:
  6.5 1.8 broadcast_in_dim.89
  8.3 7.3 all-to-all-start
  16.3 1.4 broadcast_clamp_fusion
  18.8 5.8 sort.15
  24.8 0.9 stack.39
  25.7 1.9 copy.68.cols_ref
  27.6 5.2 all-to-all-done.src_ref
  32.9 0.8 copy-done.1
  33.7 15.0 %shard_map.118 = bf16[80,4096]{1,0:T(8,128)(2,1)} custom-call(s32[1]{0:T(128)} %slice.51.live, bf16[8,73,512]{2,1,0:T(8,128)(2,1)} %copy-done.1, f32[4096,8]{1,0:T(8,128)} %copy.68.cols_ref, f32[1,4096]{1,0:T(1,128)} %bitcast.64), custom_call_target="tpu_custom_call" | custom-call | flops 8589934592 | bytes 1048576 | tf_op jit(solution)/shard_map/pallas_call | solution.py:169
  49.0 0.8 copy.71
  49.9 2.6 cosine_multiply_fusion
  52.8 1.2 copy.72
  54.8 19.5 %multiply_convert_fusion.1 = (bf16[8,192,512,1]{1,0,3,2:T(8,128)(2,1)S(1)}, bf16[8,192,512,1]{1,0,3,2:T(8,128)(2,1)S(1)}) fusion(s32[512]{0:T(512)S(1)} %reshape.369, s32[8,192]{1,0:T(8,128)S(1)} %iota_add_fusion.1), kind=kLoop, calls=%fused_computation.31 | loop fusion | flops 10223616 | bytes 3153920 | tf_op jit(solution)/shard_map/convert
  74.3 2.7 pad_maximum_fusion
  77.0 5.7 copy.70
  83.3 2.0 broadcast_select_fusion.1.basis_ref
  85.3 1.9 broadcast_select_fusion.refs_2_
  87.2 47.2 %all-gather.3.cloned.1.call-done = bf16[640,4096]{1,0:T(8,128)(2,1)} async-done(((bf16[80,4096]{1,0:T(8,128)(2,1)}), bf16[640,4096]{1,0:T(8,128)(2,1)}) %all-gather.3.cloned.1.call-update) | async-done | bytes 5242896 | tf_op jit(solution)/shard_map/all_gather | solution.py:638
  134.3 0.8 slice.61
  135.7 46.8 %shard_map.119 = (bf16[4,60,32,256]{3,2,1,0:T(8,128)(2,1)}, bf16[32816,256]{1,0:T(8,128)(2,1)}, bf16[32816,128]{1,0:T(8,128)(2,1)}, f32[128,256]{1,0:T(8,128)}) custom-call(s32[8,181]{1,0:T(8,128)} %fusion.39.starts, bf16[8,80,4096]{2,1,0:T(8,128)(2,1)} %bitcast.66, bf16[80,256]{1,0:T(8,128)(2,1)} %scatter.9.w1_ref, f32[1,256]{1,0:T(1,128)} %bitcast.67, ...), custom_call_target="tpu_custom_call" | custom-call | flops 53687091200 | bytes 33554432 | tf_op jit(solution)/shard_map/pallas_call | solution.py:363
  182.5 4.8 all-to-all-start.1
  187.3 33.5 %shard_map.120 = (bf16[4,120,16,256]{3,2,1,0:T(8,128)(2,1)}, bf16[4,120,16,256]{3,2,1,0:T(8,128)(2,1)}) custom-call(s32[8,181]{1,0:T(8,128)} %fusion.39.starts, bf16[32816,256]{1,0:T(8,128)(2,1)} %get-tuple-element.52.delta, bf16[32816,128]{1,0:T(8,128)(2,1)} %get-tuple-element.53.hots, f32[128,256]{1,0:T(8,128)} %get-tuple-element.54.base), custom_call_target="tpu_custom_call" | custom-call | flops 53687091200 | bytes 33554432 | tf_op jit(solution)/shard_map/pallas_call | solution.py:389
  220.8 11.9 %all-to-all-done.1.refs_0_ = bf16[4,60,32,256]{3,2,1,0:T(8,128)(2,1)} async-done(((bf16[4,60,32,256]{3,2,1,0:T(8,128)(2,1)}), bf16[4,60,32,256]{3,2,1,0:T(8,128)(2,1)}, u32[]{:S(2)}, u32[]{:S(2)}) %all-to-all-start.1) | async-done | bytes 3932192 | tf_op jit(solution)/shard_map/all_to_all | solution.py:693
  232.8 51.0 %all_to_all.45.refs_1_ = bf16[4,120,16,256]{3,2,1,0:T(8,128)(2,1)} all-to-all(bf16[4,120,16,256]{3,2,1,0:T(8,128)(2,1)} %get-tuple-element.59), channel_id=1, replica_groups=mesh['lat'=4,'lon'=8] {'lat'}, dimensions={0} | all-to-all | bytes 7864320 | tf_op jit(solution)/shard_map/all_to_all | solution.py:693
  283.7 5.2 all-to-all-start.3
  289.2 0.8 maximum_bitcast_fusion.refs_4_
  290.8 27.3 %shard_map.121 = bf16[16,2,45,16,128]{4,3,2,1,0:T(8,128)(2,1)} custom-call(s32[720]{0:T(1024)} %constant.252.clone.place, bf16[4,60,32,256]{3,2,1,0:T(8,128)(2,1)} %all-to-all-done.1.refs_0_, bf16[4,120,16,256]{3,2,1,0:T(8,128)(2,1)} %all_to_all.45.refs_1_, bf16[16,720,512]{2,1,0:T(8,128)(2,1)} %bitcast.43, bf16[16,720,512]{2,1,0:T(8,128)(2,1)} %refs_3_.3, ...), custom_call_target="tpu_custom_call" | custom-call | flops 8187281408 | bytes 23592960 | tf_op jit(solution)/shard_map/pallas_call | solution.py:488
  318.1 16.2 %all-to-all-done.3.refs_1_ = bf16[4,120,16,256]{3,2,1,0:T(8,128)(2,1)} async-done(((bf16[4,120,16,256]{3,2,1,0:T(8,128)(2,1)}), bf16[4,120,16,256]{3,2,1,0:T(8,128)(2,1)}, u32[]{:S(2)}, u32[]{:S(2)}) %all-to-all-start.3) | async-done | bytes 3932192 | tf_op jit(solution)/shard_map/all_to_all | solution.py:693
  334.3 3.6 all-to-all-start.4
  338.7 44.9 %scatter_custom_fusion = f32[32400,73]{1,0:T(8,128)} fusion(s32[4096]{0:T(1024)} %get-tuple-element.87, f32[]{:T(128)} %constant.199.clone.1, f32[4096]{0:T(1024)S(1)} %copy-done.4, pred[4096]{0:T(1024)(128)(4,1)S(1)} %compare_and_fusion, bf16[]{:T(256)} %constant.222.clone.1, bf16[4096,73]{1,0:T(8,128)(2,1)S(1)} %bitcast.49, s32[4096]{0:T(1024)S(1)} %copy-done.9), kind=kCustom, calls=%fused_computation.24 | custom fusion | flops 1196032 | bytes 10096704 | tf_op jit(solution)/shard_map/scatter-add | solution.py:52
  383.6 8.8 convert_element_type.121
  392.4 27.4 %shard_map.122 = bf16[16,2,45,16,128]{4,3,2,1,0:T(8,128)(2,1)} custom-call(s32[720]{0:T(1024)} %constant.252.clone.place, bf16[4,60,32,256]{3,2,1,0:T(8,128)(2,1)} %all-to-all-done.1.refs_0_, bf16[4,120,16,256]{3,2,1,0:T(8,128)(2,1)} %all-to-all-done.3.refs_1_, bf16[16,720,512]{2,1,0:T(8,128)(2,1)} %bitcast.44, bf16[16,720,512]{2,1,0:T(8,128)(2,1)} %refs_3_.3, ...), custom_call_target="tpu_custom_call" | custom-call | flops 8187281408 | bytes 23592960 | tf_op jit(solution)/shard_map/pallas_call | solution.py:488
  419.8 49.8 %all-to-all-done.4.refs_0_ = bf16[32,45,16,128]{3,2,1,0:T(8,128)(2,1)} async-done(((bf16[32,45,16,128]{3,2,1,0:T(8,128)(2,1)}), bf16[32,45,16,128]{3,2,1,0:T(8,128)(2,1)}, u32[]{:S(2)}, u32[]{:S(2)}) %all-to-all-start.4) | async-done | bytes 5898272 | tf_op jit(solution)/shard_map/all_to_all | solution.py:730
  469.6 3.6 all-to-all-start.5
  473.3 81.0 %fusion.enc_ref = bf16[32400,256]{1,0:T(8,128)(2,1)} fusion(bf16[256,256]{1,0:T(8,128)(2,1)S(1)} %copy-done.8, f32[256]{0:T(256)S(1)} %copy-done.14, bf16[32400,73]{1,0:T(8,128)(2,1)} %convert_element_type.121, bf16[256,73]{0,1:T(8,128)(2,1)S(1)} %copy-done.12, f32[256]{0:T(256)S(1)} %copy-done.13), kind=kOutput, calls=%fused_computation.5 | convolution fusion | flops 6021734400 | bytes 21489696 | tf_op jit(solution)/shard_map/dot_general | solution.py:90
  554.3 50.6 %all-to-all-done.5.refs_1_ = bf16[32,45,16,128]{3,2,1,0:T(8,128)(2,1)} async-done(((bf16[32,45,16,128]{3,2,1,0:T(8,128)(2,1)}), bf16[32,45,16,128]{3,2,1,0:T(8,128)(2,1)}, u32[]{:S(2)}, u32[]{:S(2)}) %all-to-all-start.5) | async-done | bytes 5898272 | tf_op jit(solution)/shard_map/all_to_all | solution.py:730
  604.9 9.0 shard_map.125
  613.9 3.6 all-to-all-start.8
  617.6 18.8 %shard_map.124 = bf16[8,4320,128]{2,1,0:T(8,128)(2,1)} custom-call(bf16[32,45,16,128]{3,2,1,0:T(8,128)(2,1)} %all-to-all-done.4.refs_0_, bf16[32,45,16,128]{3,2,1,0:T(8,128)(2,1)} %all-to-all-done.5.refs_1_, bf16[8,192,1024]{2,1,0:T(8,128)(2,1)} %broadcast_select_fusion.refs_2_), custom_call_target="tpu_custom_call" | custom-call | flops 9663676416 | bytes 17694720 | tf_op jit(solution)/shard_map/pallas_call | solution.py:548
  636.4 47.8 %all-to-all-done.8 = bf16[8,1440,128]{2,1,0:T(8,128)(2,1)S(1)} async-done(((bf16[8,1440,128]{2,1,0:T(8,128)(2,1)}), bf16[8,1440,128]{2,1,0:T(8,128)(2,1)S(1)}, u32[]{:S(2)}, u32[]{:S(2)}) %all-to-all-start.8) | async-done | bytes 2949152 | tf_op jit(solution)/shard_map/all_to_all | solution.py:741
  684.2 5.0 all-to-all-start.7
  689.2 13.7 %shard_map.123 = bf16[8,2340,128]{2,1,0:T(8,128)(2,1)} custom-call(bf16[32,45,16,128]{3,2,1,0:T(8,128)(2,1)} %all-to-all-done.4.refs_0_, bf16[32,45,16,128]{3,2,1,0:T(8,128)(2,1)} %all-to-all-done.5.refs_1_, bf16[8,192,1024]{2,1,0:T(8,128)(2,1)} %broadcast_select_fusion.refs_2_), custom_call_target="tpu_custom_call" | custom-call | flops 5234491392 | bytes 9584640 | tf_op jit(solution)/shard_map/pallas_call | solution.py:548
  702.9 178.6 %all-to-all-done.7 = bf16[8,4320,128]{2,1,0:T(8,128)(2,1)} async-done(((bf16[8,4320,128]{2,1,0:T(8,128)(2,1)}), bf16[8,4320,128]{2,1,0:T(8,128)(2,1)}, u32[]{:S(2)}, u32[]{:S(2)}) %all-to-all-start.7) | async-done | bytes 8847392 | tf_op jit(solution)/shard_map/all_to_all | solution.py:741
  881.5 4.7 all-to-all-start.6
  886.2 5.1 shard_map.126.enc_ref
  891.3 10.9 %shard_map.127.enc_ref = bf16[32400,256]{1,0:T(8,128)(2,1)} custom-call(bf16[4,2,4320,128]{3,2,1,0:T(8,128)(2,1)} %bitcast.25.part_ref, bf16[32400,256]{1,0:T(8,128)(2,1)} %shard_map.126.enc_ref), custom_call_target="tpu_custom_call", output_to_operand_aliasing={{}: (1, {})} | custom-call | flops 17694720 | bytes 26542080 | tf_op jit(solution)/shard_map/pallas_call | solution.py:589
  902.2 89.4 %all-to-all-done.6 = bf16[8,2340,128]{2,1,0:T(8,128)(2,1)} async-done(((bf16[8,2340,128]{2,1,0:T(8,128)(2,1)}), bf16[8,2340,128]{2,1,0:T(8,128)(2,1)}, u32[]{:S(2)}, u32[]{:S(2)}) %all-to-all-start.6) | async-done | bytes 4792352 | tf_op jit(solution)/shard_map/all_to_all | solution.py:741
  991.6 5.7 shard_map.128
  (67 shorter events, 6.4 us)
Async XLA Ops:
  8.3 24.5 %all-to-all-start = ((bf16[8,73,512]{2,1,0:T(8,128)(2,1)}), bf16[8,73,512]{2,1,0:T(8,128)(2,1)S(1)}, u32[]{:S(2)}, u32[]{:S(2)}) async-start(bf16[8,73,512]{2,1,0:T(8,128)(2,1)} %broadcast_in_dim.89), calls=%async_computation | async-start | bytes 1310720 | tf_op jit(solution)/shard_map/all_to_all | solution.py:634
  15.6 118.7 %all-gather.3.cloned.1.call-start = ((), (), s32[]{:S(2)}) async-start(), calls=%async_computation.9 | async-start | bytes 5898240 | tf_op jit(solution)/shard_map/all_gather | solution.py:638
  15.7 0.6 copy-start.5
  27.6 21.4 %copy-start.7 = (bf16[256,256]{1,0:T(8,128)(2,1)S(1)}, bf16[256,256]{1,0:T(8,128)(2,1)}, u32[]{:S(2)}) copy-start(bf16[256,256]{1,0:T(8,128)(2,1)} %param.22) | copy-start | bytes 393220
  32.9 0.8 copy-start.1
  48.7 33.9 %copy-start.11 = (bf16[256,73]{0,1:T(8,128)(2,1)S(1)}, bf16[256,73]{0,1:T(8,128)(2,1)}, u32[]{:S(2)}) copy-start(bf16[256,73]{0,1:T(8,128)(2,1)} %param.20) | copy-start | bytes 112132
  182.5 50.2 %all-to-all-start.1 = ((bf16[4,60,32,256]{3,2,1,0:T(8,128)(2,1)}), bf16[4,60,32,256]{3,2,1,0:T(8,128)(2,1)}, u32[]{:S(2)}, u32[]{:S(2)}) async-start(bf16[4,60,32,256]{3,2,1,0:T(8,128)(2,1)} %get-tuple-element.56), calls=%async_computation.1 | async-start | bytes 7864320 | tf_op jit(solution)/shard_map/all_to_all | solution.py:693
  187.3 101.6 %copy-start.3 = (bf16[2,256,256]{2,1,0:T(8,128)(2,1)S(1)}, bf16[2,256,256]{2,1,0:T(8,128)(2,1)}, u32[]{:S(2)}) copy-start(bf16[2,256,256]{2,1,0:T(8,128)(2,1)} %param.24) | copy-start | bytes 786436
  283.7 50.6 %all-to-all-start.3 = ((bf16[4,120,16,256]{3,2,1,0:T(8,128)(2,1)}), bf16[4,120,16,256]{3,2,1,0:T(8,128)(2,1)}, u32[]{:S(2)}, u32[]{:S(2)}) async-start(bf16[4,120,16,256]{3,2,1,0:T(8,128)(2,1)} %get-tuple-element.61), calls=%async_computation.3 | async-start | bytes 7864320 | tf_op jit(solution)/shard_map/all_to_all | solution.py:693
  290.8 47.2 %copy-start.6 = (s32[1,4,8,128]{3,1,2,0:T(4,128)S(1)}, s32[1,4,8,128]{3,1,2,0:T(4,128)}, u32[]{:S(2)}) copy-start(s32[1,4,8,128]{3,1,2,0:T(4,128)} %copy-done.5) | copy-start | bytes 49156
  290.8 47.2 %copy-start.10 = (s32[4096]{0:T(1024)S(1)}, s32[4096]{0:T(1024)}, u32[]{:S(2)}) copy-start(s32[4096]{0:T(1024)} %param.17) | copy-start | bytes 49156
  290.8 47.2 %copy-start.2 = (bf16[8,73,512]{2,1,0:T(8,128)(2,1)S(1)}, bf16[8,73,512]{2,1,0:T(8,128)(2,1)}, u32[]{:S(2)}) copy-start(bf16[8,73,512]{2,1,0:T(8,128)(2,1)} %copy-done.1) | copy-start | bytes 1794052
  290.8 47.9 %copy-start.4 = (f32[4096]{0:T(1024)S(1)}, f32[4096]{0:T(1024)}, u32[]{:S(2)}) copy-start(f32[4096]{0:T(1024)} %param.19) | copy-start | bytes 49156
  290.8 47.9 %copy-start.9 = (s32[4096]{0:T(1024)S(1)}, s32[4096]{0:T(1024)}, u32[]{:S(2)}) copy-start(s32[4096]{0:T(1024)} %get-tuple-element.76) | copy-start | bytes 49156
  334.3 135.3 %all-to-all-start.4 = ((bf16[32,45,16,128]{3,2,1,0:T(8,128)(2,1)}), bf16[32,45,16,128]{3,2,1,0:T(8,128)(2,1)}, u32[]{:S(2)}, u32[]{:S(2)}) async-start(bf16[32,45,16,128]{3,2,1,0:T(8,128)(2,1)} %bitcast.45), calls=%async_computation.4 | async-start | bytes 11796480 | tf_op jit(solution)/shard_map/all_to_all | solution.py:730
  392.4 80.9 %copy-start.8 = (bf16[256,256]{1,0:T(8,128)(2,1)S(1)}, bf16[256,256]{1,0:T(8,128)(2,1)}, u32[]{:S(2)}) copy-start(bf16[256,256]{1,0:T(8,128)(2,1)} %param.22) | copy-start | bytes 393220
  392.4 80.9 %copy-start.12 = (bf16[256,73]{0,1:T(8,128)(2,1)S(1)}, bf16[256,73]{0,1:T(8,128)(2,1)}, u32[]{:S(2)}) copy-start(bf16[256,73]{0,1:T(8,128)(2,1)} %param.20) | copy-start | bytes 112132
  392.4 80.9 %copy-start.13 = (f32[256]{0:T(256)S(1)}, f32[256]{0:T(256)}, u32[]{:S(2)}) copy-start(f32[256]{0:T(256)} %param.21) | copy-start | bytes 3076
  392.4 80.9 %copy-start.14 = (f32[256]{0:T(256)S(1)}, f32[256]{0:T(256)}, u32[]{:S(2)}) copy-start(f32[256]{0:T(256)} %param.23) | copy-start | bytes 3076
  469.6 135.3 %all-to-all-start.5 = ((bf16[32,45,16,128]{3,2,1,0:T(8,128)(2,1)}), bf16[32,45,16,128]{3,2,1,0:T(8,128)(2,1)}, u32[]{:S(2)}, u32[]{:S(2)}) async-start(bf16[32,45,16,128]{3,2,1,0:T(8,128)(2,1)} %bitcast.46), calls=%async_computation.5 | async-start | bytes 11796480 | tf_op jit(solution)/shard_map/all_to_all | solution.py:730
  613.9 70.3 %all-to-all-start.8 = ((bf16[8,1440,128]{2,1,0:T(8,128)(2,1)}), bf16[8,1440,128]{2,1,0:T(8,128)(2,1)S(1)}, u32[]{:S(2)}, u32[]{:S(2)}) async-start(bf16[8,1440,128]{2,1,0:T(8,128)(2,1)} %shard_map.125), calls=%async_computation.8 | async-start | bytes 5898240 | tf_op jit(solution)/shard_map/all_to_all | solution.py:741
  684.2 18.7 %copy-start = (bf16[8,1440,128]{2,1,0:T(8,128)(2,1)}, bf16[8,1440,128]{2,1,0:T(8,128)(2,1)S(1)}, u32[]{:S(2)}) copy-start(bf16[8,1440,128]{2,1,0:T(8,128)(2,1)S(1)} %all-to-all-done.8) | copy-start | bytes 8847364
  684.2 197.3 %all-to-all-start.7 = ((bf16[8,4320,128]{2,1,0:T(8,128)(2,1)}), bf16[8,4320,128]{2,1,0:T(8,128)(2,1)}, u32[]{:S(2)}, u32[]{:S(2)}) async-start(bf16[8,4320,128]{2,1,0:T(8,128)(2,1)} %shard_map.124), calls=%async_computation.7 | async-start | bytes 17694720 | tf_op jit(solution)/shard_map/all_to_all | solution.py:741
  881.5 110.1 %all-to-all-start.6 = ((bf16[8,2340,128]{2,1,0:T(8,128)(2,1)}), bf16[8,2340,128]{2,1,0:T(8,128)(2,1)}, u32[]{:S(2)}, u32[]{:S(2)}) async-start(bf16[8,2340,128]{2,1,0:T(8,128)(2,1)} %shard_map.123), calls=%async_computation.6 | async-start | bytes 9601024 | tf_op jit(solution)/shard_map/all_to_all | solution.py:741
Sparse Core Ops, SparseCore 0:
  48.9 85.3 all-gather.2

commit v8 on v7

--- a/solution.py
+++ b/solution.py
@@ -16,7 +16,7 @@
 WINDOW = 48
 UNROLL = 5
 LATS = 8
-CHUNK_CUTS = (1, 4)
+CHUNK_CUTS = (1, 5)
 ORDER_GROUP = 8
 VMEM_BYTES = 60 * 1024 * 1024
 
@@ -114,7 +114,7 @@
             contrib[at, LANES : LANES + channels] = lower
             return carry
 
-        lax.fori_loop(0, shards, one, 0)
+        lax.fori_loop(0, shards, one, 0, unroll=4)
 
     here = pl.ds(pl.multiple_of(step * rows, rows), rows)
     used = jnp.logical_or(step == 0, step * rows < live[0])

time: 1010 us -> 1010 us (level)
  no operation moved by 1% of the time
where the time goes in v8:
time: 1010 us; the launch traced here: 1000 us
  waiting for transfers between devices  495 us (49%)
  Pallas kernels  212 us (21%)
  other arithmetic  93 us (9%)
  matrix products  81 us (8%)
  blocking collectives  50.9 us (5%)
  starting transfers between devices  37.2 us (4%)
  local copies, waits for them, and re-layouts  18.9 us (2%)
  between operations  14 us (1%)
    all_to_all x3, waiting for transfers between devices, listed_plan(): part = lax.all_to_all(part, 'lon', split_axis=0, concat_axis=0, tiled=True)  316 us
    all_to_all x2, waiting for transfers between devices, listed_plan(): lax.all_to_all(made, ('lat', 'lon'), split_axis=0, concat_axis=0, tiled=T...  101 us
    dot_general x1, matrix products, encoder_by_cell(): jnp.dot(hidden, enc_w2.T, preferred_element_type=F32) + enc_b2  81 us
    pallas_call x2, Pallas kernels, order_steps(): pl.pallas_call(functools.partial(orders_kernel, group=group, pieces=piece...  54.7 us
    all_to_all x1, blocking collectives, exchange(): return lax.all_to_all(piece, 'lat', split_axis=0, concat_axis=0, tiled=True)  50.9 us
    pallas_call x1, Pallas kernels, zonal_transform(): pl.pallas_call(functools.partial(zonal_first_kernel, channels=channels, b...  46.8 us
    all_gather x1, waiting for transfers between devices, listed_plan(): band = lax.all_gather(listed, 'lon', axis=0, tiled=False)  46.2 us
    scatter-add x1, other arithmetic, spread(): return running.at[targets.reshape(-1)].add(contrib.reshape(-1, channels))  44.9 us
  transfers between devices with their start and end apart: 9, of which 9 were waited for; matrix products, arithmetic and copies ran while one was open for 19% of the time, Pallas kernels for 14%

profile of v8, /device:TPU:0, one launch (start us, length us, event | category | flops | bytes accessed | tf_op | source)
XLA Modules:
  0.0 1002.2 jit_solution(3597450169620582957)
XLA Ops:
  6.5 1.8 broadcast_in_dim.89
  8.3 7.3 all-to-all-start
  16.3 1.4 broadcast_clamp_fusion
  18.8 5.8 sort.15
  24.9 0.9 stack.39
  25.8 1.9 copy.68.cols_ref
  27.7 5.1 all-to-all-done.src_ref
  32.9 0.8 copy-done.2
  33.7 14.1 %shard_map.118 = bf16[80,4096]{1,0:T(8,128)(2,1)} custom-call(s32[1]{0:T(128)} %slice.51.live, bf16[8,73,512]{2,1,0:T(8,128)(2,1)} %copy-done.2, f32[4096,8]{1,0:T(8,128)} %copy.68.cols_ref, f32[1,4096]{1,0:T(1,128)} %bitcast.65), custom_call_target="tpu_custom_call" | custom-call | flops 8589934592 | bytes 1048576 | tf_op jit(solution)/shard_map/pallas_call | solution.py:169
  48.9 2.6 cosine_multiply_fusion
  51.9 1.2 copy.72
  53.9 19.5 %multiply_convert_fusion.1 = (bf16[8,192,512,1]{1,0,3,2:T(8,128)(2,1)S(1)}, bf16[8,192,512,1]{1,0,3,2:T(8,128)(2,1)S(1)}) fusion(s32[512]{0:T(512)S(1)} %reshape.369, s32[8,192]{1,0:T(8,128)S(1)} %iota_add_fusion.1), kind=kLoop, calls=%fused_computation.31 | loop fusion | flops 10223616 | bytes 3153920 | tf_op jit(solution)/shard_map/convert
  73.3 2.7 pad_maximum_fusion
  76.0 5.7 copy.70
  82.4 2.0 broadcast_select_fusion.1.basis_ref
  84.3 1.9 broadcast_select_fusion.refs_2_
  86.2 46.2 %all-gather.3.cloned.1.call-done = bf16[640,4096]{1,0:T(8,128)(2,1)} async-done(((bf16[80,4096]{1,0:T(8,128)(2,1)}), bf16[640,4096]{1,0:T(8,128)(2,1)}) %all-gather.3.cloned.1.call-update) | async-done | bytes 5242896 | tf_op jit(solution)/shard_map/all_gather | solution.py:638
  132.4 0.8 slice.61
  133.8 46.8 %shard_map.119 = (bf16[4,60,32,256]{3,2,1,0:T(8,128)(2,1)}, bf16[32816,256]{1,0:T(8,128)(2,1)}, bf16[32816,128]{1,0:T(8,128)(2,1)}, f32[128,256]{1,0:T(8,128)}) custom-call(s32[8,181]{1,0:T(8,128)} %fusion.39.starts, bf16[8,80,4096]{2,1,0:T(8,128)(2,1)} %bitcast.67, bf16[80,256]{1,0:T(8,128)(2,1)} %scatter.9.w1_ref, f32[1,256]{1,0:T(1,128)} %bitcast.68, ...), custom_call_target="tpu_custom_call" | custom-call | flops 53687091200 | bytes 33554432 | tf_op jit(solution)/shard_map/pallas_call | solution.py:363
  180.6 5.3 all-to-all-start.1
  185.9 33.5 %shard_map.120 = (bf16[4,120,16,256]{3,2,1,0:T(8,128)(2,1)}, bf16[4,120,16,256]{3,2,1,0:T(8,128)(2,1)}) custom-call(s32[8,181]{1,0:T(8,128)} %fusion.39.starts, bf16[32816,256]{1,0:T(8,128)(2,1)} %get-tuple-element.52.delta, bf16[32816,128]{1,0:T(8,128)(2,1)} %get-tuple-element.53.hots, f32[128,256]{1,0:T(8,128)} %get-tuple-element.54.base), custom_call_target="tpu_custom_call" | custom-call | flops 53687091200 | bytes 33554432 | tf_op jit(solution)/shard_map/pallas_call | solution.py:389
  219.5 11.9 %all-to-all-done.1.refs_0_ = bf16[4,60,32,256]{3,2,1,0:T(8,128)(2,1)} async-done(((bf16[4,60,32,256]{3,2,1,0:T(8,128)(2,1)}), bf16[4,60,32,256]{3,2,1,0:T(8,128)(2,1)}, u32[]{:S(2)}, u32[]{:S(2)}) %all-to-all-start.1) | async-done | bytes 3932192 | tf_op jit(solution)/shard_map/all_to_all | solution.py:693
  231.3 50.9 %all_to_all.45.refs_1_ = bf16[4,120,16,256]{3,2,1,0:T(8,128)(2,1)} all-to-all(bf16[4,120,16,256]{3,2,1,0:T(8,128)(2,1)} %get-tuple-element.59), channel_id=1, replica_groups=mesh['lat'=4,'lon'=8] {'lat'}, dimensions={0} | all-to-all | bytes 7864320 | tf_op jit(solution)/shard_map/all_to_all | solution.py:693
  282.3 4.8 all-to-all-start.3
  287.4 0.8 maximum_bitcast_fusion.refs_4_
  289.0 27.4 %shard_map.121 = bf16[16,2,45,16,128]{4,3,2,1,0:T(8,128)(2,1)} custom-call(s32[720]{0:T(1024)} %constant.252.clone.place, bf16[4,60,32,256]{3,2,1,0:T(8,128)(2,1)} %all-to-all-done.1.refs_0_, bf16[4,120,16,256]{3,2,1,0:T(8,128)(2,1)} %all_to_all.45.refs_1_, bf16[16,720,512]{2,1,0:T(8,128)(2,1)} %bitcast.43, bf16[16,720,512]{2,1,0:T(8,128)(2,1)} %refs_3_.3, ...), custom_call_target="tpu_custom_call" | custom-call | flops 8187281408 | bytes 23592960 | tf_op jit(solution)/shard_map/pallas_call | solution.py:488
  316.4 16.1 %all-to-all-done.3.refs_1_ = bf16[4,120,16,256]{3,2,1,0:T(8,128)(2,1)} async-done(((bf16[4,120,16,256]{3,2,1,0:T(8,128)(2,1)}), bf16[4,120,16,256]{3,2,1,0:T(8,128)(2,1)}, u32[]{:S(2)}, u32[]{:S(2)}) %all-to-all-start.3) | async-done | bytes 3932192 | tf_op jit(solution)/shard_map/all_to_all | solution.py:693
  332.5 3.6 all-to-all-start.4
  336.9 44.9 %scatter_custom_fusion = f32[32400,73]{1,0:T(8,128)} fusion(s32[4096]{0:T(1024)} %get-tuple-element.87, f32[]{:T(128)} %constant.199.clone.1, f32[4096]{0:T(1024)S(1)} %copy-done.5, pred[4096]{0:T(1024)(128)(4,1)S(1)} %compare_and_fusion, bf16[]{:T(256)} %constant.222.clone.1, bf16[4096,73]{1,0:T(8,128)(2,1)S(1)} %bitcast.50, s32[4096]{0:T(1024)S(1)} %copy-done.10), kind=kCustom, calls=%fused_computation.24 | custom fusion | flops 1196032 | bytes 10096704 | tf_op jit(solution)/shard_map/scatter-add | solution.py:52
  381.8 8.8 convert_element_type.121
  390.6 27.3 %shard_map.122 = bf16[16,2,45,16,128]{4,3,2,1,0:T(8,128)(2,1)} custom-call(s32[720]{0:T(1024)} %constant.252.clone.place, bf16[4,60,32,256]{3,2,1,0:T(8,128)(2,1)} %all-to-all-done.1.refs_0_, bf16[4,120,16,256]{3,2,1,0:T(8,128)(2,1)} %all-to-all-done.3.refs_1_, bf16[16,720,512]{2,1,0:T(8,128)(2,1)} %bitcast.44, bf16[16,720,512]{2,1,0:T(8,128)(2,1)} %refs_3_.3, ...), custom_call_target="tpu_custom_call" | custom-call | flops 8187281408 | bytes 23592960 | tf_op jit(solution)/shard_map/pallas_call | solution.py:488
  417.9 49.9 %all-to-all-done.4.refs_0_ = bf16[32,45,16,128]{3,2,1,0:T(8,128)(2,1)} async-done(((bf16[32,45,16,128]{3,2,1,0:T(8,128)(2,1)}), bf16[32,45,16,128]{3,2,1,0:T(8,128)(2,1)}, u32[]{:S(2)}, u32[]{:S(2)}) %all-to-all-start.4) | async-done | bytes 5898272 | tf_op jit(solution)/shard_map/all_to_all | solution.py:730
  467.8 3.6 all-to-all-start.5
  471.5 81.0 %fusion.enc_ref = bf16[32400,256]{1,0:T(8,128)(2,1)} fusion(bf16[256,256]{1,0:T(8,128)(2,1)S(1)} %copy-done.9, f32[256]{0:T(256)S(1)} %copy-done.15, bf16[32400,73]{1,0:T(8,128)(2,1)} %convert_element_type.121, bf16[256,73]{0,1:T(8,128)(2,1)S(1)} %copy-done.13, f32[256]{0:T(256)S(1)} %copy-done.14), kind=kOutput, calls=%fused_computation.5 | convolution fusion | flops 6021734400 | bytes 21489696 | tf_op jit(solution)/shard_map/dot_general | solution.py:90
  552.5 50.6 %all-to-all-done.5.refs_1_ = bf16[32,45,16,128]{3,2,1,0:T(8,128)(2,1)} async-done(((bf16[32,45,16,128]{3,2,1,0:T(8,128)(2,1)}), bf16[32,45,16,128]{3,2,1,0:T(8,128)(2,1)}, u32[]{:S(2)}, u32[]{:S(2)}) %all-to-all-start.5) | async-done | bytes 5898272 | tf_op jit(solution)/shard_map/all_to_all | solution.py:730
  603.1 9.0 shard_map.125
  612.1 3.6 all-to-all-start.8
  615.8 23.8 %shard_map.124 = bf16[8,5760,128]{2,1,0:T(8,128)(2,1)} custom-call(bf16[32,45,16,128]{3,2,1,0:T(8,128)(2,1)} %all-to-all-done.4.refs_0_, bf16[32,45,16,128]{3,2,1,0:T(8,128)(2,1)} %all-to-all-done.5.refs_1_, bf16[8,192,1024]{2,1,0:T(8,128)(2,1)} %broadcast_select_fusion.refs_2_), custom_call_target="tpu_custom_call" | custom-call | flops 12884901888 | bytes 23592960 | tf_op jit(solution)/shard_map/pallas_call | solution.py:548
  639.6 42.8 %all-to-all-done.8 = bf16[8,1440,128]{2,1,0:T(8,128)(2,1)S(1)} async-done(((bf16[8,1440,128]{2,1,0:T(8,128)(2,1)}), bf16[8,1440,128]{2,1,0:T(8,128)(2,1)S(1)}, u32[]{:S(2)}, u32[]{:S(2)}) %all-to-all-start.8) | async-done | bytes 2949152 | tf_op jit(solution)/shard_map/all_to_all | solution.py:741
  682.4 5.3 all-to-all-start.7
  687.8 8.5 shard_map.123
  696.2 247.0 %all-to-all-done.7 = bf16[8,5760,128]{2,1,0:T(8,128)(2,1)} async-done(((bf16[8,5760,128]{2,1,0:T(8,128)(2,1)}), bf16[8,5760,128]{2,1,0:T(8,128)(2,1)}, u32[]{:S(2)}, u32[]{:S(2)}) %all-to-all-start.7) | async-done | bytes 11796512 | tf_op jit(solution)/shard_map/all_to_all | solution.py:741
  943.2 3.6 all-to-all-start.6
  946.9 5.1 shard_map.126.enc_ref
  951.9 12.4 %shard_map.127.enc_ref = bf16[32400,256]{1,0:T(8,128)(2,1)} custom-call(bf16[4,2,5760,128]{3,2,1,0:T(8,128)(2,1)} %bitcast.25.part_ref, bf16[32400,256]{1,0:T(8,128)(2,1)} %shard_map.126.enc_ref), custom_call_target="tpu_custom_call", output_to_operand_aliasing={{}: (1, {})} | custom-call | flops 23592960 | bytes 35389440 | tf_op jit(solution)/shard_map/pallas_call | solution.py:589
  964.3 25.7 %all-to-all-done.6 = bf16[8,900,128]{2,1,0:T(8,128)(2,1)S(1)} async-done(((bf16[8,900,128]{2,1,0:T(8,128)(2,1)}), bf16[8,900,128]{2,1,0:T(8,128)(2,1)S(1)}, u32[]{:S(2)}, u32[]{:S(2)}) %all-to-all-start.6) | async-done | bytes 1843232 | tf_op jit(solution)/shard_map/all_to_all | solution.py:741
  990.0 1.3 copy-done.1
  991.3 3.9 shard_map.128
  (69 shorter events, 7.2 us)
Async XLA Ops:
  8.3 24.5 %all-to-all-start = ((bf16[8,73,512]{2,1,0:T(8,128)(2,1)}), bf16[8,73,512]{2,1,0:T(8,128)(2,1)S(1)}, u32[]{:S(2)}, u32[]{:S(2)}) async-start(bf16[8,73,512]{2,1,0:T(8,128)(2,1)} %broadcast_in_dim.89), calls=%async_computation | async-start | bytes 1310720 | tf_op jit(solution)/shard_map/all_to_all | solution.py:634
  15.6 116.8 %all-gather.3.cloned.1.call-start = ((), (), s32[]{:S(2)}) async-start(), calls=%async_computation.9 | async-start | bytes 5898240 | tf_op jit(solution)/shard_map/all_gather | solution.py:638
  15.7 0.6 copy-start.6
  27.7 20.4 %copy-start.8 = (bf16[256,256]{1,0:T(8,128)(2,1)S(1)}, bf16[256,256]{1,0:T(8,128)(2,1)}, u32[]{:S(2)}) copy-start(bf16[256,256]{1,0:T(8,128)(2,1)} %param.22) | copy-start | bytes 393220
  32.9 0.8 copy-start.2
  47.8 33.9 %copy-start.12 = (bf16[256,73]{0,1:T(8,128)(2,1)S(1)}, bf16[256,73]{0,1:T(8,128)(2,1)}, u32[]{:S(2)}) copy-start(bf16[256,73]{0,1:T(8,128)(2,1)} %param.20) | copy-start | bytes 112132
  180.6 50.7 %all-to-all-start.1 = ((bf16[4,60,32,256]{3,2,1,0:T(8,128)(2,1)}), bf16[4,60,32,256]{3,2,1,0:T(8,128)(2,1)}, u32[]{:S(2)}, u32[]{:S(2)}) async-start(bf16[4,60,32,256]{3,2,1,0:T(8,128)(2,1)} %get-tuple-element.56), calls=%async_computation.1 | async-start | bytes 7864320 | tf_op jit(solution)/shard_map/all_to_all | solution.py:693
  185.9 101.2 %copy-start.4 = (bf16[2,256,256]{2,1,0:T(8,128)(2,1)S(1)}, bf16[2,256,256]{2,1,0:T(8,128)(2,1)}, u32[]{:S(2)}) copy-start(bf16[2,256,256]{2,1,0:T(8,128)(2,1)} %param.24) | copy-start | bytes 786436
  282.3 50.2 %all-to-all-start.3 = ((bf16[4,120,16,256]{3,2,1,0:T(8,128)(2,1)}), bf16[4,120,16,256]{3,2,1,0:T(8,128)(2,1)}, u32[]{:S(2)}, u32[]{:S(2)}) async-start(bf16[4,120,16,256]{3,2,1,0:T(8,128)(2,1)} %get-tuple-element.61), calls=%async_computation.3 | async-start | bytes 7864320 | tf_op jit(solution)/shard_map/all_to_all | solution.py:693
  288.9 47.2 %copy-start.7 = (s32[1,4,8,128]{3,1,2,0:T(4,128)S(1)}, s32[1,4,8,128]{3,1,2,0:T(4,128)}, u32[]{:S(2)}) copy-start(s32[1,4,8,128]{3,1,2,0:T(4,128)} %copy-done.6) | copy-start | bytes 49156
  288.9 47.2 %copy-start.11 = (s32[4096]{0:T(1024)S(1)}, s32[4096]{0:T(1024)}, u32[]{:S(2)}) copy-start(s32[4096]{0:T(1024)} %param.17) | copy-start | bytes 49156
  289.0 47.2 %copy-start.3 = (bf16[8,73,512]{2,1,0:T(8,128)(2,1)S(1)}, bf16[8,73,512]{2,1,0:T(8,128)(2,1)}, u32[]{:S(2)}) copy-start(bf16[8,73,512]{2,1,0:T(8,128)(2,1)} %copy-done.2) | copy-start | bytes 1794052
  289.0 47.9 %copy-start.5 = (f32[4096]{0:T(1024)S(1)}, f32[4096]{0:T(1024)}, u32[]{:S(2)}) copy-start(f32[4096]{0:T(1024)} %param.19) | copy-start | bytes 49156
  289.0 47.9 %copy-start.10 = (s32[4096]{0:T(1024)S(1)}, s32[4096]{0:T(1024)}, u32[]{:S(2)}) copy-start(s32[4096]{0:T(1024)} %get-tuple-element.76) | copy-start | bytes 49156
  332.5 135.3 %all-to-all-start.4 = ((bf16[32,45,16,128]{3,2,1,0:T(8,128)(2,1)}), bf16[32,45,16,128]{3,2,1,0:T(8,128)(2,1)}, u32[]{:S(2)}, u32[]{:S(2)}) async-start(bf16[32,45,16,128]{3,2,1,0:T(8,128)(2,1)} %bitcast.45), calls=%async_computation.4 | async-start | bytes 11796480 | tf_op jit(solution)/shard_map/all_to_all | solution.py:730
  390.6 80.8 %copy-start.9 = (bf16[256,256]{1,0:T(8,128)(2,1)S(1)}, bf16[256,256]{1,0:T(8,128)(2,1)}, u32[]{:S(2)}) copy-start(bf16[256,256]{1,0:T(8,128)(2,1)} %param.22) | copy-start | bytes 393220
  390.6 80.8 %copy-start.13 = (bf16[256,73]{0,1:T(8,128)(2,1)S(1)}, bf16[256,73]{0,1:T(8,128)(2,1)}, u32[]{:S(2)}) copy-start(bf16[256,73]{0,1:T(8,128)(2,1)} %param.20) | copy-start | bytes 112132
  390.6 80.8 %copy-start.14 = (f32[256]{0:T(256)S(1)}, f32[256]{0:T(256)}, u32[]{:S(2)}) copy-start(f32[256]{0:T(256)} %param.21) | copy-start | bytes 3076
  390.6 80.9 %copy-start.15 = (f32[256]{0:T(256)S(1)}, f32[256]{0:T(256)}, u32[]{:S(2)}) copy-start(f32[256]{0:T(256)} %param.23) | copy-start | bytes 3076
  467.8 135.3 %all-to-all-start.5 = ((bf16[32,45,16,128]{3,2,1,0:T(8,128)(2,1)}), bf16[32,45,16,128]{3,2,1,0:T(8,128)(2,1)}, u32[]{:S(2)}, u32[]{:S(2)}) async-start(bf16[32,45,16,128]{3,2,1,0:T(8,128)(2,1)} %bitcast.46), calls=%async_computation.5 | async-start | bytes 11796480 | tf_op jit(solution)/shard_map/all_to_all | solution.py:730
  612.1 70.3 %all-to-all-start.8 = ((bf16[8,1440,128]{2,1,0:T(8,128)(2,1)}), bf16[8,1440,128]{2,1,0:T(8,128)(2,1)S(1)}, u32[]{:S(2)}, u32[]{:S(2)}) async-start(bf16[8,1440,128]{2,1,0:T(8,128)(2,1)} %shard_map.125), calls=%async_computation.8 | async-start | bytes 5898240 | tf_op jit(solution)/shard_map/all_to_all | solution.py:741
  682.4 13.8 %copy-start = (bf16[8,1440,128]{2,1,0:T(8,128)(2,1)}, bf16[8,1440,128]{2,1,0:T(8,128)(2,1)S(1)}, u32[]{:S(2)}) copy-start(bf16[8,1440,128]{2,1,0:T(8,128)(2,1)S(1)} %all-to-all-done.8) | copy-start | bytes 8847364
  682.4 260.8 %all-to-all-start.7 = ((bf16[8,5760,128]{2,1,0:T(8,128)(2,1)}), bf16[8,5760,128]{2,1,0:T(8,128)(2,1)}, u32[]{:S(2)}, u32[]{:S(2)}) async-start(bf16[8,5760,128]{2,1,0:T(8,128)(2,1)} %shard_map.124), calls=%async_computation.7 | async-start | bytes 23592960 | tf_op jit(solution)/shard_map/all_to_all | solution.py:741
  943.2 46.8 %all-to-all-start.6 = ((bf16[8,900,128]{2,1,0:T(8,128)(2,1)}), bf16[8,900,128]{2,1,0:T(8,128)(2,1)S(1)}, u32[]{:S(2)}, u32[]{:S(2)}) async-start(bf16[8,900,128]{2,1,0:T(8,128)(2,1)} %shard_map.123), calls=%async_computation.6 | async-start | bytes 3702784 | tf_op jit(solution)/shard_map/all_to_all | solution.py:741
  990.0 1.3 copy-start.1
Sparse Core Ops, SparseCore 0:
  47.9 84.4 all-gather.2
